TPU v7x, 32 devices: a whole 2x2x4 slice. The times are simulated.
32 devices in a mesh: tp: 2 (over y), dp: 4 (over z), hg: 4 (over x, core).
Axes of the slice: x: 2, y: 2, z: 4, core: 2. Of those that a mesh axis runs over, the one named last changes fastest.
Arguments:
- hidden_in: bfloat16 [4, 4, 256, 4096], P('dp', 'hg', 'tp'), may hold values from -45 to 45
- norm_gain: float32 [4096], replicated, may hold values from 0.1 to 1.9
- qkv_weight: bfloat16 [4096, 3, 32, 128], P(('dp', 'hg'), None, 'tp'), may hold values from -0.09375 to 0.09375
- out_weight: bfloat16 [32, 128, 4096], P('tp', None, ('dp', 'hg')), may hold values from -0.5 to 0.5
- cache_kv: bfloat16 [4, 32, 1024, 256], P('dp', 'tp'), may hold values from -200 to 200
- cached_lengths: int32 [4], replicated, may hold values from 128 to 1024, as said below
- owner_table: int32 [4, 16], replicated, may hold values from 0 to 3, as said below
Outputs:
- hidden_out: bfloat16 [4, 4, 256, 4096], P('dp', 'hg', 'tp')
- decode_kv: bfloat16 [4, 32, 4, 4, 128, 256], P('dp', ('tp', 'hg'))
Inputs may be any that keep to these rules, and one draw needn't show every extreme that they name: `cached_lengths`: multiples of 128; one request has exactly 1024. `owner_table`: a request has at most 4 valid blocks with one owner; one owner holds exactly 4 valid blocks of every request.
All inputs are finite; a program needn't handle non-finite values.
Results may differ from a plain program's by a relative error of at most 0.015.
Values may be sent and summed in bfloat16 or wider, within the bound.
No kernel may reach another device: no remote copies, remote signals or barrier semaphores. Data moves between devices by JAX's collectives and lax.ppermute only.
A program may use at most 128 MiB of HBM per device.

v0:
```python
import math

import jax
import jax.numpy as jnp
from jax import lax
from jax.sharding import PartitionSpec as P

ROT = 32
BLOCK = 128


epsilon = 1e-05


def layer_norm(row_data, gain_row):
    row_data = row_data.astype(jnp.float32)
    centered = row_data - jnp.mean(row_data, axis=-1, keepdims=True)
    spread = jnp.mean(centered * centered, axis=-1, keepdims=True)
    return (centered * lax.rsqrt(spread + epsilon) * gain_row).astype(jnp.bfloat16)


def rotate(vectors, positions, rot_dims):
    half_dims = rot_dims // 2
    frequency = 10000.0 ** (-2.0 * jnp.arange(half_dims, dtype=jnp.float32) / rot_dims)
    angles = positions.astype(jnp.float32)[:, None, None] * frequency[None, None, :]
    cosine = jnp.cos(angles)
    sine_part = jnp.sin(angles)
    first_half = vectors[..., :half_dims]
    second = vectors[..., half_dims:rot_dims]
    return jnp.concatenate(
        [
            first_half * cosine - second * sine_part,
            second * cosine + first_half * sine_part,
            vectors[..., rot_dims:],
        ],
        axis=-1,
    )


def attend(queries, key_rows, value_rows, limit_base):
    scores = jnp.dot(queries, key_rows.T, preferred_element_type=jnp.float32) / math.sqrt(
        queries.shape[-1]
    )
    row_limit = limit_base + jnp.arange(queries.shape[0], dtype=jnp.int32)
    allowed = jnp.arange(key_rows.shape[0], dtype=jnp.int32)[None, :] <= row_limit[:, None]
    scores = jnp.where(allowed, scores, -jnp.inf)
    row_max = jnp.max(scores, axis=1, keepdims=True)
    weights = jnp.exp(scores - row_max)
    row_total = jnp.sum(weights, axis=1, keepdims=True)
    attended = (
        jnp.dot(weights.astype(jnp.bfloat16), value_rows, preferred_element_type=jnp.float32)
        / row_total
    )
    return attended.astype(jnp.bfloat16)


def selector(owner_row, valid_end, low_block, high_block, owner_count, slot_cap):
    block_ids = jnp.arange(owner_row.shape[0], dtype=jnp.int32)
    is_valid = block_ids < valid_end
    same_owner = (
        (owner_row[:, None] == owner_row[None, :])
        & is_valid[None, :]
        & (block_ids[None, :] < block_ids[:, None])
    )
    slot_rank = jnp.sum(same_owner.astype(jnp.int32), axis=1)
    chosen = is_valid & (block_ids >= low_block) & (block_ids < high_block)
    slot_ids = jnp.arange(owner_count * slot_cap, dtype=jnp.int32)
    picked = (
        chosen[None, :]
        & (owner_row[None, :] == (slot_ids // slot_cap)[:, None])
        & (slot_rank[None, :] == (slot_ids % slot_cap)[:, None])
    )
    return picked.astype(jnp.bfloat16)


def on_device(hidden_in, norm_gain, qkv_weight, out_weight, cache_kv, cached_lengths, owner_table):
    tp_count = lax.axis_size("tp")
    run_count = lax.axis_size("hg")
    owner_count = lax.axis_size("dp")
    request = lax.axis_index("dp")
    run_index = lax.axis_index("hg")
    length = lax.dynamic_index_in_dim(cached_lengths, request, 0, keepdims=False)
    owner_row = lax.dynamic_index_in_dim(owner_table, request, 0, keepdims=False)
    local_rows = hidden_in.shape[2]
    run_len = local_rows * tp_count
    stretch_len = run_len * run_count
    model_width = hidden_in.shape[3]
    local_heads = qkv_weight.shape[2]
    head_dim = qkv_weight.shape[3]
    head_width = local_heads * head_dim
    group_heads = local_heads // run_count
    seq_span = cache_kv.shape[2] + stretch_len
    block_count = seq_span // BLOCK
    slot_cap = (block_count + owner_count - 1) // owner_count
    valid_end = (length + stretch_len) // BLOCK
    run_first = run_index * run_len
    zero_index = jnp.zeros((), jnp.int32)
    extended = jnp.concatenate(
        [cache_kv[0], jnp.zeros((local_heads, stretch_len, 2 * head_dim), jnp.bfloat16)], axis=1
    )
    run_rows = lax.all_gather(hidden_in, "tp", axis=2, tiled=True)[0, 0]
    normed = layer_norm(run_rows, norm_gain)
    piece = lax.all_gather(qkv_weight, ("dp", "hg"), axis=0, tiled=True)
    projected = jnp.dot(
        normed, piece.reshape(piece.shape[0], 3 * head_width), preferred_element_type=jnp.float32
    )
    positions = length + run_first + jnp.arange(run_len, dtype=jnp.int32)
    queries = rotate(
        projected[:, :head_width].reshape(run_len, local_heads, head_dim), positions, ROT
    ).astype(jnp.bfloat16)
    new_keys = rotate(
        projected[:, head_width : 2 * head_width].reshape(run_len, local_heads, head_dim),
        positions,
        ROT,
    ).astype(jnp.bfloat16)
    new_values = (
        projected[:, 2 * head_width :].reshape(run_len, local_heads, head_dim).astype(jnp.bfloat16)
    )
    run_kv = jnp.concatenate([new_keys, new_values], axis=2).transpose(1, 0, 2)
    stretch_kv = lax.all_gather(run_kv, "hg", axis=1, tiled=True)

    def one_head(operands):
        head_queries, head_extended, head_stretch = operands
        sequence = lax.dynamic_update_slice(head_extended, head_stretch, (length, zero_index))
        return (
            attend(
                head_queries, sequence[:, :head_dim], sequence[:, head_dim:], length + run_first
            ),
            sequence,
        )

    attended, sequence = lax.map(one_head, (queries.transpose(1, 0, 2), extended, stretch_kv))
    attended_rows = attended.transpose(1, 0, 2).reshape(run_len, head_width)
    out_full = lax.all_gather(out_weight, ("dp", "hg"), axis=2, tiled=True)
    out_flat = out_full.reshape(head_width, model_width)
    reduced = lax.psum_scatter(
        jnp.dot(attended_rows, out_flat, preferred_element_type=jnp.float32).astype(jnp.bfloat16),
        "tp",
        scatter_dimension=0,
        tiled=True,
    ).astype(jnp.float32)
    hidden_out = (hidden_in[0, 0].astype(jnp.float32) + reduced).astype(jnp.bfloat16)[None, None]
    mine = lax.dynamic_slice_in_dim(sequence, run_index * group_heads, group_heads, 0)
    picked = selector(owner_row, valid_end, 0, valid_end, owner_count, slot_cap).reshape(
        owner_count, slot_cap, block_count
    )
    blocks = mine.reshape(group_heads, block_count, BLOCK * 2 * head_dim)
    placed = jnp.einsum("ocb,hbx->ohcx", picked, blocks, preferred_element_type=jnp.float32)
    received = lax.all_to_all(
        placed.astype(jnp.bfloat16).reshape(
            owner_count, group_heads, 1, slot_cap, BLOCK, 2 * head_dim
        ),
        "dp",
        split_axis=0,
        concat_axis=2,
        tiled=True,
    )
    return (hidden_out, received)


def solution(mesh):
    return jax.shard_map(
        on_device,
        mesh=mesh,
        in_specs=(
            P("dp", "hg", "tp", None),
            P(),
            P(("dp", "hg"), None, "tp", None),
            P("tp", None, ("dp", "hg")),
            P("dp", "tp", None, None),
            P(),
            P(),
        ),
        out_specs=(P("dp", "hg", "tp", None), P("dp", ("tp", "hg"), None, None, None, None)),
        check_vma=False,
    )
```

profile of v0, /device:TPU:0, one launch (start us, length us, event | category | flops | bytes accessed | tf_op | source)
XLA Modules:
  0.0 692.5 jit_solution(6166970390497965264)
XLA Ops:
  10.4 35.0 %all-gather.5.cloned.1.call-done = bf16[1,1,256,4096]{3,2,1,0:T(8,128)(2,1)} async-done(((bf16[1,1,128,4096]{3,2,1,0:T(8,128)(2,1)}), bf16[1,1,256,4096]{3,2,1,0:T(8,128)(2,1)}) %all-gather.5.cloned.1.call-update) | async-done | bytes 2097168 | tf_op jit(solution)/shard_map/all_gather | solution.py:101
  45.5 2.1 convert_reduce_fusion
  48.4 245.8 %all-gather.7.cloned.1.call-done = bf16[4096,3,16,128]{3,2,1,0:T(8,128)(2,1)} async-done(((bf16[256,3,16,128]{3,2,1,0:T(8,128)(2,1)}), bf16[4096,3,16,128]{3,2,1,0:T(8,128)(2,1)}) %all-gather.7.cloned.1.call-update) | async-done | bytes 50331664 | tf_op jit(solution)/shard_map/all_gather | solution.py:103
  294.2 32.3 %fusion.13 = f32[256,6144]{1,0:T(8,128)} fusion(bf16[512,8,48,128]{3,2,1,0:T(8,128)(2,1)} %bitcast.97, bf16[1,1,256,4096]{3,2,1,0:T(8,128)(2,1)S(1)} %copy-done.2, f32[4096]{0:T(1024)S(1)} %copy-done.5, f32[256]{0:T(256)S(1)} %add_rsqrt_fusion, f32[256]{0:T(256)S(1)} %broadcast_multiply_fusion), kind=kOutput, calls=%fused_computation.20 | convolution fusion | flops 12890144768 | bytes 58738688 | tf_op jit(solution)/shard_map/dot_general | solution.py:104
  326.5 2.5 slice_bitcast_fusion
  329.0 1.8 copy_bitcast_fusion
  331.9 1.3 fusion.52
  333.5 3.7 subtract_convert_fusion
  337.3 2.9 maximum_bitcast_fusion
  343.5 10.0 %concatenate.14 = bf16[16,2048,256]{2,1,0:T(8,128)(2,1)} pad(bf16[16,1024,256]{2,1,0:T(8,128)(2,1)} %bitcast.96, bf16[]{:T(256)} %constant.113.clone.1), padding=0_0x0_1024x0_0 | pad | bytes 25165826 | tf_op jit(solution)/shard_map/concatenate | solution.py:98
  355.0 2.0 maximum_bitcast_fusion.1
  356.9 41.7 %all-gather.9.cloned.1.call-done = bf16[16,1024,256]{2,1,0:T(8,128)(2,1)} async-done(((bf16[16,256,256]{2,1,0:T(8,128)(2,1)}), bf16[16,1024,256]{2,1,0:T(8,128)(2,1)}) %all-gather.9.cloned.1.call-update) | async-done | bytes 8388624 | tf_op jit(solution)/shard_map/all_gather | solution.py:120
  398.6 152.5 %while.14 = (s32[]{:T(128)}, bf16[16,256,128]{2,1,0:T(8,128)(2,1)}, bf16[16,2048,256]{2,1,0:T(8,128)(2,1)}, s32[]{:T(128)}, bf16[16,256,128]{2,1,0:T(8,128)(2,1)...) while((s32[]{:T(128)}, bf16[16,256,128]{2,1,0:T(8,128)(2,1)}, ...), condition=%wide.region_5.6_spmd, body=%wide.region_2.5_spmd.sunk | while | flops 272695040 | bytes 13771381 | solution.py:132
  398.6 1.3 dynamic-slice_bitcast_fusion.5
  401.0 3.0 dynamic_update_slice.24
  404.1 1.4 fusion.63
  408.2 1.4 dynamic-slice_bitcast_fusion.5
  410.7 3.0 dynamic_update_slice.24
  413.8 1.4 fusion.63
  417.9 1.3 dynamic-slice_bitcast_fusion.5
  420.2 3.0 dynamic_update_slice.24
  423.3 1.4 fusion.63
  427.3 1.3 dynamic-slice_bitcast_fusion.5
  429.7 3.0 dynamic_update_slice.24
  432.8 1.4 fusion.63
  439.3 3.0 dynamic_update_slice.24
  442.3 1.4 fusion.63
  448.8 3.0 dynamic_update_slice.24
  451.8 1.4 fusion.63
  455.9 1.3 dynamic-slice_bitcast_fusion.5
  458.3 3.0 dynamic_update_slice.24
  461.4 1.4 fusion.63
  467.8 3.0 dynamic_update_slice.24
  470.9 1.4 fusion.63
  477.4 3.0 dynamic_update_slice.24
  480.4 1.4 fusion.63
  484.5 1.3 dynamic-slice_bitcast_fusion.5
  486.9 3.0 dynamic_update_slice.24
  489.9 1.4 fusion.63
  496.5 3.0 dynamic_update_slice.24
  499.5 1.4 fusion.63
  503.6 1.3 dynamic-slice_bitcast_fusion.5
  506.0 3.0 dynamic_update_slice.24
  509.0 1.4 fusion.63
  515.4 3.0 dynamic_update_slice.24
  518.5 1.4 fusion.63
  525.0 3.0 dynamic_update_slice.24
  528.0 1.4 fusion.63
  532.1 1.3 dynamic-slice_bitcast_fusion.5
  534.5 3.0 dynamic_update_slice.24
  537.6 1.4 fusion.63
  544.0 3.0 dynamic_update_slice.24
  547.1 1.4 fusion.63
  551.2 4.5 constant_dynamic-slice_fusion
  555.6 7.4 %reshape.208 = bf16[4,16,32768,1]{2,1,0,3:T(8,128)(2,1)} reshape(bf16[4,2048,256]{2,1,0:T(8,128)(2,1)} %constant_dynamic-slice_fusion) | data formatting | bytes 8388608 | tf_op jit(solution)/shard_map/reshape | solution.py:147
  563.0 6.8 fusion.16
  569.9 7.7 %reshape.205 = bf16[4,4,1,4,128,256]{5,4,3,0,1,2:T(8,128)(2,1)} reshape(bf16[4,4,4,32768]{3,2,0,1:T(4,128)(2,1)} %fusion.16) | data formatting | bytes 8388608 | tf_op jit(solution)/shard_map/reshape | solution.py:150
  577.6 4.7 copy.43
  582.3 5.0 all-to-all-start
  587.4 9.3 %fusion.17 = bf16[256,4096]{1,0:T(8,128)(2,1)} fusion(bf16[16,128,4096]{2,1,0:T(8,128)(2,1)} %all-gather.11.cloned.1.call-done, bf16[16,256,128]{2,1,0:T(8,128)(2,1)S(1)} %copy-done.7), kind=kOutput, calls=%fused_computation.29 | convolution fusion | flops 4296015872 | bytes 19922944 | tf_op jit(solution)/shard_map/dot_general | solution.py:137
  596.7 32.5 %reduce-scatter.2.cloned.1.call-done = bf16[128,4096]{1,0:T(8,128)(2,1)} async-done(((bf16[256,4096]{1,0:T(8,128)(2,1)}), bf16[128,4096]{1,0:T(8,128)(2,1)}) %reduce-scatter.2.cloned.1.call-update) | async-done | bytes 1048592 | tf_op jit(solution)/shard_map/reduce_scatter | solution.py:136
  629.2 2.6 fusion.31
  631.7 49.5 %all-to-all-done = bf16[4,4,1,4,128,256]{5,4,3,1,2,0:T(8,128)(2,1)} async-done(((bf16[4,4,1,4,128,256]{5,4,3,1,2,0:T(8,128)(2,1)}), bf16[4,4,1,4,128,256]{5,4,3,1,2,0:T(8,128)(2,1)}, u32[]{:S(2)}, u32[]{:S(2)}) %all-to-all-start) | async-done | bytes 4194336 | tf_op jit(solution)/shard_map/all_to_all | solution.py:149
  681.2 4.7 copy.44
  (136 shorter events, 77.1 us)
Async XLA Ops:
  7.2 346.3 %copy-start = (s32[4,16]{1,0:T(4,128)S(1)}, s32[4,16]{1,0:T(4,128)}, u32[]{:S(2)}) copy-start(s32[4,16]{1,0:T(4,128)} %param.15) | copy-start | bytes 772
  7.2 1.5 copy-start.6
  7.2 38.3 %all-gather.5.cloned.1.call-start = ((), (), s32[]{:S(2)}) async-start(), calls=%async_computation.2 | async-start | bytes 3145728 | tf_op jit(solution)/shard_map/all_gather | solution.py:101
  7.9 286.2 %all-gather.7.cloned.1.call-start = ((), (), s32[]{:S(2)}) async-start(), calls=%async_computation.3 | async-start | bytes 53477376 | tf_op jit(solution)/shard_map/all_gather | solution.py:103
  8.7 390.0 %all-gather.9.cloned.1.call-start = ((), (), s32[]{:S(2)}) async-start(), calls=%async_computation.4 | async-start | bytes 10485760 | tf_op jit(solution)/shard_map/all_gather | solution.py:120
  45.4 2.2 copy-start.2
  45.5 248.7 %copy-start.5 = (f32[4096]{0:T(1024)S(1)}, f32[4096]{0:T(1024)}, u32[]{:S(2)}) copy-start(f32[4096]{0:T(1024)} %param.10) | copy-start | bytes 49156
  340.2 247.1 %all-gather.11.cloned.1.call-start = ((), (), s32[]{:S(2)}) async-start(), calls=%async_computation.5 | async-start | bytes 17825792 | tf_op jit(solution)/shard_map/all_gather | solution.py:134
  353.7 1.2 copy-start.4
  582.3 5.1 copy-start.7
  582.3 98.9 %all-to-all-start = ((bf16[4,4,1,4,128,256]{5,4,3,1,2,0:T(8,128)(2,1)}), bf16[4,4,1,4,128,256]{5,4,3,1,2,0:T(8,128)(2,1)}, u32[]{:S(2)}, u32[]{:S(2)}) async-start(bf16[4,4,1,4,128,256]{5,4,3,1,2,0:T(8,128)(2,1)} %copy.43), calls=%async_computation.1 | async-start | bytes 8388608 | tf_op jit(solution)/shard_map/all_to_all | solution.py:149
  587.3 41.9 %reduce-scatter.2.cloned.1.call-start = ((), (), s32[]{:S(2)}) async-start(), calls=%async_computation.6 | async-start | bytes 3145728 | tf_op jit(solution)/shard_map/reduce_scatter | solution.py:136
  596.7 32.5 %copy-start.3 = (bf16[1,1,128,4096]{3,2,1,0:T(8,128)(2,1)S(1)}, bf16[1,1,128,4096]{3,2,1,0:T(8,128)(2,1)}, u32[]{:S(2)}) copy-start(bf16[1,1,128,4096]{3,2,1,0:T(8,128)(2,1)} %param.9) | copy-start | bytes 3145732
  681.2 4.7 copy-start.1
Sparse Core Ops, SparseCore 0:
  9.6 35.8 all-gather.4
  47.0 247.0 all-gather.6
  340.3 58.2 all-gather.8
  400.7 130.3 all-gather.10
  596.8 32.2 reduce-scatter.1
where the time goes:
time: 695 us; the launch traced here: 692 us
  waiting for transfers between devices  406 us (58%)
  local copies, waits for them, and re-layouts  152 us (22%)
  matrix products  89.9 us (13%)
  other arithmetic  21.4 us (3%)
  between operations  17.4 us (3%)
    all_gather x1, waiting for transfers between devices, on_device(): piece = lax.all_gather(qkv_weight, ('dp', 'hg'), axis=0, tiled=True)  246 us
    all_to_all x1, waiting for transfers between devices, on_device(): lax.all_to_all(placed.astype(jnp.bfloat16).reshape(owner_count, group_hea...  49.5 us
    dynamic_update_slice x16, local copies, waits for them, and re-layouts, one_head(): lax.dynamic_update_slice(head_extended, head_stretch, (length, zero_index))  48.4 us
    all_gather x1, waiting for transfers between devices, on_device(): stretch_kv = lax.all_gather(run_kv, 'hg', axis=1, tiled=True)  41.7 us
    squeeze x32, local copies, waits for them, and re-layouts, on_device(): lax.map(one_head, (queries.transpose(1, 0, 2), extended, stretch_kv))  38.3 us
    all_gather x1, waiting for transfers between devices, on_device(): run_rows = lax.all_gather(hidden_in, 'tp', axis=2, tiled=True)[0, 0]  35 us
    reduce_scatter x1, waiting for transfers between devices, on_device(): lax.psum_scatter(jnp.dot(attended_rows, out_flat, preferred_element_type=...  32.5 us
    dot_general x1, matrix products, on_device(): jnp.dot(normed, piece.reshape(piece.shape[0], 3 * head_width), preferred_...  32.3 us
  transfers between devices with their start and end apart: 6, of which 5 were waited for; matrix products, arithmetic and copies ran while one was open for 31% of the time, Pallas kernels for 0%

commit v1 on v0

v1 whole, which is shorter than its diff:
```python
import math

import jax
import jax.numpy as jnp
from jax import lax
from jax.experimental import pallas as pl
from jax.experimental.pallas import tpu as pltpu
from jax.sharding import PartitionSpec as P

ROT = 32
BLOCK = 128
EPSILON = 1e-05
VMEM_LIMIT = 48 * 1024 * 1024

SMEM = pltpu.SMEM
BF16 = jnp.bfloat16
F32 = jnp.float32


def params():
    return pltpu.CompilerParams(vmem_limit_bytes=VMEM_LIMIT)


def cost():
    return pl.CostEstimate(flops=1, bytes_accessed=1, transcendentals=0)


def swap(x, axis, stride):
    size = lax.axis_size(axis)
    return lax.ppermute(x, axis, [(i, i ^ stride) for i in range(size)])


def halving(size, last):
    strides = []
    step = size // 2
    while step >= last:
        strides.append(step)
        step //= 2
    return strides


def offsets(strides):
    order = [0]
    for stride in strides:
        order = order + [o ^ stride for o in order]
    return order


def after(value, token):
    return lax.optimization_barrier((value, token))[0]


def dot(a, b):
    return jnp.dot(a, b, preferred_element_type=F32)


def dot_t(a, b):
    return lax.dot_general(a, b, (((1,), (1,)), ((), ())), preferred_element_type=F32)


def norm_body(depth, own_rel, meta, hidden, gain, own, sent, scratch):
    rows = hidden[...].astype(F32)
    centered = rows - jnp.mean(rows, axis=-1, keepdims=True)
    spread = jnp.mean(centered * centered, axis=-1, keepdims=True)
    scratch[...] = (centered * lax.rsqrt(spread + EPSILON) * gain[...]).astype(BF16)
    me = meta[0]
    for e, rel in enumerate(own_rel):
        start = pl.multiple_of((me ^ rel) * depth, 128)
        own[e] = scratch[:, pl.ds(start, depth)]
        start = pl.multiple_of((me ^ rel ^ 1) * depth, 128)
        sent[e] = scratch[:, pl.ds(start, depth)]


def norm_call(meta, hidden, gain, depth, own_rel):
    rows, width = hidden.shape
    shape = jax.ShapeDtypeStruct((len(own_rel), rows, depth), BF16)
    return pl.pallas_call(
        lambda *refs: norm_body(depth, own_rel, *refs),
        out_shape=(shape, shape),
        in_specs=[
            pl.BlockSpec(memory_space=SMEM),
            pl.BlockSpec(memory_space=pltpu.VMEM),
            pl.BlockSpec(memory_space=pltpu.VMEM),
        ],
        out_specs=(pl.BlockSpec(memory_space=pltpu.VMEM), pl.BlockSpec(memory_space=pltpu.VMEM)),
        scratch_shapes=[pltpu.VMEM((rows, width), BF16)],
        compiler_params=params(),
        cost_estimate=cost(),
        name="layer_norm",
    )(meta, hidden, gain)


def load_weights(hg, refs):
    weights = []
    for ref in refs:
        blocks = [ref[0, hg ^ q] for q in range(ref.shape[1])]
        weights.append(jnp.concatenate(blocks, axis=0))
    return weights


def product(xs, ws):
    total = None
    k = 0
    for x in xs:
        for e in range(x.shape[0]):
            part = x[e]
            part = part.reshape(-1, part.shape[-1])
            term = dot(part, ws[k])
            total = term if total is None else total + term
            k += 1
    return total


def whole(x):
    nd = len(x.shape)
    return pl.BlockSpec(x.shape, lambda *_: (0,) * nd)


def by_step(x, first=0):
    nd = len(x.shape) - 1
    return pl.BlockSpec((1,) + tuple(x.shape[1:]), lambda i, *_: (first + i,) + (0,) * nd)


def weight_specs(ws):
    return [by_step(w) for w in ws]


def partner_body(streams, count, meta, *refs):
    xs, ws, out = refs[: 2 * streams], refs[2 * streams : 2 * streams + count], refs[-1]
    ws = load_weights(meta[2], ws)
    half = out.shape[1] // 2
    for core in (0, 1):
        out[0, core * half : (core + 1) * half] = product(xs[core * streams : (core + 1) * streams], ws).astype(BF16)


def partner_call(meta, xs, ws, rows, heads):
    streams = len(xs) // 2
    width = ws[0].shape[-1]
    out = jax.ShapeDtypeStruct((heads, rows, width), BF16)
    return pl.pallas_call(
        lambda *refs: partner_body(streams, len(ws), *refs),
        out_shape=out,
        grid_spec=pltpu.PrefetchScalarGridSpec(
            num_scalar_prefetch=1,
            grid=(heads,),
            in_specs=[whole(x) for x in xs] + weight_specs(ws),
            out_specs=by_step(out),
        ),
        compiler_params=params(),
        cost_estimate=cost(),
        name="partner_product",
    )(meta, *xs, *ws)


def finish_body(streams, count, cap, order_h, order_t, meta, lengths, owners, *refs):
    xs, ws = refs[: 2 * streams], refs[2 * streams : 2 * streams + count]
    arrived, cosine, sine, cache, query, kv = refs[2 * streams + count : 2 * streams + count + 6]
    placed, total, slots, counts = refs[-4:]
    me, tp, hg = meta[0], meta[1], meta[2]
    ws = load_weights(hg, ws)
    half = total.shape[0] // 2
    for core in (0, 1):
        rows = slice(core * half, (core + 1) * half)
        total[rows] = product(xs[core * streams : (core + 1) * streams], ws) + arrived[0, rows].astype(F32)
    hd = query.shape[2]
    nt = len(order_t)
    run_rows = total.shape[0] // (len(order_h) * nt)
    lane = lax.broadcasted_iota(jnp.int32, (run_rows, hd), 1)
    half_rot = ROT // 2
    m = 0
    for rel_h in order_h:
        for rel_t in order_t:
            start = pl.multiple_of(((hg ^ rel_h) * nt + (tp ^ rel_t)) * run_rows, run_rows)
            rows = slice(m * run_rows, (m + 1) * run_rows)
            cos_rows, sin_rows = cosine[pl.ds(start, run_rows)], sine[pl.ds(start, run_rows)]

            def rotated(part):
                other = jnp.where(
                    lane < half_rot, pltpu.roll(part, hd - half_rot, 1), pltpu.roll(part, half_rot, 1)
                )
                return (part * cos_rows + other * sin_rows).astype(BF16)

            query[0, pl.ds(start, run_rows)] = rotated(total[rows, :hd])
            kv[0, pl.ds(start, run_rows), :hd] = rotated(total[rows, hd : 2 * hd])
            kv[0, pl.ds(start, run_rows), hd:] = total[rows, 2 * hd :].astype(BF16)
            m += 1
    owner_count = placed.shape[0]
    blocks = owners.shape[1]
    cached_blocks = lengths[me] // BLOCK
    valid_end = cached_blocks + query.shape[1] // BLOCK
    for s in range(owner_count * cap):
        slots[s] = -1
    for o in range(owner_count):
        counts[o] = 0
    for b in range(blocks):

        @pl.when(b < valid_end)
        def _():
            owner = owners[me, b]
            rank = counts[owner]

            @pl.when(rank < cap)
            def _():
                slots[owner * cap + rank] = b

            counts[owner] = rank + 1

    for s in range(owner_count * cap):
        block = slots[s]
        o, c = divmod(s, cap)

        @pl.when(block < 0)
        def _():
            placed[o, 0, c] = jnp.zeros(placed.shape[3:], BF16)

        @pl.when((block >= 0) & (block < cached_blocks))
        def _():
            at = pl.multiple_of(block * BLOCK, BLOCK)
            placed[o, 0, c] = cache[0, 0, pl.ds(at, BLOCK)]

        @pl.when(block >= cached_blocks)
        def _():
            at = pl.multiple_of((block - cached_blocks) * BLOCK, BLOCK)
            placed[o, 0, c] = kv[0, pl.ds(at, BLOCK)]


def cache_by_step(cache, first):
    return pl.BlockSpec((1, 1) + cache.shape[2:], lambda i, meta, *_: (0, meta[3] + first + i, 0, 0))


def finish_call(meta, lengths, owners, xs, ws, arrived, cosine, sine, cache, first, cap, owner_count, order_h, order_t):
    streams = len(xs) // 2
    heads, rows, width = arrived.shape
    hd = width // 3
    cache_spec = cache_by_step(cache, first)
    outs = [(heads, rows, hd), (heads, rows, 2 * hd), (owner_count, heads, cap, BLOCK, 2 * hd)]
    outs = tuple(jax.ShapeDtypeStruct(o, BF16) for o in outs)
    placed_spec = pl.BlockSpec((owner_count, 1, cap, BLOCK, 2 * hd), lambda i, *_: (0, i, 0, 0, 0))
    return pl.pallas_call(
        lambda *refs: finish_body(streams, len(ws), cap, order_h, order_t, *refs),
        out_shape=outs,
        grid_spec=pltpu.PrefetchScalarGridSpec(
            num_scalar_prefetch=3,
            grid=(heads,),
            in_specs=[whole(x) for x in xs]
            + weight_specs(ws)
            + [by_step(arrived), whole(cosine), whole(sine), cache_spec],
            out_specs=(by_step(outs[0]), by_step(outs[1]), placed_spec),
            scratch_shapes=[
                pltpu.VMEM((rows, width), F32),
                pltpu.SMEM((owner_count * cap,), jnp.int32),
                pltpu.SMEM((owner_count,), jnp.int32),
            ],
        ),
        compiler_params=params(),
        cost_estimate=cost(),
        name="finish_projection",
    )(meta, lengths, owners, *xs, *ws, arrived, cosine, sine, cache)


def attend_body(q_rows, meta, lengths, query, kv, cache, out):
    hd = query.shape[2]
    length = lengths[meta[0]]
    factor = math.log2(math.e) / math.sqrt(hd)
    old_col = lax.broadcasted_iota(jnp.int32, (q_rows, cache.shape[2]), 1)
    causal = lax.broadcasted_iota(jnp.int32, (q_rows, q_rows), 1) <= lax.broadcasted_iota(
        jnp.int32, (q_rows, q_rows), 0
    )
    for step in range(query.shape[1] // q_rows):
        first = step * q_rows
        q = query[0, first : first + q_rows]
        old = jnp.where(old_col < length, dot_t(q, cache[0, 0, :, :hd]), -jnp.inf)
        diag = jnp.where(causal, dot_t(q, kv[0, first : first + q_rows, :hd]), -jnp.inf)
        top = jnp.maximum(jnp.max(old, axis=1, keepdims=True), jnp.max(diag, axis=1, keepdims=True))
        if step:
            new = dot_t(q, kv[0, :first, :hd])
            top = jnp.maximum(top, jnp.max(new, axis=1, keepdims=True))
        old = jnp.exp2((old - top) * factor)
        diag = jnp.exp2((diag - top) * factor)
        total = jnp.sum(old, axis=1, keepdims=True) + jnp.sum(diag, axis=1, keepdims=True)
        result = dot(old.astype(BF16), cache[0, 0, :, hd:]) + dot(diag.astype(BF16), kv[0, first : first + q_rows, hd:])
        if step:
            new = jnp.exp2((new - top) * factor)
            total = total + jnp.sum(new, axis=1, keepdims=True)
            result = result + dot(new.astype(BF16), kv[0, :first, hd:])
        out[0, first : first + q_rows] = (result / total).astype(BF16)


def attend_call(meta, lengths, query, kv, cache, first, q_rows=256):
    heads, rows, hd = query.shape
    out = jax.ShapeDtypeStruct((heads, rows, hd), BF16)
    return pl.pallas_call(
        lambda *refs: attend_body(q_rows, *refs),
        out_shape=out,
        grid_spec=pltpu.PrefetchScalarGridSpec(
            num_scalar_prefetch=2,
            grid=(heads,),
            in_specs=[by_step(query), by_step(kv), cache_by_step(cache, first)],
            out_specs=by_step(out),
        ),
        compiler_params=params(),
        cost_estimate=cost(),
        name="attention",
    )(meta, lengths, query, kv, cache)


def split_body(order_t, meta, *refs):
    held, outs = refs[: -len(order_t)], refs[-len(order_t) :]
    cols = outs[0].shape[-1]
    for r, out in zip(order_t, outs):
        start = pl.multiple_of((meta[1] ^ r) * cols, cols)
        for d, ref in enumerate(held):
            out[d] = ref[:, :, pl.ds(start, cols)]


def split_call(meta, held, order_t):
    heads, hd, width = held[0].shape
    cols = width // len(order_t)
    if cols % 128:
        stacked = jnp.stack(held).reshape(len(held), heads, hd, len(order_t), cols)
        return [lax.dynamic_index_in_dim(stacked, meta[1] ^ r, 3, keepdims=False) for r in order_t]
    vmem = pl.BlockSpec(memory_space=pltpu.VMEM)
    return pl.pallas_call(
        lambda *refs: split_body(order_t, *refs),
        out_shape=[jax.ShapeDtypeStruct((len(held), heads, hd, cols), BF16) for _ in order_t],
        in_specs=[pl.BlockSpec(memory_space=SMEM)] + [vmem] * len(held),
        out_specs=[vmem] * len(order_t),
        compiler_params=params(),
        cost_estimate=cost(),
        name="split_columns",
    )(meta, *held)


def output_body(first, heads, group, order_h, order_t, with_sum, meta, *refs):
    parts, weights = refs[: 2 * heads], refs[2 * heads : 2 * heads + len(order_t)]
    out = refs[-1]
    hg = meta[2]
    dps = weights[0].shape[0]
    total = refs[-2][...] if with_sum else None
    for j in range(heads):
        left, right = [], []
        for i, rel_h in enumerate(order_h):
            core, h = divmod(i, len(order_h) // 2)
            for t in range(len(order_t)):
                left.append(parts[2 * j + core][h, t])
                head = (hg ^ rel_h) * group + first + j
                right.append(jnp.concatenate([weights[t][meta[4 + d], head] for d in range(dps)], axis=1))
        term = dot(jnp.concatenate(left, axis=1), jnp.concatenate(right, axis=0))
        total = term if total is None else total + term
    out[...] = total.astype(out.dtype)


def output_call(meta, parts, weights, rows, first, group, order_h, order_t, total=None, dtype=F32):
    dps, _, _, cols = weights[0].shape
    vmem = pl.BlockSpec(memory_space=pltpu.VMEM)
    operands = (meta, *parts, *weights) + (() if total is None else (total,))
    return pl.pallas_call(
        lambda *refs: output_body(first, len(parts) // 2, group, order_h, order_t, total is not None, *refs),
        out_shape=jax.ShapeDtypeStruct((rows, dps * cols), dtype),
        in_specs=[pl.BlockSpec(memory_space=SMEM)] + [vmem] * (len(operands) - 1),
        out_specs=vmem,
        compiler_params=params(),
        cost_estimate=cost(),
        name="output_projection",
    )(*operands)


def output_plain(meta, tp, hg, parts, weights, rows, group, order_h, order_t):
    del tp
    dps, heads, hd, cols = weights[0].shape
    stacked = jnp.stack(weights).reshape(len(order_t), dps, len(order_h), group, hd, cols)
    stacked = jnp.take(stacked, meta[4 : 4 + dps], axis=1)
    stacked = jnp.take(stacked, hg ^ jnp.array(order_h, jnp.int32), axis=2)
    total = None
    for j in range(group):
        left = jnp.concatenate([parts[2 * j], parts[2 * j + 1]], axis=0)
        left = left.transpose(2, 0, 1, 3).reshape(rows, -1)
        right = stacked[:, :, :, j].transpose(2, 0, 3, 1, 4).reshape(-1, dps * cols)
        term = dot(left, right)
        total = term if total is None else total + term
    return total.astype(BF16)


def collect_body(*refs):
    head = 0
    for piece in refs[:-1]:
        for j in range(piece.shape[1]):
            refs[-1][0, head, 0] = piece[0, j]
            head += 1


def collect_call(pieces):
    heads = sum(p.shape[1] for p in pieces)
    requests = pieces[0].shape[0]
    tail = pieces[0].shape[2:]
    return pl.pallas_call(
        collect_body,
        grid=(requests,),
        out_shape=jax.ShapeDtypeStruct((1, heads, requests) + tail, BF16),
        in_specs=[by_step(p) for p in pieces],
        out_specs=pl.BlockSpec((1, heads, 1) + tail, lambda r: (0, 0, r, 0, 0, 0)),
        compiler_params=params(),
        cost_estimate=cost(),
        name="collect_blocks",
    )(*pieces)


def residual_body(nd, hidden, summed, out):
    members, _, columns = summed.shape
    cols = columns // nd
    for d in range(nd):
        for m in range(members):
            at = slice((d * members + m) * cols, (d * members + m + 1) * cols)
            out[:, at] = (hidden[:, at].astype(F32) + summed[m, :, d * cols : (d + 1) * cols].astype(F32)).astype(BF16)


def residual_call(hidden, summed, nd):
    vmem = pl.BlockSpec(memory_space=pltpu.VMEM)
    return pl.pallas_call(
        lambda *refs: residual_body(nd, *refs),
        out_shape=jax.ShapeDtypeStruct(hidden.shape, BF16),
        in_specs=[vmem, vmem],
        out_specs=vmem,
        compiler_params=params(),
        cost_estimate=cost(),
        name="residual",
    )(hidden, summed)


def plane_gather(x, dim_h, dim_t, h_strides, t_strides, h_first, token=None):
    def over_h(x):
        for s in h_strides[:-1]:
            x = jnp.concatenate([x, swap(x, "hg", s)], axis=dim_h)
        return x

    def over_t(x):
        for s in t_strides:
            x = jnp.concatenate([x, swap(x, "tp", s)], axis=dim_t)
        return x

    x = over_t(over_h(x)) if h_first else over_h(over_t(x))
    if token is not None:
        x = after(x, token)
    return x, swap(x, "hg", h_strides[-1])


def head_gather(attended, h_strides, t_strides, token=None):
    parts = []
    for j in range(attended.shape[0]):
        parts += plane_gather(attended[j][None, None], 0, 1, h_strides, t_strides, j % 2 == 0, token)
    return parts


def chunks_of(group):
    return [group // 2, group - group // 2] if group > 1 else [1]


def on_device(hidden_in, norm_gain, qkv_weight, out_weight, cache_kv, cached_lengths, owner_table):
    nt, nh, nd = lax.axis_size("tp"), lax.axis_size("hg"), lax.axis_size("dp")
    tp, hg, dp = lax.axis_index("tp"), lax.axis_index("hg"), lax.axis_index("dp")
    local_rows, width = hidden_in.shape[2:]
    local_depth, _, local_heads, hd = qkv_weight.shape
    group = local_heads // nh
    depth = local_depth * nh
    rows = local_rows * nt * nh
    cap = (cache_kv.shape[2] + rows) // BLOCK // nd
    length = lax.dynamic_index_in_dim(cached_lengths, dp, 0, keepdims=False)

    far, all_d = halving(nd, 2), halving(nd, 1)
    own_rel = offsets(far)
    h_strides, t_strides = halving(nh, 1), halving(nt, 1)
    order_h, order_t = offsets(h_strides), offsets(t_strides)
    members = dp ^ jnp.arange(nd, dtype=jnp.int32)
    place = sum(jnp.where(members == rel, k, 0) for k, rel in enumerate(offsets(all_d))).astype(jnp.int32)
    meta = jnp.concatenate([jnp.stack([dp, tp, hg, hg * group]).astype(jnp.int32), place])

    out_held = [out_weight]
    for s in far:
        out_held = out_held + [swap(w, "dp", s) for w in out_held]
    out_near = [swap(out_weight, "dp", 1)]
    by_head = qkv_weight.reshape(local_depth, 3, nh, group, hd).transpose(2, 3, 0, 1, 4)
    by_head = by_head.reshape(nh, group, local_depth, 3 * hd)
    given = [lax.dynamic_index_in_dim(by_head, hg ^ s, 0, keepdims=False) for s in range(nh)]
    own, sent = norm_call(meta, hidden_in[0, 0], norm_gain.reshape(1, width), depth, own_rel)
    sent = swap(sent, "dp", 1)

    positions = length + jnp.arange(rows, dtype=jnp.int32)
    half_rot = ROT // 2
    frequency = 10000.0 ** (-2.0 * jnp.arange(half_rot, dtype=F32) / ROT)
    angles = positions.astype(F32)[:, None] * frequency[None, :]
    cos_half, sin_half = jnp.cos(angles), jnp.sin(angles)
    cosine = jnp.concatenate([cos_half, cos_half, jnp.ones((rows, hd - ROT), F32)], axis=1)
    sine = jnp.concatenate([-sin_half, sin_half, jnp.zeros((rows, hd - ROT), F32)], axis=1)
    sizes = chunks_of(group)
    firsts = [sum(sizes[:c]) for c in range(len(sizes))]
    mine = []
    for f, size in zip(firsts, sizes):
        parts = [piece[f : f + size] for piece in given]
        mine.append(jnp.stack([swap(p, "hg", s) if s else p for s, p in enumerate(parts)], axis=1))

    live = dict(out=out_held, near=out_near, mine=mine, x=(own, sent), tables=(cosine, sine))
    live = lax.optimization_barrier(live)

    cols = out_weight.shape[2] // nt
    weights, arrived, gathered, handed = [], [], [], []
    chunks = len(sizes)
    for stage in range(1, chunks + 3):
        c = stage - 1
        if c < chunks:
            held = [live["mine"][c]]
            for s in far:
                held = held + [swap(w, "dp", s) for w in held]
            weights.append(held)
        if stage == 1:
            cut = len(own_rel) // 2
            for name, x in zip(("own", "pair"), live.pop("x")):
                x = x[:, None, None]
                streams = [
                    plane_gather(x[:cut], 1, 2, h_strides, t_strides, True),
                    plane_gather(x[cut:], 1, 2, h_strides, t_strides, False),
                ]
                live[name] = [s[0] for s in streams] + [s[1] for s in streams]
            live["near"] = live["near"] + [swap(w, "dp", 1) for w in live["out"][1:]]
        if stage == 2:
            held = split_call(meta, live.pop("out") + live.pop("near"), order_t)
            live["out_weights"] = [swap(w, "tp", r) if r else w for w, r in zip(held, order_t)]
        if "attended" in live:
            gathered.append(head_gather(live["attended"], h_strides, t_strides))
        c = stage - 3
        if 0 <= c < chunks:
            query, kv, placed = finish_call(
                meta, cached_lengths, owner_table, live["own"], live["weights"][c], live["arrived"][c],
                *live["tables"], cache_kv, firsts[c], cap, nd, order_h, order_t,
            )
            handed.append(lax.all_to_all(placed, "dp", 0, 0, tiled=True))
            live["attended"] = attend_call(meta, cached_lengths, query, kv, cache_kv, firsts[c])
        c = stage - 2
        if 0 <= c < chunks:
            partial = partner_call(meta, live["pair"], live["weights"][c], rows, sizes[c])
            arrived.append(swap(partial, "dp", 1))
        if stage == chunks + 2:
            break
        live.update(weights=weights, arrived=arrived, handed=handed, gathered=gathered)
        live = lax.optimization_barrier(live)
        weights, arrived, handed, gathered = (list(live[k]) for k in ("weights", "arrived", "handed", "gathered"))
    out_weights = live["out_weights"]
    attended = live["attended"]
    if cols % 128 == 0:
        summed = None
        for c, parts in enumerate(gathered):
            summed = output_call(meta, parts, out_weights, rows, firsts[c], group, order_h, order_t, summed)
        parts = head_gather(attended, h_strides, t_strides, summed)
        summed = output_call(meta, parts, out_weights, rows, firsts[-1], group, order_h, order_t, summed, BF16)
    else:
        gathered.append(head_gather(attended, h_strides, t_strides))
        parts = [p for parts in gathered for p in parts]
        summed = output_plain(meta, tp, hg, parts, out_weights, rows, group, order_h, order_t)
    summed = after(summed, handed[-1])
    summed = lax.all_to_all(
        summed.reshape(nh * nt, local_rows, nd * cols), ("hg", "tp"), 0, 0, tiled=True
    )
    if cols % 128 == 0:
        hidden_out = residual_call(hidden_in[0, 0], summed, nd)
    else:
        summed = summed.reshape(nh, nt, local_rows, nd, cols).transpose(2, 3, 0, 1, 4).reshape(local_rows, width)
        hidden_out = (hidden_in[0, 0].astype(F32) + summed.astype(F32)).astype(BF16)
    return hidden_out[None, None], collect_call(handed)


def solution(mesh):
    return jax.shard_map(
        on_device,
        mesh=mesh,
        in_specs=(
            P("dp", "hg", "tp", None),
            P(),
            P(("dp", "hg"), None, "tp", None),
            P("tp", None, ("dp", "hg")),
            P("dp", "tp", None, None),
            P(),
            P(),
        ),
        out_specs=(P("dp", "hg", "tp", None), P("dp", ("tp", "hg"), None, None, None, None)),
        check_vma=False,
    )
```

time: 695 us -> 429 us (0.62)
  waiting for transfers between devices: 406 us -> 244 us
  local copies, waits for them, and re-layouts: 152 us -> 41.5 us
  matrix products: 89.9 us -> 0 us
  Pallas kernels: 0 us -> 74.1 us
  starting transfers between devices: 5.18 us -> 56 us
  between operations: 17.4 us -> 1.16 us
  other arithmetic: 21.4 us -> 11.4 us
    all_gather x4 -> x0, waiting for transfers between devices: 323 us -> none  [the longest x1 246 us: on_device(): piece = lax.all_gather(qkv_weight, ('dp', 'hg'), axis=0, tiled=True)]
    ppermute x0 -> x39, waiting for transfers between devices: none -> 233 us  [swap(): return lax.ppermute(x, axis, [(i, i ^ stride) for i in range(size)])]
    dot_general x35 -> x0, matrix products: 89.9 us -> none  [the longest x1 32.3 us: on_device(): jnp.dot(normed, piece.reshape(piece.shape[0], 3 * head_width), preferred_...]
    pallas_call x0 -> x12, Pallas kernels: none -> 74.1 us  [the longest x2 20.5 us: finish_call(): pl.pallas_call(lambda *refs: finish_body(streams, len(ws), cap, order_h,...]
    dynamic_update_slice x32 -> x0, local copies, waits for them, and re-layouts: 65.3 us -> none  [the longest x16 48.4 us: one_head(): lax.dynamic_update_slice(head_extended, head_stretch, (length, zero_index))]
    ppermute x0 -> x39, starting transfers between devices: none -> 43.5 us  [swap(): return lax.ppermute(x, axis, [(i, i ^ stride) for i in range(size)])]
    all_to_all x1 -> x3, waiting for transfers between devices: 49.5 us -> 10.2 us  [the longest x1 10.2 us: on_device(): lax.all_to_all(summed.reshape(nh * nt, local_rows, nd * cols), ('hg', 'tp...]
    squeeze x32 -> x0, local copies, waits for them, and re-layouts: 38.3 us -> none  [on_device(): lax.map(one_head, (queries.transpose(1, 0, 2), extended, stretch_kv))]
  transfers between devices with their start and end apart: 6 -> 42, of which waited for: 5 -> 19; matrix products, arithmetic and copies ran while one was open for 31% -> 6% of each run, Pallas kernels for 0% -> 13%
where the time goes in v1:
time: 429 us; the launch traced here: 428 us
  waiting for transfers between devices  244 us (57%)
  Pallas kernels  74.1 us (17%)
  starting transfers between devices  56 us (13%)
  local copies, waits for them, and re-layouts  41.5 us (10%)
  other arithmetic  11.4 us (3%)
    ppermute x39, waiting for transfers between devices, swap(): return lax.ppermute(x, axis, [(i, i ^ stride) for i in range(size)])  233 us
    ppermute x39, starting transfers between devices, swap(): return lax.ppermute(x, axis, [(i, i ^ stride) for i in range(size)])  43.5 us
    unnamed x103, local copies, waits for them, and re-layouts  29.8 us
    pallas_call x2, Pallas kernels, finish_call(): pl.pallas_call(lambda *refs: finish_body(streams, len(ws), cap, order_h,...  20.5 us
    pallas_call x2, Pallas kernels, attend_call(): pl.pallas_call(lambda *refs: attend_body(q_rows, *refs), out_shape=out, g...  15.4 us
    pallas_call x2, Pallas kernels, partner_call(): pl.pallas_call(lambda *refs: partner_body(streams, len(ws), *refs), out_s...  13.4 us
    pallas_call x2, Pallas kernels, output_call(): pl.pallas_call(lambda *refs: output_body(first, len(parts) // 2, group, o...  12.1 us
    all_to_all x1, waiting for transfers between devices, on_device(): lax.all_to_all(summed.reshape(nh * nt, local_rows, nd * cols), ('hg', 'tp...  10.2 us
  transfers between devices with their start and end apart: 42, of which 19 were waited for; matrix products, arithmetic and copies ran while one was open for 6% of the time, Pallas kernels for 13%

profile of v1, /device:TPU:0, one launch (start us, length us, event | category | flops | bytes accessed | tf_op | source)
XLA Modules:
  0.0 427.7 jit_solution(13965555844531117278)
XLA Ops:
  0.6 4.9 %copy.29 = bf16[256,3,16,128]{0,3,1,2:T(8,128)(2,1)} copy(bf16[256,3,16,128]{3,2,1,0:T(8,128)(2,1)} %param.9) | data formatting | bytes 6291456 | tf_op args[2]
  5.5 3.5 constant_dynamic-slice_fusion.7
  10.4 2.6 collective-permute-start.6
  13.0 2.6 collective-permute-start.7
  15.5 1.9 copy.52
  17.4 1.5 collective-permute-start.4
  18.9 1.9 copy.53
  20.9 1.9 copy.45
  23.5 1.5 layer_norm.1
  26.6 2.0 copy.50
  28.6 1.9 copy.47
  33.2 1.9 fusion
  35.2 1.6 collective-permute-start.1
  36.7 1.6 collective-permute-start.2
  39.1 1.8 pad_maximum_fusion.1.refs_5_.refs_7_
  41.0 6.3 %collective-permute-done.1 = bf16[2,256,384]{2,1,0:T(8,128)(2,1)S(1)} collective-permute-done((bf16[2,256,384]{2,1,0:T(8,128)(2,1)S(1)}, bf16[2,256,384]{2,1,0:T(8,128)(2,1)S(1)}, u32[]{:S(2)}, u32[]{:S(2)}) %collective-permute-start.1) | collective-permute-done | bytes 393248 | tf_op jit(solution)/shard_map/ppermute | solution.py:30
  47.2 6.5 %collective-permute-done.2 = bf16[2,256,384]{2,1,0:T(8,128)(2,1)S(1)} collective-permute-done((bf16[2,256,384]{2,1,0:T(8,128)(2,1)S(1)}, bf16[2,256,384]{2,1,0:T(8,128)(2,1)S(1)}, u32[]{:S(2)}, u32[]{:S(2)}) %collective-permute-start.2) | collective-permute-done | bytes 393248 | tf_op jit(solution)/shard_map/ppermute | solution.py:30
  53.8 1.3 pad_maximum_fusion
  55.1 15.4 %collective-permute-done.8 = bf16[2,128,1024]{2,1,0:T(8,128)(2,1)S(1)} collective-permute-done((bf16[2,128,1024]{2,1,0:T(8,128)(2,1)S(1)}, bf16[2,128,1024]{2,1,0:T(8,128)(2,1)S(1)}, u32[]{:S(2)}, u32[]{:S(2)}) %collective-permute-start.8) | collective-permute-done | bytes 524320 | tf_op jit(solution)/shard_map/ppermute | solution.py:30
  70.5 1.8 collective-permute-start.18
  72.3 1.5 collective-permute-start.16
  74.4 5.4 %collective-permute-done.18 = bf16[1,1,1,128,1024]{4,3,2,1,0:T(8,128)(2,1)S(1)} collective-permute-done((bf16[1,1,1,128,1024]{4,3,2,1,0:T(8,128)(2,1)S(1)}, bf16[1,1,1,128,1024]{4,3,2,1,0:T(8,128)(2,1)S(1)}, u32[]{:S(2)}, u32[]{:S(2)}) %collective-permute-start.18) | collective-permute-done | bytes 262176 | tf_op jit(solution)/shard_map/ppermute | solution.py:30
  79.9 1.8 collective-permute-start.19
  81.9 1.8 collective-permute-start.9
  83.8 1.6 collective-permute-start.17
  85.5 1.6 collective-permute-start.13
  87.0 13.4 %collective-permute-done.10 = bf16[1,1,1,128,1024]{4,3,2,1,0:T(8,128)(2,1)S(1)} collective-permute-done((bf16[1,1,1,128,1024]{4,3,2,1,0:T(8,128)(2,1)S(1)}, bf16[1,1,1,128,1024]{4,3,2,1,0:T(8,128)(2,1)S(1)}, u32[]{:S(2)}, u32[]{:S(2)}) %collective-permute-start.10) | collective-permute-done | bytes 262176 | tf_op jit(solution)/shard_map/ppermute | solution.py:30
  100.5 1.8 collective-permute-start.11
  102.2 2.6 collective-permute-start.22
  105.2 3.4 collective-permute-done.13
  109.8 2.8 collective-permute-done.9.refs_4_
  112.6 53.5 %collective-permute-done.22 = bf16[2,4,256,384]{3,2,0,1:T(8,128)(2,1)S(1)} collective-permute-done((bf16[2,4,256,384]{3,2,0,1:T(8,128)(2,1)S(1)}, bf16[2,4,256,384]{3,2,0,1:T(8,128)(2,1)S(1)}, u32[]{:S(2)}, u32[]{:S(2)}) %collective-permute-start.22) | collective-permute-done | bytes 1572896 | tf_op jit(solution)/shard_map/ppermute | solution.py:30
  168.3 4.3 %split_columns.1 = (bf16[4,16,128,128]{3,2,1,0:T(8,128)(2,1)}, bf16[4,16,128,128]{3,2,1,0:T(8,128)(2,1)}) custom-call(s32[8]{0:T(128)S(1)} %concatenate.57.refs_0_, bf16[16,128,256]{2,1,0:T(8,128)(2,1)S(1)} %copy-done.16, bf16[16,128,256]{2,1,0:T(8,128)(2,1)} %collective-permute-done.7.refs_2_, bf16[16,128,256]{2,1,0:T(8,128)(2,1)S(1)} %copy-done.18, ...), custom_call_target="tpu_custom_call" | custom-call | flops 1 | bytes 1 | tf_op jit(solution)/shard_map/split_columns/pallas_call | solution.py:323
  173.9 1.3 copy.38.refs_5_
  175.2 1.3 copy.39.refs_6_
  176.5 6.8 %partner_product.2 = bf16[2,1024,384]{2,1,0:T(8,128)(2,1)S(1)} custom-call(s32[8]{0:T(128)S(1)} %concatenate.57.refs_0_, bf16[1,2,2,128,1024]{4,3,2,1,0:T(8,128)(2,1)S(1)} %pad_maximum_fusion.4.refs_1_, bf16[1,2,2,128,1024]{4,3,2,1,0:T(8,128)(2,1)S(1)} %pad_maximum_fusion.5.refs_2_, bf16[1,2,2,128,1024]{4,3,2,1,0:T(8,128)(2,1)S(1)} %collective-permute-done.20.refs_3_, ...), custom_call_target="tpu_custom_call" | custom-call | flops 1 | bytes 1 | tf_op jit(solution)/shard_map/partner_product/pallas_call | solution.py:140
  183.5 3.4 collective-permute-start.25
  186.8 60.5 %collective-permute-done.23.refs_9_ = bf16[2,1024,384]{2,1,0:T(8,128)(2,1)S(1)} collective-permute-done((bf16[2,1024,384]{2,1,0:T(8,128)(2,1)S(1)}, bf16[2,1024,384]{2,1,0:T(8,128)(2,1)S(1)}, u32[]{:S(2)}, u32[]{:S(2)}) %collective-permute-start.23) | collective-permute-done | bytes 1572896 | tf_op jit(solution)/shard_map/ppermute | solution.py:30
  247.4 2.9 collective-permute-done.25.refs_6_.refs_8_
  250.3 1.3 copy.40.refs_7_
  252.9 1.3 copy.41.refs_8_
  254.3 10.2 %finish_projection.2 = (bf16[2,1024,128]{2,1,0:T(8,128)(2,1)S(1)}, bf16[2,1024,256]{2,1,0:T(8,128)(2,1)S(1)}, bf16[4,2,4,128,256]{4,3,2,1,0:T(8,128)(2,1)}) custom-call(s32[8]{0:T(128)S(1)} %concatenate.57.refs_0_, s32[4]{0:T(128)S(1)} %copy-done.30, s32[4,16]{1,0:T(4,128)S(1)} %copy-done.31, bf16[1,2,2,128,1024]{4,3,2,1,0:T(8,128)(2,1)S(1)} %pad_maximum_fusion.2.refs_3_, ...), custom_call_target="tpu_custom_call" | custom-call | flops 1 | bytes 1 | tf_op jit(solution)/shard_map/finish_projection/pallas_call | solution.py:239
  266.3 4.4 %all-to-all-start = ((bf16[4,2,4,128,256]{4,3,2,1,0:T(8,128)(2,1)}), bf16[4,2,4,128,256]{4,3,2,1,0:T(8,128)(2,1)}, u32[]{:S(2)}, u32[]{:S(2)}) async-start(bf16[4,2,4,128,256]{4,3,2,1,0:T(8,128)(2,1)} %get-tuple-element.118), calls=%async_computation | async-start | bytes 4194304 | tf_op jit(solution)/shard_map/all_to_all | solution.py:535
  274.5 6.6 %partner_product.3 = bf16[2,1024,384]{2,1,0:T(8,128)(2,1)S(1)} custom-call(s32[8]{0:T(128)S(1)} %concatenate.57.refs_0_, bf16[1,2,2,128,1024]{4,3,2,1,0:T(8,128)(2,1)S(1)} %copy-done.1, bf16[1,2,2,128,1024]{4,3,2,1,0:T(8,128)(2,1)S(1)} %pad_maximum_fusion.5.refs_2_, bf16[1,2,2,128,1024]{4,3,2,1,0:T(8,128)(2,1)S(1)} %copy-done.11, ...), custom_call_target="tpu_custom_call" | custom-call | flops 1 | bytes 1 | tf_op jit(solution)/shard_map/partner_product/pallas_call | solution.py:140
  281.1 2.0 collective-permute-start.26
  283.1 7.7 %attention.2 = bf16[2,1024,128]{2,1,0:T(8,128)(2,1)S(1)} custom-call(s32[8]{0:T(128)S(1)} %concatenate.57.refs_0_, s32[4]{0:T(128)S(1)} %copy-done.30, bf16[2,1024,128]{2,1,0:T(8,128)(2,1)S(1)} %copy-done.28, bf16[2,1024,256]{2,1,0:T(8,128)(2,1)S(1)} %copy-done.22, bf16[1,16,1024,256]{3,2,1,0:T(8,128)(2,1)} %refs_4_.3), custom_call_target="tpu_custom_call" | custom-call | flops 1 | bytes 1 | tf_op jit(solution)/shard_map/attention/pallas_call | solution.py:292
  291.7 44.4 %collective-permute-done.26.refs_9_ = bf16[2,1024,384]{2,1,0:T(8,128)(2,1)} collective-permute-done((bf16[2,1024,384]{2,1,0:T(8,128)(2,1)S(1)}, bf16[2,1024,384]{2,1,0:T(8,128)(2,1)}, u32[]{:S(2)}, u32[]{:S(2)}) %collective-permute-start.26) | collective-permute-done | bytes 1572896 | tf_op jit(solution)/shard_map/ppermute | solution.py:30
  336.1 1.9 slice_bitcast_fusion.2
  339.0 1.5 collective-permute-start.29
  340.5 10.3 %finish_projection.3 = (bf16[2,1024,128]{2,1,0:T(8,128)(2,1)S(1)}, bf16[2,1024,256]{2,1,0:T(8,128)(2,1)S(1)}, bf16[4,2,4,128,256]{4,3,2,1,0:T(8,128)(2,1)}) custom-call(s32[8]{0:T(128)S(1)} %concatenate.57.refs_0_, s32[4]{0:T(128)S(1)} %copy-done.30, s32[4,16]{1,0:T(4,128)S(1)} %copy-done.31, bf16[1,2,2,128,1024]{4,3,2,1,0:T(8,128)(2,1)S(1)} %pad_maximum_fusion.2.refs_3_, ...), custom_call_target="tpu_custom_call" | custom-call | flops 1 | bytes 1 | tf_op jit(solution)/shard_map/finish_projection/pallas_call | solution.py:239
  352.6 3.8 all-to-all-start.1
  360.3 7.7 %attention.3 = bf16[2,1024,128]{2,1,0:T(8,128)(2,1)S(1)} custom-call(s32[8]{0:T(128)S(1)} %concatenate.57.refs_0_, s32[4]{0:T(128)S(1)} %copy-done.30, bf16[2,1024,128]{2,1,0:T(8,128)(2,1)S(1)} %copy-done.26, bf16[2,1024,256]{2,1,0:T(8,128)(2,1)S(1)} %copy-done.20, bf16[1,16,1024,256]{3,2,1,0:T(8,128)(2,1)} %refs_4_.3), custom_call_target="tpu_custom_call" | custom-call | flops 1 | bytes 1 | tf_op jit(solution)/shard_map/attention/pallas_call | solution.py:292
  369.2 1.5 collective-permute-start.27
  374.2 1.8 collective-permute-done.36
  376.1 1.6 collective-permute-start.37
  378.7 10.0 %collective-permute-done.37 = bf16[1,2,1024,128]{3,2,1,0:T(8,128)(2,1)S(1)} collective-permute-done((bf16[1,2,1024,128]{3,2,1,0:T(8,128)(2,1)S(1)}, bf16[1,2,1024,128]{3,2,1,0:T(8,128)(2,1)S(1)}, u32[]{:S(2)}, u32[]{:S(2)}) %collective-permute-start.37) | collective-permute-done | bytes 524320 | tf_op jit(solution)/shard_map/ppermute | solution.py:30
  390.2 6.0 %output_projection.2.refs_7_ = f32[1024,512]{1,0:T(8,128)} custom-call(s32[8]{0:T(128)S(1)} %concatenate.57.refs_0_, bf16[2,2,1024,128]{3,2,1,0:T(8,128)(2,1)S(1)} %pad_maximum_fusion.7.refs_1_, bf16[2,2,1024,128]{3,2,1,0:T(8,128)(2,1)S(1)} %collective-permute-done.31.refs_2_, bf16[2,2,1024,128]{3,2,1,0:T(8,128)(2,1)S(1)} %pad_maximum_fusion.8.refs_3_, ...), custom_call_target="tpu_custom_call" | custom-call | flops 1 | bytes 1 | tf_op jit(solution)/shard_map/output_projection/pallas_call | solution.py:357
  396.6 2.1 collective-permute-done.38.refs_4_
  398.8 1.5 collective-permute-done.35.refs_2_
  400.3 6.2 %output_projection.3 = bf16[1024,512]{1,0:T(8,128)(2,1)} custom-call(s32[8]{0:T(128)S(1)} %concatenate.57.refs_0_, bf16[2,2,1024,128]{3,2,1,0:T(8,128)(2,1)S(1)} %pad_maximum_fusion.6.refs_1_, bf16[2,2,1024,128]{3,2,1,0:T(8,128)(2,1)S(1)} %collective-permute-done.35.refs_2_, bf16[2,2,1024,128]{3,2,1,0:T(8,128)(2,1)S(1)} %pad_maximum_fusion.9.refs_3_, ...), custom_call_target="tpu_custom_call" | custom-call | flops 1 | bytes 1 | tf_op jit(solution)/shard_map/output_projection/pallas_call | solution.py:357
  406.5 4.3 all-to-all-start.2
  410.7 4.3 %collect_blocks.1 = bf16[1,4,4,4,128,256]{5,4,3,2,1,0:T(8,128)(2,1)} custom-call(bf16[4,2,4,128,256]{4,3,2,1,0:T(8,128)(2,1)} %all-to-all-done.refs_0_, bf16[4,2,4,128,256]{4,3,2,1,0:T(8,128)(2,1)S(1)} %all-to-all-done.1.refs_1_), custom_call_target="tpu_custom_call" | custom-call | flops 1 | bytes 1 | tf_op jit(solution)/shard_map/collect_blocks/pallas_call | solution.py:396
  415.0 10.2 %all-to-all-done.2.refs_1_ = bf16[8,128,512]{2,1,0:T(8,128)(2,1)} async-done(((bf16[8,128,512]{2,1,0:T(8,128)(2,1)}), bf16[8,128,512]{2,1,0:T(8,128)(2,1)}, u32[]{:S(2)}, u32[]{:S(2)}) %all-to-all-start.2) | async-done | bytes 1048608 | tf_op jit(solution)/shard_map/all_to_all | solution.py:559
  425.3 2.5 residual.1
  (173 shorter events, 35.3 us)
Async XLA Ops:
  9.0 14.5 %copy-start.12 = (bf16[1,1,128,4096]{3,2,1,0:T(8,128)(2,1)S(1)}, bf16[1,1,128,4096]{3,2,1,0:T(8,128)(2,1)}, u32[]{:S(2)}) copy-start(bf16[1,1,128,4096]{3,2,1,0:T(8,128)(2,1)} %param.7) | copy-start | bytes 3145732
  9.0 14.5 %copy-start.29 = (f32[4096]{0:T(1024)S(1)}, f32[4096]{0:T(1024)}, u32[]{:S(2)}) copy-start(f32[4096]{0:T(1024)} %param.8) | copy-start | bytes 49156
  9.9 12.9 %collective-permute-start.3 = (bf16[2,256,384]{2,1,0:T(8,128)(2,1)}, bf16[2,256,384]{2,1,0:T(8,128)(2,1)}, u32[]{:S(2)}, u32[]{:S(2)}) collective-permute-start(bf16[2,256,384]{2,1,0:T(8,128)(2,1)} %bitcast.17), channel_id=1, source_target_pairs={{0,1},{1,0},{2,3},{3,2},{4,5},{5,4},{6,7},{7,6},{8,9},{9,8},{10,11... | collective-permute-start | bytes 1179656 | tf_op jit(solution)/shard_map/ppermute | solution.py:30
  10.4 60.1 %collective-permute-start.6 = (bf16[16,128,256]{2,1,0:T(8,128)(2,1)S(1)}, bf16[16,128,256]{2,1,0:T(8,128)(2,1)S(1)}, u32[]{:S(2)}, u32[]{:S(2)}) collective-permute-start(bf16[16,128,256]{2,1,0:T(8,128)(2,1)S(1)} %copy-done.15), channel_id=1, source_target_pairs={{0,4},{4,0},{8,12},{12,8},{1,5},{5,1},{9,13},{13,9},{2,6},{6,2},{1... | collective-permute-start | bytes 3145736 | tf_op jit(solution)/shard_map/ppermute | solution.py:30
  13.0 57.5 %collective-permute-start.7 = (bf16[16,128,256]{2,1,0:T(8,128)(2,1)S(1)}, bf16[16,128,256]{2,1,0:T(8,128)(2,1)}, u32[]{:S(2)}, u32[]{:S(2)}) collective-permute-start(bf16[16,128,256]{2,1,0:T(8,128)(2,1)S(1)} %copy-done.15), channel_id=1, source_target_pairs={{0,8},{4,12},{8,0},{12,4},{1,9},{5,13},{9,1},{13,5},{2,10},{6,14},... | collective-permute-start | bytes 3145736 | tf_op jit(solution)/shard_map/ppermute | solution.py:30
  17.4 17.7 %collective-permute-start.4 = (bf16[2,256,384]{2,1,0:T(8,128)(2,1)}, bf16[2,256,384]{2,1,0:T(8,128)(2,1)}, u32[]{:S(2)}, u32[]{:S(2)}) collective-permute-start(bf16[2,256,384]{2,1,0:T(8,128)(2,1)} %bitcast.61), channel_id=1, source_target_pairs={{0,2},{1,3},{2,0},{3,1},{4,6},{5,7},{6,4},{7,5},{8,10},{9,11},{10,... | collective-permute-start | bytes 1179656 | tf_op jit(solution)/shard_map/ppermute | solution.py:30
  20.9 15.9 %collective-permute-start.5 = (bf16[2,256,384]{2,1,0:T(8,128)(2,1)}, bf16[2,256,384]{2,1,0:T(8,128)(2,1)}, u32[]{:S(2)}, u32[]{:S(2)}) collective-permute-start(bf16[2,256,384]{2,1,0:T(8,128)(2,1)} %bitcast.60), channel_id=1, source_target_pairs={{0,3},{1,2},{2,1},{3,0},{4,7},{5,6},{6,5},{7,4},{8,11},{9,10},{10,... | collective-permute-start | bytes 1179656 | tf_op jit(solution)/shard_map/ppermute | solution.py:30
  22.8 15.6 %collective-permute-start = (bf16[2,256,384]{2,1,0:T(8,128)(2,1)}, bf16[2,256,384]{2,1,0:T(8,128)(2,1)}, u32[]{:S(2)}, u32[]{:S(2)}) collective-permute-start(bf16[2,256,384]{2,1,0:T(8,128)(2,1)} %bitcast.59), channel_id=1, source_target_pairs={{0,1},{1,0},{2,3},{3,2},{4,5},{5,4},{6,7},{7,6},{8,9},{9,8},{10,11... | collective-permute-start | bytes 1179656 | tf_op jit(solution)/shard_map/ppermute | solution.py:30
  26.6 5.3 %copy-start.30 = (s32[4]{0:T(128)S(1)}, s32[4]{0:T(128)}, u32[]{:S(2)}) copy-start(s32[4]{0:T(128)} %refs_1_.8) | copy-start | bytes 52
  30.6 7.8 %copy-start.33 = (bf16[2,128,1024]{2,1,0:T(8,128)(2,1)S(1)}, bf16[2,128,1024]{2,1,0:T(8,128)(2,1)}, u32[]{:S(2)}) copy-start(bf16[2,128,1024]{2,1,0:T(8,128)(2,1)} %copy-done.32) | copy-start | bytes 1572868
  35.2 12.0 %collective-permute-start.1 = (bf16[2,256,384]{2,1,0:T(8,128)(2,1)S(1)}, bf16[2,256,384]{2,1,0:T(8,128)(2,1)S(1)}, u32[]{:S(2)}, u32[]{:S(2)}) collective-permute-start(bf16[2,256,384]{2,1,0:T(8,128)(2,1)S(1)} %bitcast.63), channel_id=1, source_target_pairs={{0,2},{1,3},{2,0},{3,1},{4,6},{5,7},{6,4},{7,5},{8,10},{9,11},{10,... | collective-permute-start | bytes 1179656 | tf_op jit(solution)/shard_map/ppermute | solution.py:30
  36.7 17.0 %collective-permute-start.2 = (bf16[2,256,384]{2,1,0:T(8,128)(2,1)S(1)}, bf16[2,256,384]{2,1,0:T(8,128)(2,1)S(1)}, u32[]{:S(2)}, u32[]{:S(2)}) collective-permute-start(bf16[2,256,384]{2,1,0:T(8,128)(2,1)S(1)} %bitcast.62), channel_id=1, source_target_pairs={{0,3},{1,2},{2,1},{3,0},{4,7},{5,6},{6,5},{7,4},{8,11},{9,10},{10,... | collective-permute-start | bytes 1179656 | tf_op jit(solution)/shard_map/ppermute | solution.py:30
  38.4 32.1 %collective-permute-start.8 = (bf16[2,128,1024]{2,1,0:T(8,128)(2,1)S(1)}, bf16[2,128,1024]{2,1,0:T(8,128)(2,1)S(1)}, u32[]{:S(2)}, u32[]{:S(2)}) collective-permute-start(bf16[2,128,1024]{2,1,0:T(8,128)(2,1)S(1)} %copy-done.33), channel_id=1, source_target_pairs={{0,4},{4,0},{8,12},{12,8},{1,5},{5,1},{9,13},{13,9},{2,6},{6,2},{1... | collective-permute-start | bytes 1572872 | tf_op jit(solution)/shard_map/ppermute | solution.py:30
  39.1 215.2 %copy-start.2 = (f32[1024,128]{1,0:T(8,128)}, f32[1024,128]{1,0:T(8,128)S(1)}, u32[]{:S(2)}) copy-start(f32[1024,128]{1,0:T(8,128)S(1)} %get-tuple-element.128.refs_10_) | copy-start | bytes 1572868
  39.1 215.2 %copy-start.4 = (f32[1024,128]{1,0:T(8,128)}, f32[1024,128]{1,0:T(8,128)S(1)}, u32[]{:S(2)}) copy-start(f32[1024,128]{1,0:T(8,128)S(1)} %get-tuple-element.129.refs_11_) | copy-start | bytes 1572868
  40.9 142.5 %copy-start.34 = (bf16[2,4,256,384]{3,2,1,0:T(8,128)(2,1)}, bf16[2,4,256,384]{3,2,1,0:T(8,128)(2,1)S(1)}, u32[]{:S(2)}) copy-start(bf16[2,4,256,384]{3,2,1,0:T(8,128)(2,1)S(1)} %pad_maximum_fusion.1.refs_5_.refs_7_) | copy-start | bytes 4718596
  53.8 20.0 %copy-start.24 = (bf16[2,128,1024]{2,1,0:T(8,128)(2,1)S(1)}, bf16[2,128,1024]{2,1,0:T(8,128)(2,1)}, u32[]{:S(2)}) copy-start(bf16[2,128,1024]{2,1,0:T(8,128)(2,1)} %copy-done.23) | copy-start | bytes 1572868
  70.5 9.4 %copy-start.17 = (bf16[16,128,256]{2,1,0:T(8,128)(2,1)}, bf16[16,128,256]{2,1,0:T(8,128)(2,1)S(1)}, u32[]{:S(2)}) copy-start(bf16[16,128,256]{2,1,0:T(8,128)(2,1)S(1)} %collective-permute-done.6.refs_3_) | copy-start | bytes 3145732
  70.5 9.2 %collective-permute-start.18 = (bf16[1,1,1,128,1024]{4,3,2,1,0:T(8,128)(2,1)S(1)}, bf16[1,1,1,128,1024]{4,3,2,1,0:T(8,128)(2,1)S(1)}, u32[]{:S(2)}, u32[]{:S(2)}) collective-permute-start(bf16[1,1,1,128,1024]{4,3,2,1,0:T(8,128)(2,1)S(1)} %get-tuple-element.152), channel_id=1, source_target_pairs={{0,16},{16,0},{1,17},{17,1},{2,18},{18,2},{3,19},{19,3},{4,20},{20... | collective-permute-start | bytes 786440 | tf_op jit(solution)/shard_map/ppermute | solution.py:30
  72.3 11.5 %collective-permute-start.16 = (bf16[1,1,1,128,1024]{4,3,2,1,0:T(8,128)(2,1)S(1)}, bf16[1,1,1,128,1024]{4,3,2,1,0:T(8,128)(2,1)S(1)}, u32[]{:S(2)}, u32[]{:S(2)}) collective-permute-start(bf16[1,1,1,128,1024]{4,3,2,1,0:T(8,128)(2,1)S(1)} %get-tuple-element.153), channel_id=1, source_target_pairs={{0,2},{1,3},{2,0},{3,1},{4,6},{5,7},{6,4},{7,5},{8,10},{9,11},{10,... | collective-permute-start | bytes 786440 | tf_op jit(solution)/shard_map/ppermute | solution.py:30
  73.8 11.6 %collective-permute-start.12 = (bf16[1,1,1,128,1024]{4,3,2,1,0:T(8,128)(2,1)S(1)}, bf16[1,1,1,128,1024]{4,3,2,1,0:T(8,128)(2,1)S(1)}, u32[]{:S(2)}, u32[]{:S(2)}) collective-permute-start(bf16[1,1,1,128,1024]{4,3,2,1,0:T(8,128)(2,1)S(1)} %get-tuple-element.154), channel_id=1, source_target_pairs={{0,16},{16,0},{1,17},{17,1},{2,18},{18,2},{3,19},{19,3},{4,20},{20... | collective-permute-start | bytes 786440 | tf_op jit(solution)/shard_map/ppermute | solution.py:30
  79.9 22.4 %collective-permute-start.19 = (bf16[1,1,2,128,1024]{4,3,2,1,0:T(8,128)(2,1)S(1)}, bf16[1,1,2,128,1024]{4,3,2,1,0:T(8,128)(2,1)S(1)}, u32[]{:S(2)}, u32[]{:S(2)}) collective-permute-start(bf16[1,1,2,128,1024]{4,3,2,1,0:T(8,128)(2,1)S(1)} %pad_maximum_fusion.13), channel_id=1, source_target_pairs={{0,2},{1,3},{2,0},{3,1},{4,6},{5,7},{6,4},{7,5},{8,10},{9,11},{10,... | collective-permute-start | bytes 1572872 | tf_op jit(solution)/shard_map/ppermute | solution.py:30
  81.6 18.8 %collective-permute-start.10 = (bf16[1,1,1,128,1024]{4,3,2,1,0:T(8,128)(2,1)S(1)}, bf16[1,1,1,128,1024]{4,3,2,1,0:T(8,128)(2,1)S(1)}, u32[]{:S(2)}, u32[]{:S(2)}) collective-permute-start(bf16[1,1,1,128,1024]{4,3,2,1,0:T(8,128)(2,1)S(1)} %get-tuple-element.155), channel_id=1, source_target_pairs={{0,2},{1,3},{2,0},{3,1},{4,6},{5,7},{6,4},{7,5},{8,10},{9,11},{10,... | collective-permute-start | bytes 786440 | tf_op jit(solution)/shard_map/ppermute | solution.py:30
  81.9 30.7 %collective-permute-start.9 = (bf16[16,128,256]{2,1,0:T(8,128)(2,1)}, bf16[16,128,256]{2,1,0:T(8,128)(2,1)S(1)}, u32[]{:S(2)}, u32[]{:S(2)}) collective-permute-start(bf16[16,128,256]{2,1,0:T(8,128)(2,1)} %collective-permute-done.7.refs_2_), channel_id=1, source_target_pairs={{0,4},{4,0},{8,12},{12,8},{1,5},{5,1},{9,13},{13,9},{2,6},{6,2},{1... | collective-permute-start | bytes 3145736 | tf_op jit(solution)/shard_map/ppermute | solution.py:30
  83.8 21.2 %collective-permute-start.17 = (bf16[1,2,1,128,1024]{4,3,2,1,0:T(8,128)(2,1)S(1)}, bf16[1,2,1,128,1024]{4,3,2,1,0:T(8,128)(2,1)S(1)}, u32[]{:S(2)}, u32[]{:S(2)}) collective-permute-start(bf16[1,2,1,128,1024]{4,3,2,1,0:T(8,128)(2,1)S(1)} %pad_maximum_fusion.12), channel_id=1, source_target_pairs={{0,16},{16,0},{1,17},{17,1},{2,18},{18,2},{3,19},{19,3},{4,20},{20... | collective-permute-start | bytes 1572872 | tf_op jit(solution)/shard_map/ppermute | solution.py:30
  85.5 23.2 %collective-permute-start.13 = (bf16[1,1,2,128,1024]{4,3,2,1,0:T(8,128)(2,1)S(1)}, bf16[1,1,2,128,1024]{4,3,2,1,0:T(8,128)(2,1)S(1)}, u32[]{:S(2)}, u32[]{:S(2)}) collective-permute-start(bf16[1,1,2,128,1024]{4,3,2,1,0:T(8,128)(2,1)S(1)} %pad_maximum_fusion.11), channel_id=1, source_target_pairs={{0,2},{1,3},{2,0},{3,1},{4,6},{5,7},{6,4},{7,5},{8,10},{9,11},{10,... | collective-permute-start | bytes 1572872 | tf_op jit(solution)/shard_map/ppermute | solution.py:30
  100.5 9.2 %collective-permute-start.11 = (bf16[1,2,1,128,1024]{4,3,2,1,0:T(8,128)(2,1)S(1)}, bf16[1,2,1,128,1024]{4,3,2,1,0:T(8,128)(2,1)S(1)}, u32[]{:S(2)}, u32[]{:S(2)}) collective-permute-start(bf16[1,2,1,128,1024]{4,3,2,1,0:T(8,128)(2,1)S(1)} %pad_maximum_fusion.10), channel_id=1, source_target_pairs={{0,16},{16,0},{1,17},{17,1},{2,18},{18,2},{3,19},{19,3},{4,20},{20... | collective-permute-start | bytes 1572872 | tf_op jit(solution)/shard_map/ppermute | solution.py:30
  102.2 63.8 %collective-permute-start.22 = (bf16[2,4,256,384]{3,2,0,1:T(8,128)(2,1)S(1)}, bf16[2,4,256,384]{3,2,0,1:T(8,128)(2,1)S(1)}, u32[]{:S(2)}, u32[]{:S(2)}) collective-permute-start(bf16[2,4,256,384]{3,2,0,1:T(8,128)(2,1)S(1)} %pad_maximum_fusion), channel_id=1, source_target_pairs={{0,8},{4,12},{8,0},{12,4},{1,9},{5,13},{9,1},{13,5},{2,10},{6,14},... | collective-permute-start | bytes 4718600 | tf_op jit(solution)/shard_map/ppermute | solution.py:30
  105.0 61.1 %collective-permute-start.21 = (bf16[1,2,2,128,1024]{4,3,2,1,0:T(8,128)(2,1)S(1)}, bf16[1,2,2,128,1024]{4,3,2,1,0:T(8,128)(2,1)S(1)}, u32[]{:S(2)}, u32[]{:S(2)}) collective-permute-start(bf16[1,2,2,128,1024]{4,3,2,1,0:T(8,128)(2,1)S(1)} %pad_maximum_fusion.5.refs_2_), channel_id=1, source_target_pairs={{0,1},{1,0},{2,3},{3,2},{4,5},{5,4},{6,7},{7,6},{8,9},{9,8},{10,11... | collective-permute-start | bytes 3145736 | tf_op jit(solution)/shard_map/ppermute | solution.py:30
  105.2 71.3 %copy-start = (bf16[1,2,2,128,1024]{4,3,2,1,0:T(8,128)(2,1)}, bf16[1,2,2,128,1024]{4,3,2,1,0:T(8,128)(2,1)S(1)}, u32[]{:S(2)}) copy-start(bf16[1,2,2,128,1024]{4,3,2,1,0:T(8,128)(2,1)S(1)} %pad_maximum_fusion.4.refs_1_) | copy-start | bytes 3145732
  108.6 57.5 %collective-permute-start.20 = (bf16[1,2,2,128,1024]{4,3,2,1,0:T(8,128)(2,1)S(1)}, bf16[1,2,2,128,1024]{4,3,2,1,0:T(8,128)(2,1)S(1)}, u32[]{:S(2)}, u32[]{:S(2)}) collective-permute-start(bf16[1,2,2,128,1024]{4,3,2,1,0:T(8,128)(2,1)S(1)} %pad_maximum_fusion.4.refs_1_), channel_id=1, source_target_pairs={{0,1},{1,0},{2,3},{3,2},{4,5},{5,4},{6,7},{7,6},{8,9},{9,8},{10,11... | collective-permute-start | bytes 3145736 | tf_op jit(solution)/shard_map/ppermute | solution.py:30
  108.7 59.5 %copy-start.16 = (bf16[16,128,256]{2,1,0:T(8,128)(2,1)S(1)}, bf16[16,128,256]{2,1,0:T(8,128)(2,1)}, u32[]{:S(2)}) copy-start(bf16[16,128,256]{2,1,0:T(8,128)(2,1)} %refs_1_.4) | copy-start | bytes 3145732
  108.8 59.5 %copy-start.18 = (bf16[16,128,256]{2,1,0:T(8,128)(2,1)S(1)}, bf16[16,128,256]{2,1,0:T(8,128)(2,1)}, u32[]{:S(2)}) copy-start(bf16[16,128,256]{2,1,0:T(8,128)(2,1)} %copy-done.17) | copy-start | bytes 3145732
  109.7 56.4 %collective-permute-start.15 = (bf16[1,2,2,128,1024]{4,3,2,1,0:T(8,128)(2,1)S(1)}, bf16[1,2,2,128,1024]{4,3,2,1,0:T(8,128)(2,1)S(1)}, u32[]{:S(2)}, u32[]{:S(2)}) collective-permute-start(bf16[1,2,2,128,1024]{4,3,2,1,0:T(8,128)(2,1)S(1)} %pad_maximum_fusion.3.refs_4_), channel_id=1, source_target_pairs={{0,1},{1,0},{2,3},{3,2},{4,5},{5,4},{6,7},{7,6},{8,9},{9,8},{10,11... | collective-permute-start | bytes 3145736 | tf_op jit(solution)/shard_map/ppermute | solution.py:30
  112.6 55.7 %collective-permute-start.14 = (bf16[1,2,2,128,1024]{4,3,2,1,0:T(8,128)(2,1)S(1)}, bf16[1,2,2,128,1024]{4,3,2,1,0:T(8,128)(2,1)S(1)}, u32[]{:S(2)}, u32[]{:S(2)}) collective-permute-start(bf16[1,2,2,128,1024]{4,3,2,1,0:T(8,128)(2,1)S(1)} %pad_maximum_fusion.2.refs_3_), channel_id=1, source_target_pairs={{0,1},{1,0},{2,3},{3,2},{4,5},{5,4},{6,7},{7,6},{8,9},{9,8},{10,11... | collective-permute-start | bytes 3145736 | tf_op jit(solution)/shard_map/ppermute | solution.py:30
  166.1 10.4 %copy-start.8 = (bf16[1,2,2,128,1024]{4,3,2,1,0:T(8,128)(2,1)}, bf16[1,2,2,128,1024]{4,3,2,1,0:T(8,128)(2,1)S(1)}, u32[]{:S(2)}) copy-start(bf16[1,2,2,128,1024]{4,3,2,1,0:T(8,128)(2,1)S(1)} %collective-permute-done.21.refs_4_) | copy-start | bytes 3145732
  166.1 10.4 %copy-start.10 = (bf16[1,2,2,128,1024]{4,3,2,1,0:T(8,128)(2,1)}, bf16[1,2,2,128,1024]{4,3,2,1,0:T(8,128)(2,1)S(1)}, u32[]{:S(2)}) copy-start(bf16[1,2,2,128,1024]{4,3,2,1,0:T(8,128)(2,1)S(1)} %collective-permute-done.20.refs_3_) | copy-start | bytes 3145732
  168.3 85.9 %copy-start.6 = (bf16[1,2,2,128,1024]{4,3,2,1,0:T(8,128)(2,1)}, bf16[1,2,2,128,1024]{4,3,2,1,0:T(8,128)(2,1)S(1)}, u32[]{:S(2)}) copy-start(bf16[1,2,2,128,1024]{4,3,2,1,0:T(8,128)(2,1)S(1)} %collective-permute-done.14.refs_5_) | copy-start | bytes 3145732
  172.6 77.7 %collective-permute-start.24 = (bf16[4,16,128,128]{3,2,1,0:T(8,128)(2,1)}, bf16[4,16,128,128]{3,2,1,0:T(8,128)(2,1)S(1)}, u32[]{:S(2)}, u32[]{:S(2)}) collective-permute-start(bf16[4,16,128,128]{3,2,1,0:T(8,128)(2,1)} %get-tuple-element.94), channel_id=1, source_target_pairs={{0,16},{16,0},{1,17},{17,1},{2,18},{18,2},{3,19},{19,3},{4,20},{20... | collective-permute-start | bytes 6291464 | tf_op jit(solution)/shard_map/ppermute | solution.py:30
  183.3 64.0 %collective-permute-start.23 = (bf16[2,1024,384]{2,1,0:T(8,128)(2,1)S(1)}, bf16[2,1024,384]{2,1,0:T(8,128)(2,1)S(1)}, u32[]{:S(2)}, u32[]{:S(2)}) collective-permute-start(bf16[2,1024,384]{2,1,0:T(8,128)(2,1)S(1)} %partner_product.2), channel_id=1, source_target_pairs={{0,4},{4,0},{8,12},{12,8},{1,5},{5,1},{9,13},{13,9},{2,6},{6,2},{1... | collective-permute-start | bytes 4718600 | tf_op jit(solution)/shard_map/ppermute | solution.py:30
  183.5 66.8 %collective-permute-start.25 = (bf16[2,4,256,384]{3,2,1,0:T(8,128)(2,1)S(1)}, bf16[2,4,256,384]{3,2,1,0:T(8,128)(2,1)S(1)}, u32[]{:S(2)}, u32[]{:S(2)}) collective-permute-start(bf16[2,4,256,384]{3,2,1,0:T(8,128)(2,1)S(1)} %pad_maximum_fusion.1.refs_5_.refs_7_), channel_id=1, source_target_pairs={{0,8},{4,12},{8,0},{12,4},{1,9},{5,13},{9,1},{13,5},{2,10},{6,14},... | collective-permute-start | bytes 4718600 | tf_op jit(solution)/shard_map/ppermute | solution.py:30
  247.4 6.9 %copy-start.41 = (bf16[2,1024,384]{2,1,0:T(8,128)(2,1)}, bf16[2,1024,384]{2,1,0:T(8,128)(2,1)S(1)}, u32[]{:S(2)}) copy-start(bf16[2,1024,384]{2,1,0:T(8,128)(2,1)S(1)} %collective-permute-done.23.refs_9_) | copy-start | bytes 4718596
  250.3 14.2 %copy-start.36 = (bf16[2,4,256,384]{3,2,1,0:T(8,128)(2,1)}, bf16[2,4,256,384]{3,2,1,0:T(8,128)(2,1)S(1)}, u32[]{:S(2)}) copy-start(bf16[2,4,256,384]{3,2,1,0:T(8,128)(2,1)S(1)} %collective-permute-done.25.refs_6_.refs_8_) | copy-start | bytes 4718596
  266.3 69.7 %all-to-all-start = ((bf16[4,2,4,128,256]{4,3,2,1,0:T(8,128)(2,1)}), bf16[4,2,4,128,256]{4,3,2,1,0:T(8,128)(2,1)}, u32[]{:S(2)}, u32[]{:S(2)}) async-start(bf16[4,2,4,128,256]{4,3,2,1,0:T(8,128)(2,1)} %get-tuple-element.118), calls=%async_computation | async-start | bytes 4194304 | tf_op jit(solution)/shard_map/all_to_all | solution.py:535
  274.5 8.7 %copy-start.22 = (bf16[2,1024,256]{2,1,0:T(8,128)(2,1)S(1)}, bf16[2,1024,256]{2,1,0:T(8,128)(2,1)}, u32[]{:S(2)}) copy-start(bf16[2,1024,256]{2,1,0:T(8,128)(2,1)} %copy-done.21) | copy-start | bytes 3145732
  274.5 8.7 %copy-start.28 = (bf16[2,1024,128]{2,1,0:T(8,128)(2,1)S(1)}, bf16[2,1024,128]{2,1,0:T(8,128)(2,1)}, u32[]{:S(2)}) copy-start(bf16[2,1024,128]{2,1,0:T(8,128)(2,1)} %copy-done.27) | copy-start | bytes 1572868
  281.1 55.0 %collective-permute-start.26 = (bf16[2,1024,384]{2,1,0:T(8,128)(2,1)S(1)}, bf16[2,1024,384]{2,1,0:T(8,128)(2,1)}, u32[]{:S(2)}, u32[]{:S(2)}) collective-permute-start(bf16[2,1024,384]{2,1,0:T(8,128)(2,1)S(1)} %partner_product.3), channel_id=1, source_target_pairs={{0,4},{4,0},{8,12},{12,8},{1,5},{5,1},{9,13},{13,9},{2,6},{6,2},{1... | collective-permute-start | bytes 4718600 | tf_op jit(solution)/shard_map/ppermute | solution.py:30
  283.1 57.4 %copy-start.3 = (f32[1024,128]{1,0:T(8,128)S(1)}, f32[1024,128]{1,0:T(8,128)}, u32[]{:S(2)}) copy-start(f32[1024,128]{1,0:T(8,128)} %copy-done.2) | copy-start | bytes 1572868
  283.1 57.4 %copy-start.5 = (f32[1024,128]{1,0:T(8,128)S(1)}, f32[1024,128]{1,0:T(8,128)}, u32[]{:S(2)}) copy-start(f32[1024,128]{1,0:T(8,128)} %copy-done.4) | copy-start | bytes 1572868
  337.9 18.5 %collective-permute-start.32 = (bf16[1,1,1024,128]{3,2,1,0:T(8,128)(2,1)}, bf16[1,1,1024,128]{3,2,1,0:T(8,128)(2,1)}, u32[]{:S(2)}, u32[]{:S(2)}) collective-permute-start(bf16[1,1,1024,128]{3,2,1,0:T(8,128)(2,1)} %get-tuple-element.150), channel_id=1, source_target_pairs={{0,16},{16,0},{1,17},{17,1},{2,18},{18,2},{3,19},{19,3},{4,20},{20... | collective-permute-start | bytes 786440 | tf_op jit(solution)/shard_map/ppermute | solution.py:30
  339.0 19.3 %collective-permute-start.29 = (bf16[1,1,1024,128]{3,2,1,0:T(8,128)(2,1)S(1)}, bf16[1,1,1024,128]{3,2,1,0:T(8,128)(2,1)}, u32[]{:S(2)}, u32[]{:S(2)}) collective-permute-start(bf16[1,1,1024,128]{3,2,1,0:T(8,128)(2,1)S(1)} %get-tuple-element.151), channel_id=1, source_target_pairs={{0,2},{1,3},{2,0},{3,1},{4,6},{5,7},{6,4},{7,5},{8,10},{9,11},{10,... | collective-permute-start | bytes 786440 | tf_op jit(solution)/shard_map/ppermute | solution.py:30
  352.6 53.8 %all-to-all-start.1 = ((bf16[4,2,4,128,256]{4,3,2,1,0:T(8,128)(2,1)}), bf16[4,2,4,128,256]{4,3,2,1,0:T(8,128)(2,1)S(1)}, u32[]{:S(2)}, u32[]{:S(2)}) async-start(bf16[4,2,4,128,256]{4,3,2,1,0:T(8,128)(2,1)} %get-tuple-element.137), calls=%async_computation.1 | async-start | bytes 4194304 | tf_op jit(solution)/shard_map/all_to_all | solution.py:535
  357.7 13.0 %collective-permute-start.33 = (bf16[1,2,1024,128]{3,2,1,0:T(8,128)(2,1)S(1)}, bf16[1,2,1024,128]{3,2,1,0:T(8,128)(2,1)S(1)}, u32[]{:S(2)}, u32[]{:S(2)}) collective-permute-start(bf16[1,2,1024,128]{3,2,1,0:T(8,128)(2,1)S(1)} %pad_maximum_fusion.16), channel_id=1, source_target_pairs={{0,2},{1,3},{2,0},{3,1},{4,6},{5,7},{6,4},{7,5},{8,10},{9,11},{10,... | collective-permute-start | bytes 1572872 | tf_op jit(solution)/shard_map/ppermute | solution.py:30
  359.3 13.8 %collective-permute-start.30 = (bf16[2,1,1024,128]{3,2,1,0:T(8,128)(2,1)S(1)}, bf16[2,1,1024,128]{3,2,1,0:T(8,128)(2,1)S(1)}, u32[]{:S(2)}, u32[]{:S(2)}) collective-permute-start(bf16[2,1,1024,128]{3,2,1,0:T(8,128)(2,1)S(1)} %pad_maximum_fusion.15), channel_id=1, source_target_pairs={{0,16},{16,0},{1,17},{17,1},{2,18},{18,2},{3,19},{19,3},{4,20},{20... | collective-permute-start | bytes 1572872 | tf_op jit(solution)/shard_map/ppermute | solution.py:30
  368.0 8.0 %collective-permute-start.36 = (bf16[1,1,1024,128]{3,2,1,0:T(8,128)(2,1)S(1)}, bf16[1,1,1024,128]{3,2,1,0:T(8,128)(2,1)S(1)}, u32[]{:S(2)}, u32[]{:S(2)}) collective-permute-start(bf16[1,1,1024,128]{3,2,1,0:T(8,128)(2,1)S(1)} %get-tuple-element.148), channel_id=1, source_target_pairs={{0,16},{16,0},{1,17},{17,1},{2,18},{18,2},{3,19},{19,3},{4,20},{20... | collective-permute-start | bytes 786440 | tf_op jit(solution)/shard_map/ppermute | solution.py:30
  369.2 8.5 %collective-permute-start.27 = (bf16[1,1,1024,128]{3,2,1,0:T(8,128)(2,1)S(1)}, bf16[1,1,1024,128]{3,2,1,0:T(8,128)(2,1)S(1)}, u32[]{:S(2)}, u32[]{:S(2)}) collective-permute-start(bf16[1,1,1024,128]{3,2,1,0:T(8,128)(2,1)S(1)} %get-tuple-element.149), channel_id=1, source_target_pairs={{0,2},{1,3},{2,0},{3,1},{4,6},{5,7},{6,4},{7,5},{8,10},{9,11},{10,... | collective-permute-start | bytes 786440 | tf_op jit(solution)/shard_map/ppermute | solution.py:30
  371.8 18.3 %collective-permute-start.34 = (bf16[2,2,1024,128]{3,2,1,0:T(8,128)(2,1)S(1)}, bf16[2,2,1024,128]{3,2,1,0:T(8,128)(2,1)S(1)}, u32[]{:S(2)}, u32[]{:S(2)}) collective-permute-start(bf16[2,2,1024,128]{3,2,1,0:T(8,128)(2,1)S(1)} %pad_maximum_fusion.8.refs_3_), channel_id=1, source_target_pairs={{0,1},{1,0},{2,3},{3,2},{4,5},{5,4},{6,7},{7,6},{8,9},{9,8},{10,11... | collective-permute-start | bytes 3145736 | tf_op jit(solution)/shard_map/ppermute | solution.py:30
  374.1 16.0 %collective-permute-start.31 = (bf16[2,2,1024,128]{3,2,1,0:T(8,128)(2,1)S(1)}, bf16[2,2,1024,128]{3,2,1,0:T(8,128)(2,1)S(1)}, u32[]{:S(2)}, u32[]{:S(2)}) collective-permute-start(bf16[2,2,1024,128]{3,2,1,0:T(8,128)(2,1)S(1)} %pad_maximum_fusion.7.refs_1_), channel_id=1, source_target_pairs={{0,1},{1,0},{2,3},{3,2},{4,5},{5,4},{6,7},{7,6},{8,9},{9,8},{10,11... | collective-permute-start | bytes 3145736 | tf_op jit(solution)/shard_map/ppermute | solution.py:30
  376.1 12.6 %collective-permute-start.37 = (bf16[1,2,1024,128]{3,2,1,0:T(8,128)(2,1)S(1)}, bf16[1,2,1024,128]{3,2,1,0:T(8,128)(2,1)S(1)}, u32[]{:S(2)}, u32[]{:S(2)}) collective-permute-start(bf16[1,2,1024,128]{3,2,1,0:T(8,128)(2,1)S(1)} %pad_maximum_fusion.17), channel_id=1, source_target_pairs={{0,2},{1,3},{2,0},{3,1},{4,6},{5,7},{6,4},{7,5},{8,10},{9,11},{10,... | collective-permute-start | bytes 1572872 | tf_op jit(solution)/shard_map/ppermute | solution.py:30
  377.7 12.3 %collective-permute-start.28 = (bf16[2,1,1024,128]{3,2,1,0:T(8,128)(2,1)S(1)}, bf16[2,1,1024,128]{3,2,1,0:T(8,128)(2,1)S(1)}, u32[]{:S(2)}, u32[]{:S(2)}) collective-permute-start(bf16[2,1,1024,128]{3,2,1,0:T(8,128)(2,1)S(1)} %pad_maximum_fusion.14), channel_id=1, source_target_pairs={{0,16},{16,0},{1,17},{17,1},{2,18},{18,2},{3,19},{19,3},{4,20},{20... | collective-permute-start | bytes 1572872 | tf_op jit(solution)/shard_map/ppermute | solution.py:30
  396.1 2.7 collective-permute-start.38
  396.1 4.2 collective-permute-start.35
  406.5 18.8 %all-to-all-start.2 = ((bf16[8,128,512]{2,1,0:T(8,128)(2,1)}), bf16[8,128,512]{2,1,0:T(8,128)(2,1)}, u32[]{:S(2)}, u32[]{:S(2)}) async-start(bf16[8,128,512]{2,1,0:T(8,128)(2,1)} %bitcast.35), calls=%async_computation.2 | async-start | bytes 2097152 | tf_op jit(solution)/shard_map/all_to_all | solution.py:559
  410.7 14.6 %copy-start.13 = (bf16[1,1,128,4096]{3,2,1,0:T(8,128)(2,1)S(1)}, bf16[1,1,128,4096]{3,2,1,0:T(8,128)(2,1)}, u32[]{:S(2)}) copy-start(bf16[1,1,128,4096]{3,2,1,0:T(8,128)(2,1)} %param.7) | copy-start | bytes 3145732
  (25 other events, 58.1 us)

commit v2 on v1

v2 whole, which is shorter than its diff:
```python
import math

import jax
import jax.numpy as jnp
from jax import lax
from jax.experimental import pallas as pl
from jax.experimental.pallas import tpu as pltpu
from jax.sharding import PartitionSpec as P

ROT = 32
BLOCK = 128
EPSILON = 1e-05
VMEM_LIMIT = 48 * 1024 * 1024

SMEM = pltpu.SMEM
BF16 = jnp.bfloat16
F32 = jnp.float32


def params():
    return pltpu.CompilerParams(vmem_limit_bytes=VMEM_LIMIT)


def cost():
    return pl.CostEstimate(flops=1, bytes_accessed=1, transcendentals=0)


def hold(xs, microseconds):
    hbm = pl.BlockSpec(memory_space=pl.ANY)
    held = pl.pallas_call(
        lambda *refs: None,
        out_shape=[jax.ShapeDtypeStruct(x.shape, x.dtype) for x in xs],
        in_specs=[hbm] * len(xs),
        out_specs=[hbm] * len(xs),
        input_output_aliases={i: i for i in range(len(xs))},
        cost_estimate=pl.CostEstimate(flops=int(microseconds * 1e9), bytes_accessed=1, transcendentals=0),
        name="hold",
    )(*xs)
    return list(held)


def swap(x, axis, stride):
    size = lax.axis_size(axis)
    return lax.ppermute(x, axis, [(i, i ^ stride) for i in range(size)])


def halving(size, last):
    strides = []
    step = size // 2
    while step >= last:
        strides.append(step)
        step //= 2
    return strides


def offsets(strides):
    order = [0]
    for stride in strides:
        order = order + [o ^ stride for o in order]
    return order


def after(value, token):
    return lax.optimization_barrier((value, token))[0]


def dot(a, b):
    return jnp.dot(a, b, preferred_element_type=F32)


def dot_t(a, b):
    return lax.dot_general(a, b, (((1,), (1,)), ((), ())), preferred_element_type=F32)


def norm_body(depth, own_rel, meta, hidden, gain, own, sent, scratch):
    rows = hidden[...].astype(F32)
    centered = rows - jnp.mean(rows, axis=-1, keepdims=True)
    spread = jnp.mean(centered * centered, axis=-1, keepdims=True)
    scratch[...] = (centered * lax.rsqrt(spread + EPSILON) * gain[...]).astype(BF16)
    me = meta[0]
    for e, rel in enumerate(own_rel):
        start = pl.multiple_of((me ^ rel) * depth, 128)
        own[e] = scratch[:, pl.ds(start, depth)]
        start = pl.multiple_of((me ^ rel ^ 1) * depth, 128)
        sent[e] = scratch[:, pl.ds(start, depth)]


def norm_call(meta, hidden, gain, depth, own_rel):
    rows, width = hidden.shape
    shape = jax.ShapeDtypeStruct((len(own_rel), rows, depth), BF16)
    return pl.pallas_call(
        lambda *refs: norm_body(depth, own_rel, *refs),
        out_shape=(shape, shape),
        in_specs=[
            pl.BlockSpec(memory_space=SMEM),
            pl.BlockSpec(memory_space=pltpu.VMEM),
            pl.BlockSpec(memory_space=pltpu.VMEM),
        ],
        out_specs=(pl.BlockSpec(memory_space=pltpu.VMEM), pl.BlockSpec(memory_space=pltpu.VMEM)),
        scratch_shapes=[pltpu.VMEM((rows, width), BF16)],
        compiler_params=params(),
        cost_estimate=cost(),
        name="layer_norm",
    )(meta, hidden, gain)


def load_weights(refs):
    return [ref[:, 0].reshape(-1, ref.shape[-1]) for ref in refs]


def product(xs, ws, total):
    half = total.shape[0] // 2
    streams = len(xs) // 2
    for core in (0, 1):
        result = None
        k = 0
        for x in xs[core * streams : (core + 1) * streams]:
            for e in range(x.shape[0]):
                term = dot(x[e].reshape(-1, x.shape[-1]), ws[k])
                result = term if result is None else result + term
                k += 1
        total[core * half : (core + 1) * half] = result.astype(total.dtype)


def whole(x):
    nd = len(x.shape)
    return pl.BlockSpec(x.shape, lambda *_: (0,) * nd)


def by_step(x, first=0):
    nd = len(x.shape) - 1
    return pl.BlockSpec((1,) + tuple(x.shape[1:]), lambda i, *_: (first + i,) + (0,) * nd)


def weight_specs(ws, first):
    return [pl.BlockSpec((w.shape[0], 1) + w.shape[2:], lambda i, *_: (0, first + i, 0, 0)) for w in ws]


def partner_body(inputs, *refs):
    product(refs[:inputs], load_weights(refs[inputs:-1]), refs[-1].at[0])


def partner_call(xs, ws, rows, at, heads=1):
    out = jax.ShapeDtypeStruct((heads, rows, ws[0].shape[-1]), BF16)
    return pl.pallas_call(
        lambda *refs: partner_body(len(xs), *refs),
        grid=(heads,),
        out_shape=out,
        in_specs=[whole(x) for x in xs] + weight_specs(ws, at),
        out_specs=by_step(out),
        compiler_params=params(),
        cost_estimate=cost(),
        name="partner_product",
    )(*xs, *ws)


def finish_body(inputs, cap, order_h, order_t, meta, lengths, owners, *refs):
    xs, ws = refs[:inputs], load_weights(refs[inputs:-10])
    arrived, cosine, sine, cache, query, kv, placed, total, slots, counts = refs[-10:]
    me, tp, hg = meta[0], meta[1], meta[2]
    product(xs, ws, total)
    hd = query.shape[2]
    members = [(h, t) for h in order_h for t in order_t]
    run_rows = total.shape[0] // len(members)
    lane = lax.broadcasted_iota(jnp.int32, (run_rows, hd), 1)
    half_rot = ROT // 2
    for m, (rel_h, rel_t) in enumerate(members):
        rows = slice(m * run_rows, (m + 1) * run_rows)
        start = pl.multiple_of(((hg ^ rel_h) * len(order_t) + (tp ^ rel_t)) * run_rows, run_rows)
        to = pl.ds(start, run_rows)
        cos_rows, sin_rows = cosine[to], sine[to]

        def summed(low):
            return total[rows, low : low + hd] + arrived[0, rows, low : low + hd].astype(F32)

        def rotated(part):
            other = jnp.where(
                lane < half_rot, pltpu.roll(part, hd - half_rot, 1), pltpu.roll(part, half_rot, 1)
            )
            return (part * cos_rows + other * sin_rows).astype(BF16)

        query[0, to] = rotated(summed(0))
        kv[0, to, :hd] = rotated(summed(hd))
        kv[0, to, hd:] = summed(2 * hd).astype(BF16)
    owner_count = placed.shape[0]
    blocks = owners.shape[1]
    cached_blocks = lengths[me] // BLOCK
    valid_end = cached_blocks + query.shape[1] // BLOCK
    for s in range(owner_count * cap):
        slots[s] = -1
    for o in range(owner_count):
        counts[o] = 0
    for b in range(blocks):

        @pl.when(b < valid_end)
        def _():
            owner = owners[me, b]
            rank = counts[owner]

            @pl.when(rank < cap)
            def _():
                slots[owner * cap + rank] = b

            counts[owner] = rank + 1

    for s in range(owner_count * cap):
        block = slots[s]
        o, c = divmod(s, cap)

        @pl.when(block < 0)
        def _():
            placed[o, 0, c] = jnp.zeros(placed.shape[3:], BF16)

        @pl.when((block >= 0) & (block < cached_blocks))
        def _():
            at = pl.multiple_of(block * BLOCK, BLOCK)
            placed[o, 0, c] = cache[0, 0, pl.ds(at, BLOCK)]

        @pl.when(block >= cached_blocks)
        def _():
            at = pl.multiple_of((block - cached_blocks) * BLOCK, BLOCK)
            placed[o, 0, c] = kv[0, pl.ds(at, BLOCK)]


def cache_by_step(cache, first):
    return pl.BlockSpec((1, 1) + cache.shape[2:], lambda i, meta, *_: (0, meta[3] + first + i, 0, 0))


def finish_call(meta, lengths, owners, xs, ws, arrived, cosine, sine, cache, at, first, cap, owner_count, orders):
    heads, rows, width = arrived.shape
    hd = width // 3
    cache_spec = cache_by_step(cache, first)
    outs = [(heads, rows, hd), (heads, rows, 2 * hd), (owner_count, heads, cap, BLOCK, 2 * hd)]
    outs = tuple(jax.ShapeDtypeStruct(o, BF16) for o in outs)
    placed_spec = pl.BlockSpec((owner_count, 1, cap, BLOCK, 2 * hd), lambda i, *_: (0, i, 0, 0, 0))
    return pl.pallas_call(
        lambda *refs: finish_body(len(xs), cap, *orders, *refs),
        out_shape=outs,
        grid_spec=pltpu.PrefetchScalarGridSpec(
            num_scalar_prefetch=3,
            grid=(heads,),
            in_specs=[whole(x) for x in xs]
            + weight_specs(ws, at)
            + [by_step(arrived), whole(cosine), whole(sine), cache_spec],
            out_specs=(by_step(outs[0]), by_step(outs[1]), placed_spec),
            scratch_shapes=[
                pltpu.VMEM((rows, width), F32),
                pltpu.SMEM((owner_count * cap,), jnp.int32),
                pltpu.SMEM((owner_count,), jnp.int32),
            ],
        ),
        compiler_params=params(),
        cost_estimate=cost(),
        name="finish_projection",
    )(meta, lengths, owners, *xs, *ws, arrived, cosine, sine, cache)


def attend_body(q_rows, meta, lengths, query, kv, cache, out):
    hd = query.shape[2]
    length = lengths[meta[0]]
    factor = math.log2(math.e) / math.sqrt(hd)
    old_col = lax.broadcasted_iota(jnp.int32, (q_rows, cache.shape[2]), 1)
    causal = lax.broadcasted_iota(jnp.int32, (q_rows, q_rows), 1) <= lax.broadcasted_iota(
        jnp.int32, (q_rows, q_rows), 0
    )
    for step in range(query.shape[1] // q_rows):
        first = step * q_rows
        q = query[0, first : first + q_rows]
        old = jnp.where(old_col < length, dot_t(q, cache[0, 0, :, :hd]), -jnp.inf)
        diag = jnp.where(causal, dot_t(q, kv[0, first : first + q_rows, :hd]), -jnp.inf)
        top = jnp.maximum(jnp.max(old, axis=1, keepdims=True), jnp.max(diag, axis=1, keepdims=True))
        if step:
            new = dot_t(q, kv[0, :first, :hd])
            top = jnp.maximum(top, jnp.max(new, axis=1, keepdims=True))
        old = jnp.exp2((old - top) * factor)
        diag = jnp.exp2((diag - top) * factor)
        total = jnp.sum(old, axis=1, keepdims=True) + jnp.sum(diag, axis=1, keepdims=True)
        result = dot(old.astype(BF16), cache[0, 0, :, hd:]) + dot(diag.astype(BF16), kv[0, first : first + q_rows, hd:])
        if step:
            new = jnp.exp2((new - top) * factor)
            total = total + jnp.sum(new, axis=1, keepdims=True)
            result = result + dot(new.astype(BF16), kv[0, :first, hd:])
        out[0, first : first + q_rows] = (result / total).astype(BF16)


def attend_call(meta, lengths, query, kv, cache, first, q_rows=256):
    heads, rows, hd = query.shape
    out = jax.ShapeDtypeStruct((heads, rows, hd), BF16)
    return pl.pallas_call(
        lambda *refs: attend_body(q_rows, *refs),
        out_shape=out,
        grid_spec=pltpu.PrefetchScalarGridSpec(
            num_scalar_prefetch=2,
            grid=(heads,),
            in_specs=[by_step(query), by_step(kv), cache_by_step(cache, first)],
            out_specs=by_step(out),
        ),
        compiler_params=params(),
        cost_estimate=cost(),
        name="attention",
    )(meta, lengths, query, kv, cache)


def split_body(order_t, meta, *refs):
    held, outs = refs[: -len(order_t)], refs[-len(order_t) :]
    cols = outs[0].shape[-1]
    for r, out in zip(order_t, outs):
        start = pl.multiple_of((meta[1] ^ r) * cols, cols)
        for d, ref in enumerate(held):
            out[d] = ref[:, :, pl.ds(start, cols)]


def split_call(meta, held, order_t):
    heads, hd, width = held[0].shape
    cols = width // len(order_t)
    if cols % 128:
        stacked = jnp.stack(held).reshape(len(held), heads, hd, len(order_t), cols)
        return [lax.dynamic_index_in_dim(stacked, meta[1] ^ r, 3, keepdims=False) for r in order_t]
    vmem = pl.BlockSpec(memory_space=pltpu.VMEM)
    return pl.pallas_call(
        lambda *refs: split_body(order_t, *refs),
        out_shape=[jax.ShapeDtypeStruct((len(held), heads, hd, cols), BF16) for _ in order_t],
        in_specs=[pl.BlockSpec(memory_space=SMEM)] + [vmem] * len(held),
        out_specs=[vmem] * len(order_t),
        compiler_params=params(),
        cost_estimate=cost(),
        name="split_columns",
    )(meta, *held)


def output_body(first, heads, group, order_h, order_t, with_sum, spread, meta, *refs):
    pieces = len(order_h) * len(order_t)
    parts, weights = refs[: 2 * heads], refs[2 * heads : 2 * heads + len(order_t)]
    rest = refs[2 * heads + len(order_t) :]
    tp, hg = meta[1], meta[2]
    total = rest[0][...] if with_sum else None
    for j in range(heads):
        left, right = [], []
        for i, rel_h in enumerate(order_h):
            core, h = divmod(i, len(order_h) // 2)
            for t in range(len(order_t)):
                left.append(parts[2 * j + core][h, t])
                head = (hg ^ rel_h) * group + first + j
                right.append(jnp.concatenate([weights[t][d, head] for d in range(weights[t].shape[0])], axis=1))
        term = dot(jnp.concatenate(left, axis=1), jnp.concatenate(right, axis=0))
        total = term if total is None else total + term
    if not spread:
        rest[-1][...] = total
        return
    scratch, outs = rest[-1], rest[-1 - pieces : -1]
    scratch[...] = total
    run_rows = outs[0].shape[0]
    for i, rel_h in enumerate(order_h):
        for t, rel_t in enumerate(order_t):
            start = pl.multiple_of(((hg ^ rel_h) * len(order_t) + (tp ^ rel_t)) * run_rows, run_rows)
            outs[i * len(order_t) + t][...] = scratch[pl.ds(start, run_rows)].astype(BF16)


def output_call(meta, parts, weights, rows, first, group, order_h, order_t, total=None, spread=False):
    members = len(order_h) * len(order_t)
    dps, cols = weights[0].shape[0], weights[0].shape[-1]
    vmem = pl.BlockSpec(memory_space=pltpu.VMEM)
    operands = (meta, *parts, *weights) + (() if total is None else (total,))
    heads = len(parts) // 2
    out = jax.ShapeDtypeStruct((rows, dps * cols), F32)
    piece = jax.ShapeDtypeStruct((rows // members, dps * cols), BF16)
    return pl.pallas_call(
        lambda *refs: output_body(first, heads, group, order_h, order_t, total is not None, spread, *refs),
        out_shape=[piece] * members if spread else out,
        in_specs=[pl.BlockSpec(memory_space=SMEM)] + [vmem] * (len(operands) - 1),
        out_specs=[vmem] * members if spread else vmem,
        scratch_shapes=[pltpu.VMEM((rows, dps * cols), F32)] if spread else [],
        compiler_params=params(),
        cost_estimate=cost(),
        name="output_projection",
    )(*operands)


def output_plain(place, hg, parts, weights, rows, group, order_h, order_t):
    dps, heads, hd, cols = weights[0].shape
    stacked = jnp.stack(weights).reshape(len(order_t), dps, len(order_h), group, hd, cols)
    stacked = jnp.take(stacked, place, axis=1)
    stacked = jnp.take(stacked, hg ^ jnp.array(order_h, jnp.int32), axis=2)
    total = None
    for j in range(group):
        left = jnp.concatenate([parts[2 * j], parts[2 * j + 1]], axis=0)
        left = left.transpose(2, 0, 1, 3).reshape(rows, -1)
        right = stacked[:, :, :, j].transpose(2, 0, 3, 1, 4).reshape(-1, dps * cols)
        term = dot(left, right)
        total = term if total is None else total + term
    return total.astype(BF16)


def collect_body(*refs):
    head = 0
    for piece in refs[:-1]:
        for j in range(piece.shape[1]):
            refs[-1][0, head, 0] = piece[0, j]
            head += 1


def collect_call(pieces):
    heads = sum(p.shape[1] for p in pieces)
    requests = pieces[0].shape[0]
    tail = pieces[0].shape[2:]
    return pl.pallas_call(
        collect_body,
        grid=(requests,),
        out_shape=jax.ShapeDtypeStruct((1, heads, requests) + tail, BF16),
        in_specs=[by_step(p) for p in pieces],
        out_specs=pl.BlockSpec((1, heads, 1) + tail, lambda r: (0, 0, r, 0, 0, 0)),
        compiler_params=params(),
        cost_estimate=cost(),
        name="collect_blocks",
    )(*pieces)


def residual_body(order_d, order_h, order_t, meta, hidden, *refs):
    pieces, out = refs[:-1], refs[-1]
    cols = pieces[0].shape[1] // len(order_d)
    nh, nt = len(order_h), len(order_t)
    for i, rel_h in enumerate(order_h):
        for t, rel_t in enumerate(order_t):
            piece = pieces[i * nt + t]
            for d, rel_d in enumerate(order_d):
                start = (((meta[0] ^ rel_d) * nh + (meta[2] ^ rel_h)) * nt + (meta[1] ^ rel_t)) * cols
                at = pl.ds(pl.multiple_of(start, cols), cols)
                summed = piece[:, d * cols : (d + 1) * cols].astype(F32)
                out[:, at] = (hidden[:, at].astype(F32) + summed).astype(BF16)


def residual_call(meta, hidden, pieces, order_d, order_h, order_t):
    vmem = pl.BlockSpec(memory_space=pltpu.VMEM)
    return pl.pallas_call(
        lambda *refs: residual_body(order_d, order_h, order_t, *refs),
        out_shape=jax.ShapeDtypeStruct(hidden.shape, BF16),
        in_specs=[pl.BlockSpec(memory_space=SMEM)] + [vmem] * (1 + len(pieces)),
        out_specs=vmem,
        compiler_params=params(),
        cost_estimate=cost(),
        name="residual",
    )(meta, hidden, *pieces)


def plane_swap(x, rel_h, rel_t):
    nt, nh = lax.axis_size("tp"), lax.axis_size("hg")
    pairs = [(t * nh + h, (t ^ rel_t) * nh + (h ^ rel_h)) for t in range(nt) for h in range(nh)]
    return lax.ppermute(x, ("tp", "hg"), pairs)


def head_gather(x, h_strides, t_strides, h_first, token=None):
    def over_h(x):
        for s in h_strides[:-1]:
            x = jnp.concatenate([x, swap(x, "hg", s)], axis=0)
        return x

    def over_t(x):
        for s in t_strides:
            x = jnp.concatenate([x, swap(x, "tp", s)], axis=1)
        return x

    first, second = (over_h, over_t) if h_first else (over_t, over_h)
    x = first(x[None, None])
    if token is not None:
        x = after(x, token)
    x = second(x)
    return [x, swap(x, "hg", h_strides[-1])]


def plan_of(group):
    if group % 4 == 0:
        q = group // 4
        return [2 * q, 2 * q], [(0, q, 2, 3), (q, q, 3, 4), (2 * q, 2 * q, 4, 4)]
    return [group], [(0, group, 3, 3)]


def on_device(hidden_in, norm_gain, qkv_weight, out_weight, cache_kv, cached_lengths, owner_table):
    nt, nh, nd = lax.axis_size("tp"), lax.axis_size("hg"), lax.axis_size("dp")
    tp, hg, dp = lax.axis_index("tp"), lax.axis_index("hg"), lax.axis_index("dp")
    local_rows, width = hidden_in.shape[2:]
    local_depth, _, local_heads, hd = qkv_weight.shape
    group = local_heads // nh
    depth = local_depth * nh
    rows = local_rows * nt * nh
    cap = (cache_kv.shape[2] + rows) // BLOCK // nd
    length = lax.dynamic_index_in_dim(cached_lengths, dp, 0, keepdims=False)

    far, all_d = halving(nd, 2), halving(nd, 1)
    own_rel = offsets(far)
    h_strides, t_strides = halving(nh, 1), halving(nt, 1)
    order_h, order_t = offsets(h_strides), offsets(t_strides)
    members = dp ^ jnp.arange(nd, dtype=jnp.int32)
    place = sum(jnp.where(members == rel, k, 0) for k, rel in enumerate(offsets(all_d))).astype(jnp.int32)
    meta = jnp.stack([dp, tp, hg, hg * group]).astype(jnp.int32)

    cols = out_weight.shape[2] // nt
    out_held = [out_weight]
    for s in far:
        out_held = out_held + hold([swap(w, "dp", s) for w in out_held], 60)
    by_head = qkv_weight.reshape(local_depth, 3, nh, group, hd).transpose(2, 3, 0, 1, 4)
    by_head = by_head.reshape(nh, group, local_depth, 3 * hd)
    sizes, finishing = plan_of(group)
    firsts = [sum(sizes[:c]) for c in range(len(sizes))]
    given = [by_head[:, f : f + size] for f, size in zip(firsts, sizes)]
    mine = [lax.all_to_all(given[0], "hg", 0, 0, tiled=True)]

    def over_h(x):
        for s in h_strides[:-1]:
            x = jnp.concatenate([x, swap(x, "hg", s)], axis=1)
        return x

    def over_t(x):
        for s in t_strides:
            x = jnp.concatenate([x, swap(x, "tp", s)], axis=2)
        return x

    own, sent = norm_call(meta, after(hidden_in[0, 0], given[0]), norm_gain.reshape(1, width), depth, own_rel)
    cut = len(own_rel) // 2
    own, pair = own[:, None, None], swap(sent, "dp", 1)[:, None, None]
    own = [over_t(over_h(own[:cut])), over_h(over_t(own[cut:]))]
    pair = [pair[:cut], pair[cut:]]

    positions = length + jnp.arange(rows, dtype=jnp.int32)
    half_rot = ROT // 2
    frequency = 10000.0 ** (-2.0 * jnp.arange(half_rot, dtype=F32) / ROT)
    angles = positions.astype(F32)[:, None] * frequency[None, :]
    cos_half, sin_half = jnp.cos(angles), jnp.sin(angles)
    cosine = jnp.concatenate([cos_half, cos_half, jnp.ones((rows, hd - ROT), F32)], axis=1)
    sine = jnp.concatenate([-sin_half, sin_half, jnp.zeros((rows, hd - ROT), F32)], axis=1)
    live = dict(out=out_held, mine=mine, given=given[1:], own=own, pair=pair)
    live["tables"] = (cosine, sine)
    live = lax.optimization_barrier(live)

    weights, arrived, ready, placed = [], {}, {}, {}
    handed, gathered = {}, {}
    chunks = len(sizes)
    places = [(c, i) for c, size in enumerate(sizes) for i in range(size)]
    last_stage = chunks + 2
    for stage in range(1, last_stage + 1):
        if stage <= chunks:
            held = [live["mine"][stage - 1]]
            for s in far:
                held = held + hold([swap(w, "dp", s) for w in held], 60)
            weights.append(held)
        if stage == 1:
            live["mine"] = live["mine"] + [lax.all_to_all(g, "hg", 0, 0, tiled=True) for g in live.pop("given")]
            pair = [over_t(over_h(live["pair"][0])), over_h(over_t(live["pair"][1]))]
            live["pair"] = pair + [swap(x, "hg", h_strides[-1]) for x in pair]
            live["out"] = live["out"] + hold([swap(w, "dp", 1) for w in live["out"]], 45)
            own = after(live["own"], tuple(live["pair"]))
            live["own"] = own + [swap(x, "hg", h_strides[-1]) for x in own]
        for first, _, at, handover in finishing:
            if at < handover == stage:
                handed[first] = lax.all_to_all(live["placed"][first], "dp", 0, 0, tiled=True)
                if stage < last_stage:
                    (handed[first],) = hold([handed[first]], 40)
        for first, count, at, _ in finishing:
            c, i = places[first]
            if c + 2 == stage:
                partial = partner_call(live["pair"], live["weights"][c], rows, i, count)
                arrived[first] = swap(partial, "dp", 1)
                if c + 1 == chunks:
                    (arrived[first],) = hold([arrived[first]], 40)
        if stage == 2:
            held = split_call(meta, after(live["out"], partial), order_t)
            live["out"] = [swap(w, "tp", r) if r else w for w, r in zip(held, order_t)]
        for first, count, at, _ in finishing:
            if at == stage - 1 and first not in gathered:
                gathered[first] = [
                    head_gather(live["ready"][first][i], h_strides, t_strides, i % 2 == 0, partial)
                    for i in range(count)
                ]
        for first, count, at, handover in finishing:
            if at == stage:
                c, i = places[first]
                query, kv, placed[first] = finish_call(
                    meta, cached_lengths, owner_table, live["own"], live["weights"][c], arrived[first],
                    *live["tables"], cache_kv, i, first, cap, nd, (order_h, order_t),
                )
                ready[first] = attend_call(meta, cached_lengths, query, kv, cache_kv, first)
                if 2 < at < last_stage:
                    gathered[first] = [
                        head_gather(ready[first][n], h_strides, t_strides, n % 2 == 1) for n in range(count)
                    ]
                if at == handover:
                    blocks = after(placed[first], ready[first])
                    handed[first] = lax.all_to_all(blocks, "dp", 0, 0, tiled=True)
        if stage == last_stage:
            break
        live.update(weights=weights, arrived=arrived, ready=ready, placed=placed, handed=handed, gathered=gathered)
        live = lax.optimization_barrier(live)
        weights = list(live["weights"])
        arrived, ready, placed = dict(live["arrived"]), dict(live["ready"]), dict(live["placed"])
        handed, gathered = dict(live["handed"]), dict(live["gathered"])

    out_weights = live["out"]
    first, count, _, _ = finishing[-1]
    done = sorted(gathered)
    summed = None
    if done and cols % 128 == 0:
        parts = [p for f in done for head in gathered[f] for p in head]
        summed = output_call(meta, parts, out_weights, rows, 0, group, order_h, order_t)
    gathered[first] = [
        head_gather(ready[first][i], h_strides, t_strides, i % 2 == 0, summed) for i in range(count)
    ]
    if cols % 128 == 0:
        parts = [p for head in gathered[first] for p in head]
        pieces = output_call(meta, parts, out_weights, rows, first, group, order_h, order_t, summed, True)
        rels = [(h, t) for h in order_h for t in order_t]
        pieces = [plane_swap(p, h, t) if h or t else p for p, (h, t) in zip(pieces, rels)]
        hidden_out = residual_call(meta, hidden_in[0, 0], pieces, offsets(all_d), order_h, order_t)
    else:
        parts = [p for f in sorted(gathered) for head in gathered[f] for p in head]
        summed = output_plain(place, hg, parts, out_weights, rows, group, order_h, order_t)
        summed = lax.all_to_all(
            summed.reshape(nh * nt, local_rows, nd * cols), ("hg", "tp"), 0, 0, tiled=True
        )
        summed = summed.reshape(nh, nt, local_rows, nd, cols).transpose(2, 3, 0, 1, 4).reshape(local_rows, width)
        hidden_out = (hidden_in[0, 0].astype(F32) + summed.astype(F32)).astype(BF16)
    handed = [handed[f] for f, _, _, _ in finishing]
    return hidden_out[None, None], collect_call(handed)


def solution(mesh):
    return jax.shard_map(
        on_device,
        mesh=mesh,
        in_specs=(
            P("dp", "hg", "tp", None),
            P(),
            P(("dp", "hg"), None, "tp", None),
            P("tp", None, ("dp", "hg")),
            P("dp", "tp", None, None),
            P(),
            P(),
        ),
        out_specs=(P("dp", "hg", "tp", None), P("dp", ("tp", "hg"), None, None, None, None)),
        check_vma=False,
    )
```

time: 429 us -> 374 us (0.87)
  waiting for transfers between devices: 244 us -> 193 us
  local copies, waits for them, and re-layouts: 41.5 us -> 24.5 us
  Pallas kernels: 74.1 us -> 81.5 us
    ppermute x39 -> x34, waiting for transfers between devices: 233 us -> 178 us  [swap(): return lax.ppermute(x, axis, [(i, i ^ stride) for i in range(size)])]
    unnamed x103 -> x49, local copies, waits for them, and re-layouts: 29.8 us -> 14.2 us
    ppermute x39 -> x34, starting transfers between devices: 43.5 us -> 32 us  [swap(): return lax.ppermute(x, axis, [(i, i ^ stride) for i in range(size)])]
    ppermute x0 -> x7, waiting for transfers between devices: none -> 9.69 us  [plane_swap(): return lax.ppermute(x, ('tp', 'hg'), pairs)]
    all_to_all x3 -> x5, starting transfers between devices: 12.5 us -> 21.8 us  [the longest x2 9.13 us: on_device(): lax.all_to_all(live['placed'][first], 'dp', 0, 0, tiled=True)]
    pallas_call x7 -> x15, Pallas kernels: 48.5 us -> 54.2 us  [the longest x3 21.6 us: finish_call(): pl.pallas_call(lambda *refs: finish_body(len(xs), cap, *orders, *refs), o...]
    all_to_all x3 -> x5, waiting for transfers between devices: 10.2 us -> 4.66 us  [the longest x2 4.65 us: on_device(): lax.all_to_all(live['placed'][first], 'dp', 0, 0, tiled=True)]
    ppermute x0 -> x7, starting transfers between devices: none -> 4.51 us  [plane_swap(): return lax.ppermute(x, ('tp', 'hg'), pairs)]
  transfers between devices with their start and end apart: 42 -> 46, of which waited for: 19 -> 24; matrix products, arithmetic and copies ran while one was open for 6% -> 9% of each run, Pallas kernels for 13% -> 21%
where the time goes in v2:
time: 374 us; the launch traced here: 372 us
  waiting for transfers between devices  193 us (52%)
  Pallas kernels  81.5 us (22%)
  starting transfers between devices  58.3 us (16%)
  local copies, waits for them, and re-layouts  24.5 us (7%)
  other arithmetic  14.1 us (4%)
    ppermute x34, waiting for transfers between devices, swap(): return lax.ppermute(x, axis, [(i, i ^ stride) for i in range(size)])  178 us
    ppermute x34, starting transfers between devices, swap(): return lax.ppermute(x, axis, [(i, i ^ stride) for i in range(size)])  32 us
    pallas_call x3, Pallas kernels, finish_call(): pl.pallas_call(lambda *refs: finish_body(len(xs), cap, *orders, *refs), o...  21.6 us
    pallas_call x3, Pallas kernels, partner_call(): pl.pallas_call(lambda *refs: partner_body(len(xs), *refs), grid=(heads,),...  18.1 us
    pallas_call x3, Pallas kernels, attend_call(): pl.pallas_call(lambda *refs: attend_body(q_rows, *refs), out_shape=out, g...  17 us
    unnamed x49, local copies, waits for them, and re-layouts  14.2 us
    pallas_call x2, Pallas kernels, output_call(): pl.pallas_call(lambda *refs: output_body(first, heads, group, order_h, or...  12.5 us
    ppermute x7, waiting for transfers between devices, plane_swap(): return lax.ppermute(x, ('tp', 'hg'), pairs)  9.69 us
  transfers between devices with their start and end apart: 46, of which 24 were waited for; matrix products, arithmetic and copies ran while one was open for 9% of the time, Pallas kernels for 21%

profile of v2, /device:TPU:0, one launch (start us, length us, event | category | flops | bytes accessed | tf_op | source)
XLA Modules:
  0.0 371.9 jit_solution(14926271470417142065)
XLA Ops:
  0.6 4.1 %collective-permute-start = (bf16[16,128,256]{2,1,0:T(8,128)(2,1)}, bf16[16,128,256]{2,1,0:T(8,128)(2,1)S(1)}, u32[]{:S(2)}, u32[]{:S(2)}) collective-permute-start(bf16[16,128,256]{2,1,0:T(8,128)(2,1)} %refs_1_.6), channel_id=1, source_target_pairs={{0,8},{4,12},{8,0},{12,4},{1,9},{5,13},{9,1},{13,5},{2,10},{6,14},... | collective-permute-start | bytes 3145736 | tf_op jit(solution)/shard_map/ppermute | solution.py:44
  4.7 4.9 %copy.20 = bf16[256,3,16,128]{0,3,1,2:T(8,128)(2,1)} copy(bf16[256,3,16,128]{3,2,1,0:T(8,128)(2,1)} %param.9) | data formatting | bytes 6291456 | tf_op args[2]
  9.6 3.3 fusion.1
  12.9 1.6 copy.25
  14.5 4.5 %all-to-all-start = ((bf16[4,2,256,384]{3,2,1,0:T(8,128)(2,1)}), bf16[4,2,256,384]{3,2,1,0:T(8,128)(2,1)}, u32[]{:S(2)}, u32[]{:S(2)}) async-start(bf16[4,2,256,384]{3,2,1,0:T(8,128)(2,1)} %copy.25), calls=%async_computation | async-start | bytes 3145728 | tf_op jit(solution)/shard_map/all_to_all | solution.py:505
  19.1 1.5 layer_norm.1
  20.6 1.6 collective-permute-start.3
  22.2 2.0 collective-permute-start.1
  24.2 1.6 collective-permute-start.5
  27.0 3.0 fusion
  30.2 2.6 copy.24
  33.9 11.3 %collective-permute-done.1 = bf16[1,1,1,128,1024]{4,3,2,1,0:T(8,128)(2,1)} collective-permute-done((bf16[1,1,1,128,1024]{4,3,2,1,0:T(8,128)(2,1)S(1)}, bf16[1,1,1,128,1024]{4,3,2,1,0:T(8,128)(2,1)}, u32[]{:S(2)}, u32[]{:S(2)}) %collective-permute-start.1) | collective-permute-done | bytes 262176 | tf_op jit(solution)/shard_map/ppermute | solution.py:44
  46.2 1.6 collective-permute-start.2
  47.8 1.3 maximum_maximum_fusion
  49.1 9.9 %collective-permute-done.5 = bf16[2,128,1024]{2,1,0:T(8,128)(2,1)} collective-permute-done((bf16[2,128,1024]{2,1,0:T(8,128)(2,1)S(1)}, bf16[2,128,1024]{2,1,0:T(8,128)(2,1)}, u32[]{:S(2)}, u32[]{:S(2)}) %collective-permute-start.5) | collective-permute-done | bytes 524320 | tf_op jit(solution)/shard_map/ppermute | solution.py:44
  59.0 1.9 slice_bitcast_fusion.2
  65.1 1.9 collective-permute-start.7
  67.9 3.2 collective-permute-done.8
  73.9 4.5 %all-to-all-start.1 = ((bf16[4,2,256,384]{3,2,1,0:T(8,128)(2,1)}), bf16[4,2,256,384]{3,2,1,0:T(8,128)(2,1)}, u32[]{:S(2)}, u32[]{:S(2)}) async-start(bf16[4,2,256,384]{3,2,1,0:T(8,128)(2,1)} %copy.24), calls=%async_computation.1 | async-start | bytes 3145728 | tf_op jit(solution)/shard_map/all_to_all | solution.py:546
  78.9 4.1 %collective-permute-done.9 = bf16[1,2,1,128,1024]{4,3,2,1,0:T(8,128)(2,1)} collective-permute-done((bf16[1,2,1,128,1024]{4,3,2,1,0:T(8,128)(2,1)S(1)}, bf16[1,2,1,128,1024]{4,3,2,1,0:T(8,128)(2,1)}, u32[]{:S(2)}, u32[]{:S(2)}) %collective-permute-start.9) | collective-permute-done | bytes 524320 | tf_op jit(solution)/shard_map/ppermute | solution.py:44
  82.9 1.3 pad_maximum_fusion.2.refs_0_
  84.3 3.8 %collective-permute-done.11 = bf16[1,1,2,128,1024]{4,3,2,1,0:T(8,128)(2,1)} collective-permute-done((bf16[1,1,2,128,1024]{4,3,2,1,0:T(8,128)(2,1)}, bf16[1,1,2,128,1024]{4,3,2,1,0:T(8,128)(2,1)}, u32[]{:S(2)}, u32[]{:S(2)}) %collective-permute-start.11) | collective-permute-done | bytes 524320 | tf_op jit(solution)/shard_map/ppermute | solution.py:44
  88.1 2.3 pad_maximum_fusion.3.refs_1_
  90.4 30.4 %collective-permute-done.6.refs_0_ = bf16[16,128,256]{2,1,0:T(8,128)(2,1)} collective-permute-done((bf16[16,128,256]{2,1,0:T(8,128)(2,1)}, bf16[16,128,256]{2,1,0:T(8,128)(2,1)}, u32[]{:S(2)}, u32[]{:S(2)}) %collective-permute-start.6) | collective-permute-done | bytes 1048608 | tf_op jit(solution)/shard_map/ppermute | solution.py:44
  120.7 19.9 %collective-permute-done.7.refs_1_ = bf16[16,128,256]{2,1,0:T(8,128)(2,1)} collective-permute-done((bf16[16,128,256]{2,1,0:T(8,128)(2,1)}, bf16[16,128,256]{2,1,0:T(8,128)(2,1)}, u32[]{:S(2)}, u32[]{:S(2)}) %collective-permute-start.7) | collective-permute-done | bytes 1048608 | tf_op jit(solution)/shard_map/ppermute | solution.py:44
  141.2 8.8 %collective-permute-done.16.refs_0_ = bf16[4,2,256,384]{3,2,1,0:T(8,128)(2,1)} collective-permute-done((bf16[4,2,256,384]{3,2,1,0:T(8,128)(2,1)}, bf16[4,2,256,384]{3,2,1,0:T(8,128)(2,1)}, u32[]{:S(2)}, u32[]{:S(2)}) %collective-permute-start.16) | collective-permute-done | bytes 1572896 | tf_op jit(solution)/shard_map/ppermute | solution.py:44
  150.1 4.6 %partner_product.3 = bf16[1,1024,384]{2,1,0:T(8,128)(2,1)S(1)} custom-call(bf16[1,2,2,128,1024]{4,3,2,1,0:T(8,128)(2,1)S(1)} %pad_maximum_fusion.2.refs_0_, bf16[1,2,2,128,1024]{4,3,2,1,0:T(8,128)(2,1)} %pad_maximum_fusion.3.refs_1_, bf16[1,2,2,128,1024]{4,3,2,1,0:T(8,128)(2,1)} %collective-permute-done.12.refs_2_, ...), custom_call_target="tpu_custom_call" | custom-call | flops 1 | bytes 1 | tf_op jit(solution)/shard_map/partner_product/pallas_call | solution.py:145
  154.8 3.0 collective-permute-start.17
  157.7 5.5 %partner_product.4 = bf16[1,1024,384]{2,1,0:T(8,128)(2,1)} custom-call(bf16[1,2,2,128,1024]{4,3,2,1,0:T(8,128)(2,1)S(1)} %pad_maximum_fusion.2.refs_0_, bf16[1,2,2,128,1024]{4,3,2,1,0:T(8,128)(2,1)} %pad_maximum_fusion.3.refs_1_, bf16[1,2,2,128,1024]{4,3,2,1,0:T(8,128)(2,1)} %collective-permute-done.12.refs_2_, ...), custom_call_target="tpu_custom_call" | custom-call | flops 1 | bytes 1 | tf_op jit(solution)/shard_map/partner_product/pallas_call | solution.py:145
  163.4 4.7 %split_columns.1 = (bf16[4,16,128,128]{3,2,1,0:T(8,128)(2,1)}, bf16[4,16,128,128]{3,2,1,0:T(8,128)(2,1)}) custom-call(s32[4]{0:T(128)S(1)} %copy-done.13, bf16[16,128,256]{2,1,0:T(8,128)(2,1)} %refs_1_.6, bf16[16,128,256]{2,1,0:T(8,128)(2,1)S(1)} %copy-done.9, bf16[16,128,256]{2,1,0:T(8,128)(2,1)} %get-tuple-element.129.refs_3_, ...), custom_call_target="tpu_custom_call" | custom-call | flops 1 | bytes 1 | tf_op jit(solution)/shard_map/split_columns/pallas_call | solution.py:320
  168.1 1.5 collective-permute-start.19
  169.6 32.4 %collective-permute-done.17.refs_9_ = bf16[1,1024,384]{2,1,0:T(8,128)(2,1)S(1)} collective-permute-done((bf16[1,1024,384]{2,1,0:T(8,128)(2,1)S(1)}, bf16[1,1024,384]{2,1,0:T(8,128)(2,1)S(1)}, u32[]{:S(2)}, u32[]{:S(2)}) %collective-permute-start.17) | collective-permute-done | bytes 786464 | tf_op jit(solution)/shard_map/ppermute | solution.py:44
  202.0 5.7 %finish_projection.3 = (bf16[1,1024,128]{2,1,0:T(8,128)(2,1)S(1)}, bf16[1,1024,256]{2,1,0:T(8,128)(2,1)S(1)}, bf16[4,1,4,128,256]{4,3,2,1,0:T(8,128)(2,1)S(1)}) custom-call(s32[4]{0:T(128)S(1)} %copy-done.13, s32[4]{0:T(128)S(1)} %copy-done.14, s32[4,16]{1,0:T(4,128)S(1)} %copy-done.16, bf16[1,2,2,128,1024]{4,3,2,1,0:T(8,128)(2,1)S(1)} %pad_maximum_fusion.refs_3_, ...), custom_call_target="tpu_custom_call" | custom-call | flops 1 | bytes 1 | tf_op jit(solution)/shard_map/finish_projection/pallas_call | solution.py:236
  208.7 4.6 %attention.3 = bf16[1,1024,128]{2,1,0:T(8,128)(2,1)S(1)} custom-call(s32[4]{0:T(128)S(1)} %copy-done.13, s32[4]{0:T(128)S(1)} %copy-done.15, bf16[1,1024,128]{2,1,0:T(8,128)(2,1)S(1)} %get-tuple-element.140.refs_2_, bf16[1,1024,256]{2,1,0:T(8,128)(2,1)S(1)} %get-tuple-element.141.refs_3_, bf16[1,16,1024,256]{3,2,1,0:T(8,128)(2,1)} %refs_4_.5), custom_call_target="tpu_custom_call" | custom-call | flops 1 | bytes 1 | tf_op jit(solution)/shard_map/attention/pallas_call | solution.py:289
  213.4 7.2 %collective-permute-done.20.refs_0_ = bf16[4,2,256,384]{3,2,1,0:T(8,128)(2,1)} collective-permute-done((bf16[4,2,256,384]{3,2,1,0:T(8,128)(2,1)}, bf16[4,2,256,384]{3,2,1,0:T(8,128)(2,1)}, u32[]{:S(2)}, u32[]{:S(2)}) %collective-permute-start.20) | collective-permute-done | bytes 1572896 | tf_op jit(solution)/shard_map/ppermute | solution.py:44
  220.5 4.6 %collective-permute-done.18.refs_9_ = bf16[1,1024,384]{2,1,0:T(8,128)(2,1)} collective-permute-done((bf16[1,1024,384]{2,1,0:T(8,128)(2,1)}, bf16[1,1024,384]{2,1,0:T(8,128)(2,1)}, u32[]{:S(2)}, u32[]{:S(2)}) %collective-permute-start.18) | collective-permute-done | bytes 786464 | tf_op jit(solution)/shard_map/ppermute | solution.py:44
  225.1 4.5 %all-to-all-start.2 = ((bf16[4,1,4,128,256]{4,3,2,1,0:T(8,128)(2,1)}), bf16[4,1,4,128,256]{4,3,2,1,0:T(8,128)(2,1)}, u32[]{:S(2)}, u32[]{:S(2)}) async-start(bf16[4,1,4,128,256]{4,3,2,1,0:T(8,128)(2,1)} %copy-done.11), calls=%async_computation.2 | async-start | bytes 2097152 | tf_op jit(solution)/shard_map/all_to_all | solution.py:554
  229.6 1.7 collective-permute-start.22
  233.4 5.9 %finish_projection.4 = (bf16[1,1024,128]{2,1,0:T(8,128)(2,1)S(1)}, bf16[1,1024,256]{2,1,0:T(8,128)(2,1)S(1)}, bf16[4,1,4,128,256]{4,3,2,1,0:T(8,128)(2,1)S(1)}) custom-call(s32[4]{0:T(128)S(1)} %copy-done.13, s32[4]{0:T(128)S(1)} %copy-done.15, s32[4,16]{1,0:T(4,128)S(1)} %copy-done.16, bf16[1,2,2,128,1024]{4,3,2,1,0:T(8,128)(2,1)S(1)} %pad_maximum_fusion.refs_3_, ...), custom_call_target="tpu_custom_call" | custom-call | flops 1 | bytes 1 | tf_op jit(solution)/shard_map/finish_projection/pallas_call | solution.py:236
  240.4 4.6 %attention.4 = bf16[1,1024,128]{2,1,0:T(8,128)(2,1)S(1)} custom-call(s32[4]{0:T(128)S(1)} %copy-done.13, s32[4]{0:T(128)S(1)} %copy-done.15, bf16[1,1024,128]{2,1,0:T(8,128)(2,1)S(1)} %get-tuple-element.159.refs_2_, bf16[1,1024,256]{2,1,0:T(8,128)(2,1)S(1)} %get-tuple-element.160.refs_3_, bf16[1,16,1024,256]{3,2,1,0:T(8,128)(2,1)} %refs_4_.5), custom_call_target="tpu_custom_call" | custom-call | flops 1 | bytes 1 | tf_op jit(solution)/shard_map/attention/pallas_call | solution.py:289
  245.0 1.6 collective-permute-start.25
  246.6 7.9 %partner_product.5 = bf16[2,1024,384]{2,1,0:T(8,128)(2,1)} custom-call(bf16[1,2,2,128,1024]{4,3,2,1,0:T(8,128)(2,1)S(1)} %pad_maximum_fusion.2.refs_0_, bf16[1,2,2,128,1024]{4,3,2,1,0:T(8,128)(2,1)} %pad_maximum_fusion.3.refs_1_, bf16[1,2,2,128,1024]{4,3,2,1,0:T(8,128)(2,1)} %collective-permute-done.12.refs_2_, ...), custom_call_target="tpu_custom_call" | custom-call | flops 1 | bytes 1 | tf_op jit(solution)/shard_map/partner_product/pallas_call | solution.py:145
  255.7 1.7 collective-permute-start.21
  258.2 8.1 %collective-permute-done.23 = bf16[2,1,1024,128]{3,2,1,0:T(8,128)(2,1)S(1)} collective-permute-done((bf16[2,1,1024,128]{3,2,1,0:T(8,128)(2,1)S(1)}, bf16[2,1,1024,128]{3,2,1,0:T(8,128)(2,1)S(1)}, u32[]{:S(2)}, u32[]{:S(2)}) %collective-permute-start.23) | collective-permute-done | bytes 524320 | tf_op jit(solution)/shard_map/ppermute | solution.py:44
  268.7 20.9 %collective-permute-done.21.refs_0_ = bf16[2,1024,384]{2,1,0:T(8,128)(2,1)} collective-permute-done((bf16[2,1024,384]{2,1,0:T(8,128)(2,1)}, bf16[2,1024,384]{2,1,0:T(8,128)(2,1)}, u32[]{:S(2)}, u32[]{:S(2)}) %collective-permute-start.21) | collective-permute-done | bytes 1572896 | tf_op jit(solution)/shard_map/ppermute | solution.py:44
  289.7 4.6 %all-to-all-start.3 = ((bf16[4,1,4,128,256]{4,3,2,1,0:T(8,128)(2,1)}), bf16[4,1,4,128,256]{4,3,2,1,0:T(8,128)(2,1)}, u32[]{:S(2)}, u32[]{:S(2)}) async-start(bf16[4,1,4,128,256]{4,3,2,1,0:T(8,128)(2,1)} %copy-done.10), calls=%async_computation.3 | async-start | bytes 2097152 | tf_op jit(solution)/shard_map/all_to_all | solution.py:554
  294.4 10.0 %finish_projection.5 = (bf16[2,1024,128]{2,1,0:T(8,128)(2,1)S(1)}, bf16[2,1024,256]{2,1,0:T(8,128)(2,1)S(1)}, bf16[4,2,4,128,256]{4,3,2,1,0:T(8,128)(2,1)}) custom-call(s32[4]{0:T(128)S(1)} %copy-done.13, s32[4]{0:T(128)S(1)} %copy-done.15, s32[4,16]{1,0:T(4,128)S(1)} %copy-done.16, bf16[1,2,2,128,1024]{4,3,2,1,0:T(8,128)(2,1)S(1)} %pad_maximum_fusion.refs_3_, ...), custom_call_target="tpu_custom_call" | custom-call | flops 1 | bytes 1 | tf_op jit(solution)/shard_map/finish_projection/pallas_call | solution.py:236
  304.4 7.7 %attention.5 = bf16[2,1024,128]{2,1,0:T(8,128)(2,1)S(1)} custom-call(s32[4]{0:T(128)S(1)} %copy-done.13, s32[4]{0:T(128)S(1)} %copy-done.15, bf16[2,1024,128]{2,1,0:T(8,128)(2,1)S(1)} %get-tuple-element.174.refs_2_, bf16[2,1024,256]{2,1,0:T(8,128)(2,1)S(1)} %get-tuple-element.175.refs_3_, bf16[1,16,1024,256]{3,2,1,0:T(8,128)(2,1)} %refs_4_.5), custom_call_target="tpu_custom_call" | custom-call | flops 1 | bytes 1 | tf_op jit(solution)/shard_map/attention/pallas_call | solution.py:289
  312.1 4.6 %all-to-all-done.3.refs_1_ = bf16[4,1,4,128,256]{4,3,2,1,0:T(8,128)(2,1)} async-done(((bf16[4,1,4,128,256]{4,3,2,1,0:T(8,128)(2,1)}), bf16[4,1,4,128,256]{4,3,2,1,0:T(8,128)(2,1)}, u32[]{:S(2)}, u32[]{:S(2)}) %all-to-all-start.3) | async-done | bytes 1048608 | tf_op jit(solution)/shard_map/all_to_all | solution.py:554
  316.7 3.6 all-to-all-start.4
  320.4 1.6 collective-permute-start.31
  322.0 1.4 collective-permute-start.28
  323.4 7.2 %output_projection.2.refs_7_ = f32[1024,512]{1,0:T(8,128)} custom-call(s32[4]{0:T(128)S(1)} %copy-done.13, bf16[2,2,1024,128]{3,2,1,0:T(8,128)(2,1)} %constant_dynamic-update-slice_fusion.4.refs_1_, bf16[2,2,1024,128]{3,2,1,0:T(8,128)(2,1)} %collective-permute-done.24.refs_2_, bf16[2,2,1024,128]{3,2,1,0:T(8,128)(2,1)} %pad_maximum_fusion.4.refs_3_, ...), custom_call_target="tpu_custom_call" | custom-call | flops 1 | bytes 1 | tf_op jit(solution)/shard_map/output_projection/pallas_call | solution.py:367
  332.0 9.9 %collective-permute-done.32 = bf16[1,2,1024,128]{3,2,1,0:T(8,128)(2,1)S(1)} collective-permute-done((bf16[1,2,1024,128]{3,2,1,0:T(8,128)(2,1)S(1)}, bf16[1,2,1024,128]{3,2,1,0:T(8,128)(2,1)S(1)}, u32[]{:S(2)}, u32[]{:S(2)}) %collective-permute-start.32) | collective-permute-done | bytes 524320 | tf_op jit(solution)/shard_map/ppermute | solution.py:44
  342.7 2.0 collective-permute-done.33.refs_4_
  344.7 1.5 collective-permute-done.30.refs_2_
  346.2 5.3 %output_projection.3 = (bf16[128,512]{1,0:T(8,128)(2,1)S(1)}, bf16[128,512]{1,0:T(8,128)(2,1)S(1)}, bf16[128,512]{1,0:T(8,128)(2,1)S(1)}, bf16[128,512]{1,0:T(8,...) custom-call(s32[4]{0:T(128)S(1)} %copy-done.13, ...), custom_call_target="tpu_custom_call" | custom-call | flops 1 | bytes 1 | tf_op jit(solution)/shard_map/output_projection/pallas_call | solution.py:367
  352.8 2.3 collective-permute-start.36
  355.7 1.4 collective-permute-done.34.refs_3_
  357.1 1.4 collective-permute-done.35.refs_4_
  358.8 3.3 collective-permute-done.36.refs_5_
  363.0 2.7 collective-permute-done.40.refs_9_
  365.8 2.0 residual.1
  367.7 4.2 %collect_blocks.1 = bf16[1,4,4,4,128,256]{5,4,3,2,1,0:T(8,128)(2,1)} custom-call(bf16[4,1,4,128,256]{4,3,2,1,0:T(8,128)(2,1)} %hold.11.refs_0_, bf16[4,1,4,128,256]{4,3,2,1,0:T(8,128)(2,1)} %all-to-all-done.3.refs_1_, bf16[4,2,4,128,256]{4,3,2,1,0:T(8,128)(2,1)S(1)} %all-to-all-done.4.refs_2_), custom_call_target="tpu_custom_call" | custom-call | flops 1 | bytes 1 | tf_op jit(solution)/shard_map/collect_blocks/pallas_call | solution.py:406
  (129 shorter events, 26.8 us)
Async XLA Ops:
  0.6 62.4 %collective-permute-start = (bf16[16,128,256]{2,1,0:T(8,128)(2,1)}, bf16[16,128,256]{2,1,0:T(8,128)(2,1)S(1)}, u32[]{:S(2)}, u32[]{:S(2)}) collective-permute-start(bf16[16,128,256]{2,1,0:T(8,128)(2,1)} %refs_1_.6), channel_id=1, source_target_pairs={{0,8},{4,12},{8,0},{12,4},{1,9},{5,13},{9,1},{13,5},{2,10},{6,14},... | collective-permute-start | bytes 3145736 | tf_op jit(solution)/shard_map/ppermute | solution.py:44
  14.5 4.6 %copy-start.6 = (bf16[1,1,128,4096]{3,2,1,0:T(8,128)(2,1)S(1)}, bf16[1,1,128,4096]{3,2,1,0:T(8,128)(2,1)}, u32[]{:S(2)}) copy-start(bf16[1,1,128,4096]{3,2,1,0:T(8,128)(2,1)} %param.7) | copy-start | bytes 3145732
  14.5 4.6 %copy-start.17 = (f32[4096]{0:T(1024)S(1)}, f32[4096]{0:T(1024)}, u32[]{:S(2)}) copy-start(f32[4096]{0:T(1024)} %param.8) | copy-start | bytes 49156
  14.5 49.6 %all-to-all-start = ((bf16[4,2,256,384]{3,2,1,0:T(8,128)(2,1)}), bf16[4,2,256,384]{3,2,1,0:T(8,128)(2,1)}, u32[]{:S(2)}, u32[]{:S(2)}) async-start(bf16[4,2,256,384]{3,2,1,0:T(8,128)(2,1)} %copy.25), calls=%async_computation | async-start | bytes 3145728 | tf_op jit(solution)/shard_map/all_to_all | solution.py:505
  19.0 6.8 %copy-start.14 = (s32[4]{0:T(128)S(1)}, s32[4]{0:T(128)}, u32[]{:S(2)}) copy-start(s32[4]{0:T(128)} %refs_1_.12) | copy-start | bytes 52
  19.1 1.6 copy-start.12
  20.6 12.1 %collective-permute-start.3 = (bf16[1,1,1,128,1024]{4,3,2,1,0:T(8,128)(2,1)S(1)}, bf16[1,1,1,128,1024]{4,3,2,1,0:T(8,128)(2,1)}, u32[]{:S(2)}, u32[]{:S(2)}) collective-permute-start(bf16[1,1,1,128,1024]{4,3,2,1,0:T(8,128)(2,1)S(1)} %get-tuple-element.202), channel_id=1, source_target_pairs={{0,16},{16,0},{1,17},{17,1},{2,18},{18,2},{3,19},{19,3},{4,20},{20... | collective-permute-start | bytes 786440 | tf_op jit(solution)/shard_map/ppermute | solution.py:44
  22.2 23.0 %collective-permute-start.1 = (bf16[1,1,1,128,1024]{4,3,2,1,0:T(8,128)(2,1)S(1)}, bf16[1,1,1,128,1024]{4,3,2,1,0:T(8,128)(2,1)}, u32[]{:S(2)}, u32[]{:S(2)}) collective-permute-start(bf16[1,1,1,128,1024]{4,3,2,1,0:T(8,128)(2,1)S(1)} %get-tuple-element.203), channel_id=1, source_target_pairs={{0,2},{1,3},{2,0},{3,1},{4,6},{5,7},{6,4},{7,5},{8,10},{9,11},{10,... | collective-permute-start | bytes 786440 | tf_op jit(solution)/shard_map/ppermute | solution.py:44
  24.2 34.8 %collective-permute-start.5 = (bf16[2,128,1024]{2,1,0:T(8,128)(2,1)S(1)}, bf16[2,128,1024]{2,1,0:T(8,128)(2,1)}, u32[]{:S(2)}, u32[]{:S(2)}) collective-permute-start(bf16[2,128,1024]{2,1,0:T(8,128)(2,1)S(1)} %get-tuple-element.101), channel_id=1, source_target_pairs={{0,4},{4,0},{8,12},{12,8},{1,5},{5,1},{9,13},{13,9},{2,6},{6,2},{1... | collective-permute-start | bytes 1572872 | tf_op jit(solution)/shard_map/ppermute | solution.py:44
  32.7 15.1 %copy-start.18 = (f32[1024,16]{1,0:T(8,128)S(1)}, f32[1024,16]{1,0:T(8,128)}, u32[]{:S(2)}) copy-start(f32[1024,16]{1,0:T(8,128)} %get-tuple-element.206) | copy-start | bytes 196612
  33.8 27.1 %collective-permute-start.4 = (bf16[1,1,2,128,1024]{4,3,2,1,0:T(8,128)(2,1)S(1)}, bf16[1,1,2,128,1024]{4,3,2,1,0:T(8,128)(2,1)S(1)}, u32[]{:S(2)}, u32[]{:S(2)}) collective-permute-start(bf16[1,1,2,128,1024]{4,3,2,1,0:T(8,128)(2,1)S(1)} %pad_maximum_fusion.6), channel_id=1, source_target_pairs={{0,2},{1,3},{2,0},{3,1},{4,6},{5,7},{6,4},{7,5},{8,10},{9,11},{10,... | collective-permute-start | bytes 1572872 | tf_op jit(solution)/shard_map/ppermute | solution.py:44
  46.2 15.7 %collective-permute-start.2 = (bf16[1,2,1,128,1024]{4,3,2,1,0:T(8,128)(2,1)S(1)}, bf16[1,2,1,128,1024]{4,3,2,1,0:T(8,128)(2,1)S(1)}, u32[]{:S(2)}, u32[]{:S(2)}) collective-permute-start(bf16[1,2,1,128,1024]{4,3,2,1,0:T(8,128)(2,1)S(1)} %pad_maximum_fusion.5), channel_id=1, source_target_pairs={{0,16},{16,0},{1,17},{17,1},{2,18},{18,2},{3,19},{19,3},{4,20},{20... | collective-permute-start | bytes 1572872 | tf_op jit(solution)/shard_map/ppermute | solution.py:44
  63.0 1.4 copy-start.20
  64.0 7.1 %collective-permute-start.8 = (bf16[1,1,1,128,1024]{4,3,2,1,0:T(8,128)(2,1)}, bf16[1,1,1,128,1024]{4,3,2,1,0:T(8,128)(2,1)S(1)}, u32[]{:S(2)}, u32[]{:S(2)}) collective-permute-start(bf16[1,1,1,128,1024]{4,3,2,1,0:T(8,128)(2,1)} %get-tuple-element.110), channel_id=1, source_target_pairs={{0,2},{1,3},{2,0},{3,1},{4,6},{5,7},{6,4},{7,5},{8,10},{9,11},{10,... | collective-permute-start | bytes 786440 | tf_op jit(solution)/shard_map/ppermute | solution.py:44
  64.4 8.1 %collective-permute-start.10 = (bf16[1,1,1,128,1024]{4,3,2,1,0:T(8,128)(2,1)S(1)}, bf16[1,1,1,128,1024]{4,3,2,1,0:T(8,128)(2,1)S(1)}, u32[]{:S(2)}, u32[]{:S(2)}) collective-permute-start(bf16[1,1,1,128,1024]{4,3,2,1,0:T(8,128)(2,1)S(1)} %copy-done.20), channel_id=1, source_target_pairs={{0,16},{16,0},{1,17},{17,1},{2,18},{18,2},{3,19},{19,3},{4,20},{20... | collective-permute-start | bytes 786440 | tf_op jit(solution)/shard_map/ppermute | solution.py:44
  64.9 55.8 %collective-permute-start.6 = (bf16[16,128,256]{2,1,0:T(8,128)(2,1)}, bf16[16,128,256]{2,1,0:T(8,128)(2,1)}, u32[]{:S(2)}, u32[]{:S(2)}) collective-permute-start(bf16[16,128,256]{2,1,0:T(8,128)(2,1)} %refs_1_.6), channel_id=1, source_target_pairs={{0,4},{4,0},{8,12},{12,8},{1,5},{5,1},{9,13},{13,9},{2,6},{6,2},{1... | collective-permute-start | bytes 3145736 | tf_op jit(solution)/shard_map/ppermute | solution.py:44
  65.1 75.6 %collective-permute-start.7 = (bf16[16,128,256]{2,1,0:T(8,128)(2,1)}, bf16[16,128,256]{2,1,0:T(8,128)(2,1)}, u32[]{:S(2)}, u32[]{:S(2)}) collective-permute-start(bf16[16,128,256]{2,1,0:T(8,128)(2,1)} %hold.6.refs_2_), channel_id=1, source_target_pairs={{0,4},{4,0},{8,12},{12,8},{1,5},{5,1},{9,13},{13,9},{2,6},{6,2},{1... | collective-permute-start | bytes 3145736 | tf_op jit(solution)/shard_map/ppermute | solution.py:44
  71.2 2.8 copy-start.19
  71.2 11.8 %collective-permute-start.9 = (bf16[1,2,1,128,1024]{4,3,2,1,0:T(8,128)(2,1)S(1)}, bf16[1,2,1,128,1024]{4,3,2,1,0:T(8,128)(2,1)}, u32[]{:S(2)}, u32[]{:S(2)}) collective-permute-start(bf16[1,2,1,128,1024]{4,3,2,1,0:T(8,128)(2,1)S(1)} %constant_dynamic-update-slice_fusion), channel_id=1, source_target_pairs={{0,16},{16,0},{1,17},{17,1},{2,18},{18,2},{3,19},{19,3},{4,20},{20... | collective-permute-start | bytes 1572872 | tf_op jit(solution)/shard_map/ppermute | solution.py:44
  73.2 14.9 %collective-permute-start.11 = (bf16[1,1,2,128,1024]{4,3,2,1,0:T(8,128)(2,1)}, bf16[1,1,2,128,1024]{4,3,2,1,0:T(8,128)(2,1)}, u32[]{:S(2)}, u32[]{:S(2)}) collective-permute-start(bf16[1,1,2,128,1024]{4,3,2,1,0:T(8,128)(2,1)} %constant_dynamic-update-slice_fusion.2), channel_id=1, source_target_pairs={{0,2},{1,3},{2,0},{3,1},{4,6},{5,7},{6,4},{7,5},{8,10},{9,11},{10,... | collective-permute-start | bytes 1572872 | tf_op jit(solution)/shard_map/ppermute | solution.py:44
  73.9 76.1 %all-to-all-start.1 = ((bf16[4,2,256,384]{3,2,1,0:T(8,128)(2,1)}), bf16[4,2,256,384]{3,2,1,0:T(8,128)(2,1)}, u32[]{:S(2)}, u32[]{:S(2)}) async-start(bf16[4,2,256,384]{3,2,1,0:T(8,128)(2,1)} %copy.24), calls=%async_computation.1 | async-start | bytes 3145728 | tf_op jit(solution)/shard_map/all_to_all | solution.py:546
  78.5 71.5 %collective-permute-start.16 = (bf16[4,2,256,384]{3,2,1,0:T(8,128)(2,1)}, bf16[4,2,256,384]{3,2,1,0:T(8,128)(2,1)}, u32[]{:S(2)}, u32[]{:S(2)}) collective-permute-start(bf16[4,2,256,384]{3,2,1,0:T(8,128)(2,1)} %all-to-all-done.refs_4_.refs_7_), channel_id=1, source_target_pairs={{0,8},{4,12},{8,0},{12,4},{1,9},{5,13},{9,1},{13,5},{2,10},{6,14},... | collective-permute-start | bytes 4718600 | tf_op jit(solution)/shard_map/ppermute | solution.py:44
  84.2 56.4 %collective-permute-start.12 = (bf16[1,2,2,128,1024]{4,3,2,1,0:T(8,128)(2,1)S(1)}, bf16[1,2,2,128,1024]{4,3,2,1,0:T(8,128)(2,1)}, u32[]{:S(2)}, u32[]{:S(2)}) collective-permute-start(bf16[1,2,2,128,1024]{4,3,2,1,0:T(8,128)(2,1)S(1)} %pad_maximum_fusion.2.refs_0_), channel_id=1, source_target_pairs={{0,1},{1,0},{2,3},{3,2},{4,5},{5,4},{6,7},{7,6},{8,9},{9,8},{10,11... | collective-permute-start | bytes 3145736 | tf_op jit(solution)/shard_map/ppermute | solution.py:44
  90.4 50.3 %collective-permute-start.13 = (bf16[1,2,2,128,1024]{4,3,2,1,0:T(8,128)(2,1)}, bf16[1,2,2,128,1024]{4,3,2,1,0:T(8,128)(2,1)}, u32[]{:S(2)}, u32[]{:S(2)}) collective-permute-start(bf16[1,2,2,128,1024]{4,3,2,1,0:T(8,128)(2,1)} %pad_maximum_fusion.3.refs_1_), channel_id=1, source_target_pairs={{0,1},{1,0},{2,3},{3,2},{4,5},{5,4},{6,7},{7,6},{8,9},{9,8},{10,11... | collective-permute-start | bytes 3145736 | tf_op jit(solution)/shard_map/ppermute | solution.py:44
  140.6 9.4 %collective-permute-start.14 = (bf16[1,2,2,128,1024]{4,3,2,1,0:T(8,128)(2,1)S(1)}, bf16[1,2,2,128,1024]{4,3,2,1,0:T(8,128)(2,1)}, u32[]{:S(2)}, u32[]{:S(2)}) collective-permute-start(bf16[1,2,2,128,1024]{4,3,2,1,0:T(8,128)(2,1)S(1)} %pad_maximum_fusion.refs_3_), channel_id=1, source_target_pairs={{0,1},{1,0},{2,3},{3,2},{4,5},{5,4},{6,7},{7,6},{8,9},{9,8},{10,11... | collective-permute-start | bytes 3145736 | tf_op jit(solution)/shard_map/ppermute | solution.py:44
  140.7 9.3 %collective-permute-start.15 = (bf16[1,2,2,128,1024]{4,3,2,1,0:T(8,128)(2,1)S(1)}, bf16[1,2,2,128,1024]{4,3,2,1,0:T(8,128)(2,1)}, u32[]{:S(2)}, u32[]{:S(2)}) collective-permute-start(bf16[1,2,2,128,1024]{4,3,2,1,0:T(8,128)(2,1)S(1)} %pad_maximum_fusion.1.refs_4_), channel_id=1, source_target_pairs={{0,1},{1,0},{2,3},{3,2},{4,5},{5,4},{6,7},{7,6},{8,9},{9,8},{10,11... | collective-permute-start | bytes 3145736 | tf_op jit(solution)/shard_map/ppermute | solution.py:44
  150.0 70.5 %collective-permute-start.20 = (bf16[4,2,256,384]{3,2,1,0:T(8,128)(2,1)}, bf16[4,2,256,384]{3,2,1,0:T(8,128)(2,1)}, u32[]{:S(2)}, u32[]{:S(2)}) collective-permute-start(bf16[4,2,256,384]{3,2,1,0:T(8,128)(2,1)} %all-to-all-done.1.refs_4_.refs_7_), channel_id=1, source_target_pairs={{0,8},{4,12},{8,0},{12,4},{1,9},{5,13},{9,1},{13,5},{2,10},{6,14},... | collective-permute-start | bytes 4718600 | tf_op jit(solution)/shard_map/ppermute | solution.py:44
  154.7 8.7 %copy-start.9 = (bf16[16,128,256]{2,1,0:T(8,128)(2,1)S(1)}, bf16[16,128,256]{2,1,0:T(8,128)(2,1)}, u32[]{:S(2)}) copy-start(bf16[16,128,256]{2,1,0:T(8,128)(2,1)} %hold.6.refs_2_) | copy-start | bytes 3145732
  154.8 8.7 %copy-start.13 = (s32[4]{0:T(128)S(1)}, s32[4]{0:T(128)}, u32[]{:S(2)}) copy-start(s32[4]{0:T(128)} %copy-done.12) | copy-start | bytes 52
  154.8 47.2 %collective-permute-start.17 = (bf16[1,1024,384]{2,1,0:T(8,128)(2,1)S(1)}, bf16[1,1024,384]{2,1,0:T(8,128)(2,1)S(1)}, u32[]{:S(2)}, u32[]{:S(2)}) collective-permute-start(bf16[1,1024,384]{2,1,0:T(8,128)(2,1)S(1)} %partner_product.3), channel_id=1, source_target_pairs={{0,4},{4,0},{8,12},{12,8},{1,5},{5,1},{9,13},{13,9},{2,6},{6,2},{1... | collective-permute-start | bytes 2359304 | tf_op jit(solution)/shard_map/ppermute | solution.py:44
  163.3 38.7 %copy-start = (f32[1024,128]{1,0:T(8,128)S(1)}, f32[1024,128]{1,0:T(8,128)}, u32[]{:S(2)}) copy-start(f32[1024,128]{1,0:T(8,128)} %get-tuple-element.172.refs_10_) | copy-start | bytes 1572868
  163.3 38.7 %copy-start.3 = (f32[1024,128]{1,0:T(8,128)S(1)}, f32[1024,128]{1,0:T(8,128)}, u32[]{:S(2)}) copy-start(f32[1024,128]{1,0:T(8,128)} %get-tuple-element.173.refs_11_) | copy-start | bytes 1572868
  163.3 38.7 %copy-start.16 = (s32[4,16]{1,0:T(4,128)S(1)}, s32[4,16]{1,0:T(4,128)}, u32[]{:S(2)}) copy-start(s32[4,16]{1,0:T(4,128)} %refs_2_.5) | copy-start | bytes 772
  163.3 61.8 %collective-permute-start.18 = (bf16[1,1024,384]{2,1,0:T(8,128)(2,1)}, bf16[1,1024,384]{2,1,0:T(8,128)(2,1)}, u32[]{:S(2)}, u32[]{:S(2)}) collective-permute-start(bf16[1,1024,384]{2,1,0:T(8,128)(2,1)} %partner_product.4), channel_id=1, source_target_pairs={{0,4},{4,0},{8,12},{12,8},{1,5},{5,1},{9,13},{13,9},{2,6},{6,2},{1... | collective-permute-start | bytes 2359304 | tf_op jit(solution)/shard_map/ppermute | solution.py:44
  168.1 40.6 %copy-start.15 = (s32[4]{0:T(128)S(1)}, s32[4]{0:T(128)}, u32[]{:S(2)}) copy-start(s32[4]{0:T(128)} %refs_1_.12) | copy-start | bytes 52
  168.1 57.0 %collective-permute-start.19 = (bf16[4,16,128,128]{3,2,1,0:T(8,128)(2,1)}, bf16[4,16,128,128]{3,2,1,0:T(8,128)(2,1)}, u32[]{:S(2)}, u32[]{:S(2)}) collective-permute-start(bf16[4,16,128,128]{3,2,1,0:T(8,128)(2,1)} %get-tuple-element.132), channel_id=1, source_target_pairs={{0,16},{16,0},{1,17},{17,1},{2,18},{18,2},{3,19},{19,3},{4,20},{20... | collective-permute-start | bytes 6291464 | tf_op jit(solution)/shard_map/ppermute | solution.py:44
  225.1 43.6 %all-to-all-start.2 = ((bf16[4,1,4,128,256]{4,3,2,1,0:T(8,128)(2,1)}), bf16[4,1,4,128,256]{4,3,2,1,0:T(8,128)(2,1)}, u32[]{:S(2)}, u32[]{:S(2)}) async-start(bf16[4,1,4,128,256]{4,3,2,1,0:T(8,128)(2,1)} %copy-done.11), calls=%async_computation.2 | async-start | bytes 2097152 | tf_op jit(solution)/shard_map/all_to_all | solution.py:554
  229.6 24.9 %collective-permute-start.22 = (bf16[1,1,1024,128]{3,2,1,0:T(8,128)(2,1)S(1)}, bf16[1,1,1024,128]{3,2,1,0:T(8,128)(2,1)S(1)}, u32[]{:S(2)}, u32[]{:S(2)}) collective-permute-start(bf16[1,1,1024,128]{3,2,1,0:T(8,128)(2,1)S(1)} %bitcast.32), channel_id=1, source_target_pairs={{0,2},{1,3},{2,0},{3,1},{4,6},{5,7},{6,4},{7,5},{8,10},{9,11},{10,... | collective-permute-start | bytes 786440 | tf_op jit(solution)/shard_map/ppermute | solution.py:44
  231.3 1.0 copy-start.1
  239.3 1.1 copy-start.10
  245.0 10.1 %collective-permute-start.25 = (bf16[1,1,1024,128]{3,2,1,0:T(8,128)(2,1)S(1)}, bf16[1,1,1024,128]{3,2,1,0:T(8,128)(2,1)S(1)}, u32[]{:S(2)}, u32[]{:S(2)}) collective-permute-start(bf16[1,1,1024,128]{3,2,1,0:T(8,128)(2,1)S(1)} %bitcast.29), channel_id=1, source_target_pairs={{0,16},{16,0},{1,17},{17,1},{2,18},{18,2},{3,19},{19,3},{4,20},{20... | collective-permute-start | bytes 786440 | tf_op jit(solution)/shard_map/ppermute | solution.py:44
  254.6 11.7 %collective-permute-start.23 = (bf16[2,1,1024,128]{3,2,1,0:T(8,128)(2,1)S(1)}, bf16[2,1,1024,128]{3,2,1,0:T(8,128)(2,1)S(1)}, u32[]{:S(2)}, u32[]{:S(2)}) collective-permute-start(bf16[2,1,1024,128]{3,2,1,0:T(8,128)(2,1)S(1)} %pad_maximum_fusion.7), channel_id=1, source_target_pairs={{0,16},{16,0},{1,17},{17,1},{2,18},{18,2},{3,19},{19,3},{4,20},{20... | collective-permute-start | bytes 1572872 | tf_op jit(solution)/shard_map/ppermute | solution.py:44
  255.2 11.9 %collective-permute-start.26 = (bf16[1,2,1024,128]{3,2,1,0:T(8,128)(2,1)S(1)}, bf16[1,2,1024,128]{3,2,1,0:T(8,128)(2,1)S(1)}, u32[]{:S(2)}, u32[]{:S(2)}) collective-permute-start(bf16[1,2,1024,128]{3,2,1,0:T(8,128)(2,1)S(1)} %pad_maximum_fusion.8), channel_id=1, source_target_pairs={{0,2},{1,3},{2,0},{3,1},{4,6},{5,7},{6,4},{7,5},{8,10},{9,11},{10,... | collective-permute-start | bytes 1572872 | tf_op jit(solution)/shard_map/ppermute | solution.py:44
  255.7 34.0 %collective-permute-start.21 = (bf16[2,1024,384]{2,1,0:T(8,128)(2,1)}, bf16[2,1024,384]{2,1,0:T(8,128)(2,1)}, u32[]{:S(2)}, u32[]{:S(2)}) collective-permute-start(bf16[2,1024,384]{2,1,0:T(8,128)(2,1)} %partner_product.5), channel_id=1, source_target_pairs={{0,4},{4,0},{8,12},{12,8},{1,5},{5,1},{9,13},{13,9},{2,6},{6,2},{1... | collective-permute-start | bytes 4718600 | tf_op jit(solution)/shard_map/ppermute | solution.py:44
  267.1 22.5 %collective-permute-start.24 = (bf16[2,2,1024,128]{3,2,1,0:T(8,128)(2,1)}, bf16[2,2,1024,128]{3,2,1,0:T(8,128)(2,1)}, u32[]{:S(2)}, u32[]{:S(2)}) collective-permute-start(bf16[2,2,1024,128]{3,2,1,0:T(8,128)(2,1)} %constant_dynamic-update-slice_fusion.4.refs_1_), channel_id=1, source_target_pairs={{0,1},{1,0},{2,3},{3,2},{4,5},{5,4},{6,7},{7,6},{8,9},{9,8},{10,11... | collective-permute-start | bytes 3145736 | tf_op jit(solution)/shard_map/ppermute | solution.py:44
  268.2 21.4 %collective-permute-start.27 = (bf16[2,2,1024,128]{3,2,1,0:T(8,128)(2,1)}, bf16[2,2,1024,128]{3,2,1,0:T(8,128)(2,1)}, u32[]{:S(2)}, u32[]{:S(2)}) collective-permute-start(bf16[2,2,1024,128]{3,2,1,0:T(8,128)(2,1)} %pad_maximum_fusion.4.refs_3_), channel_id=1, source_target_pairs={{0,1},{1,0},{2,3},{3,2},{4,5},{5,4},{6,7},{7,6},{8,9},{9,8},{10,11... | collective-permute-start | bytes 3145736 | tf_op jit(solution)/shard_map/ppermute | solution.py:44
  289.7 4.7 %copy-start.2 = (f32[1024,128]{1,0:T(8,128)S(1)}, f32[1024,128]{1,0:T(8,128)}, u32[]{:S(2)}) copy-start(f32[1024,128]{1,0:T(8,128)} %get-tuple-element.172.refs_10_) | copy-start | bytes 1572868
  289.7 4.7 %copy-start.5 = (f32[1024,128]{1,0:T(8,128)S(1)}, f32[1024,128]{1,0:T(8,128)}, u32[]{:S(2)}) copy-start(f32[1024,128]{1,0:T(8,128)} %get-tuple-element.173.refs_11_) | copy-start | bytes 1572868
  289.7 27.1 %all-to-all-start.3 = ((bf16[4,1,4,128,256]{4,3,2,1,0:T(8,128)(2,1)}), bf16[4,1,4,128,256]{4,3,2,1,0:T(8,128)(2,1)}, u32[]{:S(2)}, u32[]{:S(2)}) async-start(bf16[4,1,4,128,256]{4,3,2,1,0:T(8,128)(2,1)} %copy-done.10), calls=%async_computation.3 | async-start | bytes 2097152 | tf_op jit(solution)/shard_map/all_to_all | solution.py:554
  316.7 51.0 %all-to-all-start.4 = ((bf16[4,2,4,128,256]{4,3,2,1,0:T(8,128)(2,1)}), bf16[4,2,4,128,256]{4,3,2,1,0:T(8,128)(2,1)S(1)}, u32[]{:S(2)}, u32[]{:S(2)}) async-start(bf16[4,2,4,128,256]{4,3,2,1,0:T(8,128)(2,1)} %get-tuple-element.195), calls=%async_computation.4 | async-start | bytes 4194304 | tf_op jit(solution)/shard_map/all_to_all | solution.py:587
  320.4 10.2 %collective-permute-start.31 = (bf16[1,1,1024,128]{3,2,1,0:T(8,128)(2,1)S(1)}, bf16[1,1,1024,128]{3,2,1,0:T(8,128)(2,1)S(1)}, u32[]{:S(2)}, u32[]{:S(2)}) collective-permute-start(bf16[1,1,1024,128]{3,2,1,0:T(8,128)(2,1)S(1)} %get-tuple-element.198), channel_id=1, source_target_pairs={{0,16},{16,0},{1,17},{17,1},{2,18},{18,2},{3,19},{19,3},{4,20},{20... | collective-permute-start | bytes 786440 | tf_op jit(solution)/shard_map/ppermute | solution.py:44
  322.0 9.3 %collective-permute-start.28 = (bf16[1,1,1024,128]{3,2,1,0:T(8,128)(2,1)S(1)}, bf16[1,1,1024,128]{3,2,1,0:T(8,128)(2,1)S(1)}, u32[]{:S(2)}, u32[]{:S(2)}) collective-permute-start(bf16[1,1,1024,128]{3,2,1,0:T(8,128)(2,1)S(1)} %get-tuple-element.199), channel_id=1, source_target_pairs={{0,2},{1,3},{2,0},{3,1},{4,6},{5,7},{6,4},{7,5},{8,10},{9,11},{10,... | collective-permute-start | bytes 786440 | tf_op jit(solution)/shard_map/ppermute | solution.py:44
  330.6 11.3 %collective-permute-start.32 = (bf16[1,2,1024,128]{3,2,1,0:T(8,128)(2,1)S(1)}, bf16[1,2,1024,128]{3,2,1,0:T(8,128)(2,1)S(1)}, u32[]{:S(2)}, u32[]{:S(2)}) collective-permute-start(bf16[1,2,1024,128]{3,2,1,0:T(8,128)(2,1)S(1)} %pad_maximum_fusion.10), channel_id=1, source_target_pairs={{0,2},{1,3},{2,0},{3,1},{4,6},{5,7},{6,4},{7,5},{8,10},{9,11},{10,... | collective-permute-start | bytes 1572872 | tf_op jit(solution)/shard_map/ppermute | solution.py:44
  331.3 11.1 %collective-permute-start.29 = (bf16[2,1,1024,128]{3,2,1,0:T(8,128)(2,1)S(1)}, bf16[2,1,1024,128]{3,2,1,0:T(8,128)(2,1)S(1)}, u32[]{:S(2)}, u32[]{:S(2)}) collective-permute-start(bf16[2,1,1024,128]{3,2,1,0:T(8,128)(2,1)S(1)} %pad_maximum_fusion.9), channel_id=1, source_target_pairs={{0,16},{16,0},{1,17},{17,1},{2,18},{18,2},{3,19},{19,3},{4,20},{20... | collective-permute-start | bytes 1572872 | tf_op jit(solution)/shard_map/ppermute | solution.py:44
  342.0 2.7 collective-permute-start.33
  342.5 23.3 %copy-start.7 = (bf16[1,1,128,4096]{3,2,1,0:T(8,128)(2,1)S(1)}, bf16[1,1,128,4096]{3,2,1,0:T(8,128)(2,1)}, u32[]{:S(2)}) copy-start(bf16[1,1,128,4096]{3,2,1,0:T(8,128)(2,1)} %param.7) | copy-start | bytes 3145732
  342.5 3.7 %collective-permute-start.30 = (bf16[2,2,1024,128]{3,2,1,0:T(8,128)(2,1)S(1)}, bf16[2,2,1024,128]{3,2,1,0:T(8,128)(2,1)S(1)}, u32[]{:S(2)}, u32[]{:S(2)}) collective-permute-start(bf16[2,2,1024,128]{3,2,1,0:T(8,128)(2,1)S(1)} %constant_dynamic-update-slice_fusion.6.refs_1_), channel_id=1, source_target_pairs={{0,1},{1,0},{2,3},{3,2},{4,5},{5,4},{6,7},{7,6},{8,9},{9,8},{10,11... | collective-permute-start | bytes 3145736 | tf_op jit(solution)/shard_map/ppermute | solution.py:44
  351.5 5.6 %collective-permute-start.34 = (bf16[128,512]{1,0:T(8,128)(2,1)S(1)}, bf16[128,512]{1,0:T(8,128)(2,1)S(1)}, u32[]{:S(2)}, u32[]{:S(2)}) collective-permute-start(bf16[128,512]{1,0:T(8,128)(2,1)S(1)} %get-tuple-element.185), channel_id=1, source_target_pairs={{0,16},{1,17},{2,18},{3,19},{16,0},{17,1},{18,2},{19,3},{4,20},{5,... | collective-permute-start | bytes 393224 | tf_op jit(solution)/shard_map/ppermute | solution.py:448
  352.1 6.4 %collective-permute-start.35 = (bf16[128,512]{1,0:T(8,128)(2,1)S(1)}, bf16[128,512]{1,0:T(8,128)(2,1)S(1)}, u32[]{:S(2)}, u32[]{:S(2)}) collective-permute-start(bf16[128,512]{1,0:T(8,128)(2,1)S(1)} %get-tuple-element.186), channel_id=1, source_target_pairs={{0,2},{1,3},{2,0},{3,1},{16,18},{17,19},{18,16},{19,17},{4,6},{5,7... | collective-permute-start | bytes 393224 | tf_op jit(solution)/shard_map/ppermute | solution.py:448
  352.8 9.4 %collective-permute-start.36 = (bf16[128,512]{1,0:T(8,128)(2,1)S(1)}, bf16[128,512]{1,0:T(8,128)(2,1)S(1)}, u32[]{:S(2)}, u32[]{:S(2)}) collective-permute-start(bf16[128,512]{1,0:T(8,128)(2,1)S(1)} %get-tuple-element.187), channel_id=1, source_target_pairs={{0,18},{1,19},{2,16},{3,17},{16,2},{17,3},{18,0},{19,1},{4,22},{5,... | collective-permute-start | bytes 393224 | tf_op jit(solution)/shard_map/ppermute | solution.py:448
  355.1 7.0 %collective-permute-start.37 = (bf16[128,512]{1,0:T(8,128)(2,1)S(1)}, bf16[128,512]{1,0:T(8,128)(2,1)S(1)}, u32[]{:S(2)}, u32[]{:S(2)}) collective-permute-start(bf16[128,512]{1,0:T(8,128)(2,1)S(1)} %get-tuple-element.188), channel_id=1, source_target_pairs={{0,1},{1,0},{2,3},{3,2},{16,17},{17,16},{18,19},{19,18},{4,5},{5,4... | collective-permute-start | bytes 393224 | tf_op jit(solution)/shard_map/ppermute | solution.py:448
  355.1 7.8 %collective-permute-start.38 = (bf16[128,512]{1,0:T(8,128)(2,1)S(1)}, bf16[128,512]{1,0:T(8,128)(2,1)S(1)}, u32[]{:S(2)}, u32[]{:S(2)}) collective-permute-start(bf16[128,512]{1,0:T(8,128)(2,1)S(1)} %get-tuple-element.189), channel_id=1, source_target_pairs={{0,17},{1,16},{2,19},{3,18},{16,1},{17,0},{18,3},{19,2},{4,21},{5,... | collective-permute-start | bytes 393224 | tf_op jit(solution)/shard_map/ppermute | solution.py:448
  357.1 5.9 %collective-permute-start.39 = (bf16[128,512]{1,0:T(8,128)(2,1)S(1)}, bf16[128,512]{1,0:T(8,128)(2,1)S(1)}, u32[]{:S(2)}, u32[]{:S(2)}) collective-permute-start(bf16[128,512]{1,0:T(8,128)(2,1)S(1)} %get-tuple-element.190), channel_id=1, source_target_pairs={{0,3},{1,2},{2,1},{3,0},{16,19},{17,18},{18,17},{19,16},{4,7},{5,6... | collective-permute-start | bytes 393224 | tf_op jit(solution)/shard_map/ppermute | solution.py:448
  358.5 7.3 %collective-permute-start.40 = (bf16[128,512]{1,0:T(8,128)(2,1)S(1)}, bf16[128,512]{1,0:T(8,128)(2,1)S(1)}, u32[]{:S(2)}, u32[]{:S(2)}) collective-permute-start(bf16[128,512]{1,0:T(8,128)(2,1)S(1)} %get-tuple-element.191), channel_id=1, source_target_pairs={{0,19},{1,18},{2,17},{3,16},{16,3},{17,2},{18,1},{19,0},{4,23},{5,... | collective-permute-start | bytes 393224 | tf_op jit(solution)/shard_map/ppermute | solution.py:448
  (3 other events, 3.0 us)

commit v3 on v2

--- a/solution.py
+++ b/solution.py
@@ -391,28 +391,30 @@
     return total.astype(BF16)
 
 
-def collect_body(*refs):
+def collect_body(count, *refs):
     head = 0
-    for piece in refs[:-1]:
+    for piece in refs[:count]:
         for j in range(piece.shape[1]):
             refs[-1][0, head, 0] = piece[0, j]
             head += 1
 
 
-def collect_call(pieces):
-    heads = sum(p.shape[1] for p in pieces)
+def collect_call(pieces, heads, first, base=None):
+    count = sum(p.shape[1] for p in pieces)
     requests = pieces[0].shape[0]
     tail = pieces[0].shape[2:]
-    return pl.pallas_call(
-        collect_body,
+    based = [] if base is None else [base]
+    return pl.pallas_call(
+        lambda *refs: collect_body(len(pieces), *refs),
         grid=(requests,),
         out_shape=jax.ShapeDtypeStruct((1, heads, requests) + tail, BF16),
-        in_specs=[by_step(p) for p in pieces],
-        out_specs=pl.BlockSpec((1, heads, 1) + tail, lambda r: (0, 0, r, 0, 0, 0)),
+        in_specs=[by_step(p) for p in pieces] + [pl.BlockSpec(memory_space=pl.ANY)] * len(based),
+        out_specs=pl.BlockSpec((1, count, 1) + tail, lambda r: (0, first // count, r, 0, 0, 0)),
+        input_output_aliases={len(pieces): 0} if based else {},
         compiler_params=params(),
         cost_estimate=cost(),
         name="collect_blocks",
-    )(*pieces)
+    )(*pieces, *based)
 
 
 def residual_body(order_d, order_h, order_t, meta, hidden, *refs):
@@ -495,8 +497,10 @@
 
     cols = out_weight.shape[2] // nt
     out_held = [out_weight]
-    for s in far:
-        out_held = out_held + hold([swap(w, "dp", s) for w in out_held], 60)
+    for s in far[:-1]:
+        out_held = out_held + [swap(w, "dp", s) for w in out_held]
+    *come, out_near = hold([swap(w, "dp", far[-1]) for w in out_held] + [swap(out_weight, "dp", 1)], 60)
+    out_held = out_held + come
     by_head = qkv_weight.reshape(local_depth, 3, nh, group, hd).transpose(2, 3, 0, 1, 4)
     by_head = by_head.reshape(nh, group, local_depth, 3 * hd)
     sizes, finishing = plan_of(group)
@@ -527,7 +531,7 @@
     cos_half, sin_half = jnp.cos(angles), jnp.sin(angles)
     cosine = jnp.concatenate([cos_half, cos_half, jnp.ones((rows, hd - ROT), F32)], axis=1)
     sine = jnp.concatenate([-sin_half, sin_half, jnp.zeros((rows, hd - ROT), F32)], axis=1)
-    live = dict(out=out_held, mine=mine, given=given[1:], own=own, pair=pair)
+    live = dict(out=out_held, near=out_near, mine=mine, given=given[1:], own=own, pair=pair)
     live["tables"] = (cosine, sine)
     live = lax.optimization_barrier(live)
 
@@ -539,42 +543,51 @@
     for stage in range(1, last_stage + 1):
         if stage <= chunks:
             held = [live["mine"][stage - 1]]
-            for s in far:
-                held = held + hold([swap(w, "dp", s) for w in held], 60)
-            weights.append(held)
+            for s in far[:-1]:
+                held = held + [swap(w, "dp", s) for w in held]
+            come = [swap(w, "dp", far[-1]) for w in held]
+            with_out = [swap(w, "dp", 1) for w in live["out"][1:]] if stage == 1 else []
+            come = hold(come + with_out, 150)
+            weights.append(held + come[: len(held)])
+            if stage == 1:
+                live["out"] = live["out"] + [live.pop("near")] + come[len(held) :]
         if stage == 1:
             live["mine"] = live["mine"] + [lax.all_to_all(g, "hg", 0, 0, tiled=True) for g in live.pop("given")]
             pair = [over_t(over_h(live["pair"][0])), over_h(over_t(live["pair"][1]))]
             live["pair"] = pair + [swap(x, "hg", h_strides[-1]) for x in pair]
-            live["out"] = live["out"] + hold([swap(w, "dp", 1) for w in live["out"]], 45)
             own = after(live["own"], tuple(live["pair"]))
             live["own"] = own + [swap(x, "hg", h_strides[-1]) for x in own]
-        for first, _, at, handover in finishing:
-            if at < handover == stage:
-                handed[first] = lax.all_to_all(live["placed"][first], "dp", 0, 0, tiled=True)
-                if stage < last_stage:
-                    (handed[first],) = hold([handed[first]], 40)
+        moved = [f for f, _, at, handover in finishing if at < handover == stage]
+        come = [lax.all_to_all(live["placed"][f], "dp", 0, 0, tiled=True) for f in moved]
+        sent = []
         for first, count, at, _ in finishing:
             c, i = places[first]
             if c + 2 == stage:
                 partial = partner_call(live["pair"], live["weights"][c], rows, i, count)
                 arrived[first] = swap(partial, "dp", 1)
-                if c + 1 == chunks:
-                    (arrived[first],) = hold([arrived[first]], 40)
+                sent.append(first)
+        if stage == chunks + 1:
+            come = hold(come + [arrived[f] for f in sent], 60)
+            arrived.update(zip(sent, come[len(moved) :]))
+        handed.update(zip(moved, come))
         if stage == 2:
             held = split_call(meta, after(live["out"], partial), order_t)
             live["out"] = [swap(w, "tp", r) if r else w for w, r in zip(held, order_t)]
         for first, count, at, _ in finishing:
             if at == stage - 1 and first not in gathered:
                 gathered[first] = [
-                    head_gather(live["ready"][first][i], h_strides, t_strides, i % 2 == 0, partial)
+                    head_gather(after(live["ready"][first], partial)[i], h_strides, t_strides, i % 2 == 0)
                     for i in range(count)
                 ]
         for first, count, at, handover in finishing:
             if at == stage:
                 c, i = places[first]
+                come = live["arrived"].get(first)
+                come = arrived[first] if come is None else come
+                if 2 < at < last_stage:
+                    come = after(come, partial)
                 query, kv, placed[first] = finish_call(
-                    meta, cached_lengths, owner_table, live["own"], live["weights"][c], arrived[first],
+                    meta, cached_lengths, owner_table, live["own"], live["weights"][c], come,
                     *live["tables"], cache_kv, i, first, cap, nd, (order_h, order_t),
                 )
                 ready[first] = attend_call(meta, cached_lengths, query, kv, cache_kv, first)
@@ -603,11 +616,16 @@
     gathered[first] = [
         head_gather(ready[first][i], h_strides, t_strides, i % 2 == 0, summed) for i in range(count)
     ]
+    collected = None
     if cols % 128 == 0:
         parts = [p for head in gathered[first] for p in head]
         pieces = output_call(meta, parts, out_weights, rows, first, group, order_h, order_t, summed, True)
         rels = [(h, t) for h in order_h for t in order_t]
         pieces = [plane_swap(p, h, t) if h or t else p for p, (h, t) in zip(pieces, rels)]
+        if 2 * count == group:
+            early = [handed[f] for f, _, _, _ in finishing[:-1]]
+            collected = collect_call(early, group, 0)
+            pieces[0] = after(pieces[0], collected)
         hidden_out = residual_call(meta, hidden_in[0, 0], pieces, offsets(all_d), order_h, order_t)
     else:
         parts = [p for f in sorted(gathered) for head in gathered[f] for p in head]
@@ -617,8 +635,11 @@
         )
         summed = summed.reshape(nh, nt, local_rows, nd, cols).transpose(2, 3, 0, 1, 4).reshape(local_rows, width)
         hidden_out = (hidden_in[0, 0].astype(F32) + summed.astype(F32)).astype(BF16)
-    handed = [handed[f] for f, _, _, _ in finishing]
-    return hidden_out[None, None], collect_call(handed)
+    if collected is not None:
+        collected = collect_call([handed[first]], group, first, collected)
+    else:
+        collected = collect_call([handed[f] for f, _, _, _ in finishing], group, 0)
+    return hidden_out[None, None], collected
 
 
 def solution(mesh):

time: 374 us -> 363 us (0.971)
  waiting for transfers between devices: 193 us -> 184 us
  starting transfers between devices: 58.3 us -> 66.4 us
  local copies, waits for them, and re-layouts: 24.5 us -> 18.7 us
  other arithmetic: 14.1 us -> 9.87 us
    ppermute x34, starting transfers between devices: 32 us -> 39.5 us  [swap(): return lax.ppermute(x, axis, [(i, i ^ stride) for i in range(size)])]
    ppermute x34, waiting for transfers between devices: 178 us -> 172 us  [swap(): return lax.ppermute(x, axis, [(i, i ^ stride) for i in range(size)])]
    unnamed x49 -> x62, local copies, waits for them, and re-layouts: 14.2 us -> 9.66 us
  transfers between devices with their start and end apart: 46 -> 46, of which waited for: 24 -> 22; matrix products, arithmetic and copies ran while one was open for 9% -> 7% of each run, Pallas kernels for 21% -> 22%
where the time goes in v3:
time: 363 us; the launch traced here: 362 us
  waiting for transfers between devices  184 us (51%)
  Pallas kernels  81.9 us (23%)
  starting transfers between devices  66.4 us (18%)
  local copies, waits for them, and re-layouts  18.7 us (5%)
  other arithmetic  9.87 us (3%)
    ppermute x34, waiting for transfers between devices, swap(): return lax.ppermute(x, axis, [(i, i ^ stride) for i in range(size)])  172 us
    ppermute x34, starting transfers between devices, swap(): return lax.ppermute(x, axis, [(i, i ^ stride) for i in range(size)])  39.5 us
    pallas_call x3, Pallas kernels, finish_call(): pl.pallas_call(lambda *refs: finish_body(len(xs), cap, *orders, *refs), o...  23.4 us
    pallas_call x3, Pallas kernels, attend_call(): pl.pallas_call(lambda *refs: attend_body(q_rows, *refs), out_shape=out, g...  17 us
    pallas_call x3, Pallas kernels, partner_call(): pl.pallas_call(lambda *refs: partner_body(len(xs), *refs), grid=(heads,),...  16.3 us
    pallas_call x2, Pallas kernels, output_call(): pl.pallas_call(lambda *refs: output_body(first, heads, group, order_h, or...  11.8 us
    unnamed x62, local copies, waits for them, and re-layouts  9.66 us
    all_to_all x2, starting transfers between devices, on_device(): lax.all_to_all(live['placed'][f], 'dp', 0, 0, tiled=True)  8.67 us
  transfers between devices with their start and end apart: 46, of which 22 were waited for; matrix products, arithmetic and copies ran while one was open for 7% of the time, Pallas kernels for 22%

profile of v3, /device:TPU:0, one launch (start us, length us, event | category | flops | bytes accessed | tf_op | source)
XLA Modules:
  0.0 361.8 jit_solution(11800495470711766464)
XLA Ops:
  0.6 4.1 %collective-permute-start = (bf16[16,128,256]{2,1,0:T(8,128)(2,1)}, bf16[16,128,256]{2,1,0:T(8,128)(2,1)}, u32[]{:S(2)}, u32[]{:S(2)}) collective-permute-start(bf16[16,128,256]{2,1,0:T(8,128)(2,1)} %refs_1_.6), channel_id=1, source_target_pairs={{0,8},{4,12},{8,0},{12,4},{1,9},{5,13},{9,1},{13,5},{2,10},{6,14},... | collective-permute-start | bytes 3145736 | tf_op jit(solution)/shard_map/ppermute | solution.py:44
  4.7 1.6 collective-permute-start.1
  6.3 4.9 %copy.21 = bf16[256,3,16,128]{0,3,1,2:T(8,128)(2,1)} copy(bf16[256,3,16,128]{3,2,1,0:T(8,128)(2,1)} %param.9) | data formatting | bytes 6291456 | tf_op args[2]
  11.2 3.3 fusion.1
  14.5 1.6 copy.26
  16.0 4.5 %all-to-all-start = ((bf16[4,2,256,384]{3,2,1,0:T(8,128)(2,1)}), bf16[4,2,256,384]{3,2,1,0:T(8,128)(2,1)}, u32[]{:S(2)}, u32[]{:S(2)}) async-start(bf16[4,2,256,384]{3,2,1,0:T(8,128)(2,1)} %copy.26), calls=%async_computation | async-start | bytes 3145728 | tf_op jit(solution)/shard_map/all_to_all | solution.py:509
  20.6 1.5 layer_norm.1
  22.2 1.6 collective-permute-start.4
  23.8 2.0 collective-permute-start.2
  27.4 3.0 fusion
  30.6 2.6 copy.25
  34.3 12.3 %collective-permute-done.2 = bf16[1,1,1,128,1024]{4,3,2,1,0:T(8,128)(2,1)S(1)} collective-permute-done((bf16[1,1,1,128,1024]{4,3,2,1,0:T(8,128)(2,1)S(1)}, bf16[1,1,1,128,1024]{4,3,2,1,0:T(8,128)(2,1)S(1)}, u32[]{:S(2)}, u32[]{:S(2)}) %collective-permute-start.2) | collective-permute-done | bytes 262176 | tf_op jit(solution)/shard_map/ppermute | solution.py:44
  46.7 1.6 collective-permute-start.3
  49.6 12.6 %collective-permute-done.6 = bf16[2,128,1024]{2,1,0:T(8,128)(2,1)} collective-permute-done((bf16[2,128,1024]{2,1,0:T(8,128)(2,1)S(1)}, bf16[2,128,1024]{2,1,0:T(8,128)(2,1)}, u32[]{:S(2)}, u32[]{:S(2)}) %collective-permute-start.6) | collective-permute-done | bytes 524320 | tf_op jit(solution)/shard_map/ppermute | solution.py:44
  63.3 2.0 pad_maximum_fusion.1.refs_4_
  67.4 1.5 collective-permute-start.9
  68.9 1.5 collective-permute-start.11
  70.5 3.8 %collective-permute-done.9 = bf16[1,1,1,128,1024]{4,3,2,1,0:T(8,128)(2,1)S(1)} collective-permute-done((bf16[1,1,1,128,1024]{4,3,2,1,0:T(8,128)(2,1)S(1)}, bf16[1,1,1,128,1024]{4,3,2,1,0:T(8,128)(2,1)S(1)}, u32[]{:S(2)}, u32[]{:S(2)}) %collective-permute-start.9) | collective-permute-done | bytes 262176 | tf_op jit(solution)/shard_map/ppermute | solution.py:44
  74.3 1.6 collective-permute-start.10
  77.5 1.7 collective-permute-start.7
  79.2 7.5 %collective-permute-done.10 = bf16[1,2,1,128,1024]{4,3,2,1,0:T(8,128)(2,1)S(1)} collective-permute-done((bf16[1,2,1,128,1024]{4,3,2,1,0:T(8,128)(2,1)S(1)}, bf16[1,2,1,128,1024]{4,3,2,1,0:T(8,128)(2,1)S(1)}, u32[]{:S(2)}, u32[]{:S(2)}) %collective-permute-start.10) | collective-permute-done | bytes 524320 | tf_op jit(solution)/shard_map/ppermute | solution.py:44
  87.6 2.0 collective-permute-start.8
  89.6 4.5 %all-to-all-start.1 = ((bf16[4,2,256,384]{3,2,1,0:T(8,128)(2,1)}), bf16[4,2,256,384]{3,2,1,0:T(8,128)(2,1)}, u32[]{:S(2)}, u32[]{:S(2)}) async-start(bf16[4,2,256,384]{3,2,1,0:T(8,128)(2,1)} %copy.25), calls=%async_computation.1 | async-start | bytes 3145728 | tf_op jit(solution)/shard_map/all_to_all | solution.py:555
  94.8 38.6 %collective-permute-done.8.refs_1_ = bf16[16,128,256]{2,1,0:T(8,128)(2,1)} collective-permute-done((bf16[16,128,256]{2,1,0:T(8,128)(2,1)}, bf16[16,128,256]{2,1,0:T(8,128)(2,1)}, u32[]{:S(2)}, u32[]{:S(2)}) %collective-permute-start.8) | collective-permute-done | bytes 1048608 | tf_op jit(solution)/shard_map/ppermute | solution.py:44
  133.4 12.5 %collective-permute-done.7.refs_0_ = bf16[4,2,256,384]{3,2,1,0:T(8,128)(2,1)} collective-permute-done((bf16[4,2,256,384]{3,2,1,0:T(8,128)(2,1)}, bf16[4,2,256,384]{3,2,1,0:T(8,128)(2,1)}, u32[]{:S(2)}, u32[]{:S(2)}) %collective-permute-start.7) | collective-permute-done | bytes 1572896 | tf_op jit(solution)/shard_map/ppermute | solution.py:44
  145.9 1.6 collective-permute-start.20
  147.5 4.0 %partner_product.3 = bf16[1,1024,384]{2,1,0:T(8,128)(2,1)S(1)} custom-call(bf16[1,2,2,128,1024]{4,3,2,1,0:T(8,128)(2,1)S(1)} %pad_maximum_fusion.2.refs_0_, bf16[1,2,2,128,1024]{4,3,2,1,0:T(8,128)(2,1)S(1)} %pad_maximum_fusion.3.refs_1_, bf16[1,2,2,128,1024]{4,3,2,1,0:T(8,128)(2,1)S(1)} %collective-permute-done.13.refs_2_, ...), custom_call_target="tpu_custom_call" | custom-call | flops 1 | bytes 1 | tf_op jit(solution)/shard_map/partner_product/pallas_call | solution.py:145
  151.5 2.5 collective-permute-start.17
  154.1 4.9 %partner_product.4 = bf16[1,1024,384]{2,1,0:T(8,128)(2,1)} custom-call(bf16[1,2,2,128,1024]{4,3,2,1,0:T(8,128)(2,1)S(1)} %pad_maximum_fusion.2.refs_0_, bf16[1,2,2,128,1024]{4,3,2,1,0:T(8,128)(2,1)S(1)} %pad_maximum_fusion.3.refs_1_, bf16[1,2,2,128,1024]{4,3,2,1,0:T(8,128)(2,1)S(1)} %collective-permute-done.13.refs_2_, ...), custom_call_target="tpu_custom_call" | custom-call | flops 1 | bytes 1 | tf_op jit(solution)/shard_map/partner_product/pallas_call | solution.py:145
  159.2 4.4 %split_columns.1 = (bf16[4,16,128,128]{3,2,1,0:T(8,128)(2,1)}, bf16[4,16,128,128]{3,2,1,0:T(8,128)(2,1)}) custom-call(s32[4]{0:T(128)S(1)} %copy-done.19, bf16[16,128,256]{2,1,0:T(8,128)(2,1)S(1)} %copy-done.13, bf16[16,128,256]{2,1,0:T(8,128)(2,1)} %get-tuple-element.138.refs_2_, bf16[16,128,256]{2,1,0:T(8,128)(2,1)S(1)} %copy-done.15, ...), custom_call_target="tpu_custom_call" | custom-call | flops 1 | bytes 1 | tf_op jit(solution)/shard_map/split_columns/pallas_call | solution.py:320
  164.7 34.7 %collective-permute-done.17.refs_9_ = bf16[1,1024,384]{2,1,0:T(8,128)(2,1)S(1)} collective-permute-done((bf16[1,1024,384]{2,1,0:T(8,128)(2,1)S(1)}, bf16[1,1024,384]{2,1,0:T(8,128)(2,1)S(1)}, u32[]{:S(2)}, u32[]{:S(2)}) %collective-permute-start.17) | collective-permute-done | bytes 786464 | tf_op jit(solution)/shard_map/ppermute | solution.py:44
  199.4 6.3 %finish_projection.3 = (bf16[1,1024,128]{2,1,0:T(8,128)(2,1)S(1)}, bf16[1,1024,256]{2,1,0:T(8,128)(2,1)S(1)}, bf16[4,1,4,128,256]{4,3,2,1,0:T(8,128)(2,1)S(1)}) custom-call(s32[4]{0:T(128)S(1)} %copy-done.19, s32[4]{0:T(128)S(1)} %copy-done.22, s32[4,16]{1,0:T(4,128)S(1)} %copy-done.24, bf16[1,2,2,128,1024]{4,3,2,1,0:T(8,128)(2,1)} %pad_maximum_fusion.refs_3_, ...), custom_call_target="tpu_custom_call" | custom-call | flops 1 | bytes 1 | tf_op jit(solution)/shard_map/finish_projection/pallas_call | solution.py:236
  205.8 4.6 %attention.3 = bf16[1,1024,128]{2,1,0:T(8,128)(2,1)S(1)} custom-call(s32[4]{0:T(128)S(1)} %copy-done.19, s32[4]{0:T(128)S(1)} %copy-done.22, bf16[1,1024,128]{2,1,0:T(8,128)(2,1)S(1)} %get-tuple-element.150.refs_2_, bf16[1,1024,256]{2,1,0:T(8,128)(2,1)S(1)} %get-tuple-element.151.refs_3_, bf16[1,16,1024,256]{3,2,1,0:T(8,128)(2,1)} %refs_4_.5), custom_call_target="tpu_custom_call" | custom-call | flops 1 | bytes 1 | tf_op jit(solution)/shard_map/attention/pallas_call | solution.py:289
  210.4 5.3 %collective-permute-done.20.refs_0_ = bf16[4,2,256,384]{3,2,1,0:T(8,128)(2,1)} collective-permute-done((bf16[4,2,256,384]{3,2,1,0:T(8,128)(2,1)}, bf16[4,2,256,384]{3,2,1,0:T(8,128)(2,1)}, u32[]{:S(2)}, u32[]{:S(2)}) %collective-permute-start.20) | collective-permute-done | bytes 1572896 | tf_op jit(solution)/shard_map/ppermute | solution.py:44
  215.7 4.0 %collective-permute-done.18.refs_9_ = bf16[1,1024,384]{2,1,0:T(8,128)(2,1)} collective-permute-done((bf16[1,1024,384]{2,1,0:T(8,128)(2,1)}, bf16[1,1024,384]{2,1,0:T(8,128)(2,1)}, u32[]{:S(2)}, u32[]{:S(2)}) %collective-permute-start.18) | collective-permute-done | bytes 786464 | tf_op jit(solution)/shard_map/ppermute | solution.py:44
  219.7 4.8 %all-to-all-start.2 = ((bf16[4,1,4,128,256]{4,3,2,1,0:T(8,128)(2,1)}), bf16[4,1,4,128,256]{4,3,2,1,0:T(8,128)(2,1)}, u32[]{:S(2)}, u32[]{:S(2)}) async-start(bf16[4,1,4,128,256]{4,3,2,1,0:T(8,128)(2,1)} %copy-done.17), calls=%async_computation.2 | async-start | bytes 2097152 | tf_op jit(solution)/shard_map/all_to_all | solution.py:561
  224.5 7.4 %partner_product.5 = bf16[2,1024,384]{2,1,0:T(8,128)(2,1)} custom-call(bf16[1,2,2,128,1024]{4,3,2,1,0:T(8,128)(2,1)S(1)} %pad_maximum_fusion.2.refs_0_, bf16[1,2,2,128,1024]{4,3,2,1,0:T(8,128)(2,1)S(1)} %pad_maximum_fusion.3.refs_1_, bf16[1,2,2,128,1024]{4,3,2,1,0:T(8,128)(2,1)S(1)} %collective-permute-done.13.refs_2_, ...), custom_call_target="tpu_custom_call" | custom-call | flops 1 | bytes 1 | tf_op jit(solution)/shard_map/partner_product/pallas_call | solution.py:145
  231.9 2.0 collective-permute-start.21
  233.9 2.2 collective-permute-start.22
  236.1 6.4 %finish_projection.4 = (bf16[1,1024,128]{2,1,0:T(8,128)(2,1)S(1)}, bf16[1,1024,256]{2,1,0:T(8,128)(2,1)S(1)}, bf16[4,1,4,128,256]{4,3,2,1,0:T(8,128)(2,1)S(1)}) custom-call(s32[4]{0:T(128)S(1)} %copy-done.20, s32[4]{0:T(128)S(1)} %copy-done.23, s32[4,16]{1,0:T(4,128)S(1)} %copy-done.25, bf16[1,2,2,128,1024]{4,3,2,1,0:T(8,128)(2,1)} %pad_maximum_fusion.refs_3_, ...), custom_call_target="tpu_custom_call" | custom-call | flops 1 | bytes 1 | tf_op jit(solution)/shard_map/finish_projection/pallas_call | solution.py:236
  242.6 4.6 %attention.4 = bf16[1,1024,128]{2,1,0:T(8,128)(2,1)S(1)} custom-call(s32[4]{0:T(128)S(1)} %copy-done.20, s32[4]{0:T(128)S(1)} %copy-done.23, bf16[1,1024,128]{2,1,0:T(8,128)(2,1)S(1)} %get-tuple-element.172.refs_2_, bf16[1,1024,256]{2,1,0:T(8,128)(2,1)S(1)} %get-tuple-element.173.refs_3_, bf16[1,16,1024,256]{3,2,1,0:T(8,128)(2,1)} %refs_4_.5), custom_call_target="tpu_custom_call" | custom-call | flops 1 | bytes 1 | tf_op jit(solution)/shard_map/attention/pallas_call | solution.py:289
  247.4 2.1 collective-permute-start.23
  249.5 7.1 %collective-permute-done.25 = bf16[1,1,1024,128]{3,2,1,0:T(8,128)(2,1)S(1)} collective-permute-done((bf16[1,1,1024,128]{3,2,1,0:T(8,128)(2,1)S(1)}, bf16[1,1,1024,128]{3,2,1,0:T(8,128)(2,1)S(1)}, u32[]{:S(2)}, u32[]{:S(2)}) %collective-permute-start.25) | collective-permute-done | bytes 262176 | tf_op jit(solution)/shard_map/ppermute | solution.py:44
  256.7 8.0 %collective-permute-done.23 = bf16[2,1,1024,128]{3,2,1,0:T(8,128)(2,1)S(1)} collective-permute-done((bf16[2,1,1024,128]{3,2,1,0:T(8,128)(2,1)S(1)}, bf16[2,1,1024,128]{3,2,1,0:T(8,128)(2,1)S(1)}, u32[]{:S(2)}, u32[]{:S(2)}) %collective-permute-start.23) | collective-permute-done | bytes 524320 | tf_op jit(solution)/shard_map/ppermute | solution.py:44
  266.1 10.4 %collective-permute-done.21.refs_1_ = bf16[2,1024,384]{2,1,0:T(8,128)(2,1)} collective-permute-done((bf16[2,1024,384]{2,1,0:T(8,128)(2,1)}, bf16[2,1024,384]{2,1,0:T(8,128)(2,1)}, u32[]{:S(2)}, u32[]{:S(2)}) %collective-permute-start.21) | collective-permute-done | bytes 1572896 | tf_op jit(solution)/shard_map/ppermute | solution.py:44
  276.5 3.9 %all-to-all-start.3 = ((bf16[4,1,4,128,256]{4,3,2,1,0:T(8,128)(2,1)}), bf16[4,1,4,128,256]{4,3,2,1,0:T(8,128)(2,1)S(1)}, u32[]{:S(2)}, u32[]{:S(2)}) async-start(bf16[4,1,4,128,256]{4,3,2,1,0:T(8,128)(2,1)} %copy-done.16), calls=%async_computation.3 | async-start | bytes 2097152 | tf_op jit(solution)/shard_map/all_to_all | solution.py:561
  280.4 10.7 %finish_projection.5 = (bf16[2,1024,128]{2,1,0:T(8,128)(2,1)S(1)}, bf16[2,1024,256]{2,1,0:T(8,128)(2,1)S(1)}, bf16[4,2,4,128,256]{4,3,2,1,0:T(8,128)(2,1)}) custom-call(s32[4]{0:T(128)S(1)} %copy-done.20, s32[4]{0:T(128)S(1)} %copy-done.23, s32[4,16]{1,0:T(4,128)S(1)} %copy-done.25, bf16[1,2,2,128,1024]{4,3,2,1,0:T(8,128)(2,1)} %pad_maximum_fusion.refs_3_, ...), custom_call_target="tpu_custom_call" | custom-call | flops 1 | bytes 1 | tf_op jit(solution)/shard_map/finish_projection/pallas_call | solution.py:236
  291.1 7.8 %attention.5 = bf16[2,1024,128]{2,1,0:T(8,128)(2,1)S(1)} custom-call(s32[4]{0:T(128)S(1)} %copy-done.20, s32[4]{0:T(128)S(1)} %copy-done.23, bf16[2,1024,128]{2,1,0:T(8,128)(2,1)S(1)} %get-tuple-element.187.refs_2_, bf16[2,1024,256]{2,1,0:T(8,128)(2,1)S(1)} %get-tuple-element.188.refs_3_, bf16[1,16,1024,256]{3,2,1,0:T(8,128)(2,1)} %refs_4_.5), custom_call_target="tpu_custom_call" | custom-call | flops 1 | bytes 1 | tf_op jit(solution)/shard_map/attention/pallas_call | solution.py:289
  299.7 5.3 %all-to-all-done.3.refs_1_ = bf16[4,1,4,128,256]{4,3,2,1,0:T(8,128)(2,1)S(1)} async-done(((bf16[4,1,4,128,256]{4,3,2,1,0:T(8,128)(2,1)}), bf16[4,1,4,128,256]{4,3,2,1,0:T(8,128)(2,1)S(1)}, u32[]{:S(2)}, u32[]{:S(2)}) %all-to-all-start.3) | async-done | bytes 1048608 | tf_op jit(solution)/shard_map/all_to_all | solution.py:561
  305.0 3.6 all-to-all-start.4
  310.0 2.6 collective-permute-start.28
  313.9 6.5 %output_projection.2.refs_7_ = f32[1024,512]{1,0:T(8,128)} custom-call(s32[4]{0:T(128)S(1)} %copy-done.20, bf16[2,2,1024,128]{3,2,1,0:T(8,128)(2,1)S(1)} %copy-done.9, bf16[2,2,1024,128]{3,2,1,0:T(8,128)(2,1)} %collective-permute-done.24.refs_2_, bf16[2,2,1024,128]{3,2,1,0:T(8,128)(2,1)S(1)} %copy-done.11, ...), custom_call_target="tpu_custom_call" | custom-call | flops 1 | bytes 1 | tf_op jit(solution)/shard_map/output_projection/pallas_call | solution.py:367
  320.7 2.0 collective-permute-start.29
  322.7 10.4 %collective-permute-done.32 = bf16[1,2,1024,128]{3,2,1,0:T(8,128)(2,1)S(1)} collective-permute-done((bf16[1,2,1024,128]{3,2,1,0:T(8,128)(2,1)S(1)}, bf16[1,2,1024,128]{3,2,1,0:T(8,128)(2,1)S(1)}, u32[]{:S(2)}, u32[]{:S(2)}) %collective-permute-start.32) | collective-permute-done | bytes 524320 | tf_op jit(solution)/shard_map/ppermute | solution.py:44
  334.0 2.0 collective-permute-done.33.refs_4_
  336.0 1.5 collective-permute-done.30.refs_2_
  337.5 5.3 %output_projection.3 = (bf16[128,512]{1,0:T(8,128)(2,1)S(1)}, bf16[128,512]{1,0:T(8,128)(2,1)S(1)}, bf16[128,512]{1,0:T(8,128)(2,1)S(1)}, bf16[128,512]{1,0:T(8,...) custom-call(s32[4]{0:T(128)S(1)} %copy-done.20, ...), custom_call_target="tpu_custom_call" | custom-call | flops 1 | bytes 1 | tf_op jit(solution)/shard_map/output_projection/pallas_call | solution.py:367
  342.8 1.7 collective-permute-start.34
  346.3 1.8 collective-permute-start.38
  348.4 2.5 collective-permute-done.35.refs_4_
  351.2 3.6 collect_blocks.2.refs_1_
  354.8 3.2 collective-permute-done.40.refs_9_
  358.0 2.0 residual.1
  360.0 1.8 collect_blocks.3
  (141 shorter events, 20.8 us)
Async XLA Ops:
  0.6 65.8 %collective-permute-start = (bf16[16,128,256]{2,1,0:T(8,128)(2,1)}, bf16[16,128,256]{2,1,0:T(8,128)(2,1)}, u32[]{:S(2)}, u32[]{:S(2)}) collective-permute-start(bf16[16,128,256]{2,1,0:T(8,128)(2,1)} %refs_1_.6), channel_id=1, source_target_pairs={{0,8},{4,12},{8,0},{12,4},{1,9},{5,13},{9,1},{13,5},{2,10},{6,14},... | collective-permute-start | bytes 3145736 | tf_op jit(solution)/shard_map/ppermute | solution.py:44
  4.7 61.7 %collective-permute-start.1 = (bf16[16,128,256]{2,1,0:T(8,128)(2,1)}, bf16[16,128,256]{2,1,0:T(8,128)(2,1)S(1)}, u32[]{:S(2)}, u32[]{:S(2)}) collective-permute-start(bf16[16,128,256]{2,1,0:T(8,128)(2,1)} %refs_1_.6), channel_id=1, source_target_pairs={{0,4},{4,0},{8,12},{12,8},{1,5},{5,1},{9,13},{13,9},{2,6},{6,2},{1... | collective-permute-start | bytes 3145736 | tf_op jit(solution)/shard_map/ppermute | solution.py:44
  16.0 51.4 %all-to-all-start = ((bf16[4,2,256,384]{3,2,1,0:T(8,128)(2,1)}), bf16[4,2,256,384]{3,2,1,0:T(8,128)(2,1)}, u32[]{:S(2)}, u32[]{:S(2)}) async-start(bf16[4,2,256,384]{3,2,1,0:T(8,128)(2,1)} %copy.26), calls=%async_computation | async-start | bytes 3145728 | tf_op jit(solution)/shard_map/all_to_all | solution.py:509
  20.5 5.7 %copy-start.21 = (s32[4]{0:T(128)S(1)}, s32[4]{0:T(128)}, u32[]{:S(2)}) copy-start(s32[4]{0:T(128)} %refs_1_.12) | copy-start | bytes 52
  22.2 11.0 %collective-permute-start.4 = (bf16[1,1,1,128,1024]{4,3,2,1,0:T(8,128)(2,1)S(1)}, bf16[1,1,1,128,1024]{4,3,2,1,0:T(8,128)(2,1)}, u32[]{:S(2)}, u32[]{:S(2)}) collective-permute-start(bf16[1,1,1,128,1024]{4,3,2,1,0:T(8,128)(2,1)S(1)} %get-tuple-element.216), channel_id=1, source_target_pairs={{0,16},{16,0},{1,17},{17,1},{2,18},{18,2},{3,19},{19,3},{4,20},{20... | collective-permute-start | bytes 786440 | tf_op jit(solution)/shard_map/ppermute | solution.py:44
  23.8 22.9 %collective-permute-start.2 = (bf16[1,1,1,128,1024]{4,3,2,1,0:T(8,128)(2,1)S(1)}, bf16[1,1,1,128,1024]{4,3,2,1,0:T(8,128)(2,1)S(1)}, u32[]{:S(2)}, u32[]{:S(2)}) collective-permute-start(bf16[1,1,1,128,1024]{4,3,2,1,0:T(8,128)(2,1)S(1)} %get-tuple-element.217), channel_id=1, source_target_pairs={{0,2},{1,3},{2,0},{3,1},{4,6},{5,7},{6,4},{7,5},{8,10},{9,11},{10,... | collective-permute-start | bytes 786440 | tf_op jit(solution)/shard_map/ppermute | solution.py:44
  25.7 36.5 %collective-permute-start.6 = (bf16[2,128,1024]{2,1,0:T(8,128)(2,1)S(1)}, bf16[2,128,1024]{2,1,0:T(8,128)(2,1)}, u32[]{:S(2)}, u32[]{:S(2)}) collective-permute-start(bf16[2,128,1024]{2,1,0:T(8,128)(2,1)S(1)} %get-tuple-element.110), channel_id=1, source_target_pairs={{0,4},{4,0},{8,12},{12,8},{1,5},{5,1},{9,13},{13,9},{2,6},{6,2},{1... | collective-permute-start | bytes 1572872 | tf_op jit(solution)/shard_map/ppermute | solution.py:44
  33.1 15.1 %copy-start.27 = (f32[1024,16]{1,0:T(8,128)S(1)}, f32[1024,16]{1,0:T(8,128)}, u32[]{:S(2)}) copy-start(f32[1024,16]{1,0:T(8,128)} %get-tuple-element.220) | copy-start | bytes 196612
  34.2 29.1 %collective-permute-start.5 = (bf16[1,1,2,128,1024]{4,3,2,1,0:T(8,128)(2,1)S(1)}, bf16[1,1,2,128,1024]{4,3,2,1,0:T(8,128)(2,1)S(1)}, u32[]{:S(2)}, u32[]{:S(2)}) collective-permute-start(bf16[1,1,2,128,1024]{4,3,2,1,0:T(8,128)(2,1)S(1)} %pad_maximum_fusion.7), channel_id=1, source_target_pairs={{0,2},{1,3},{2,0},{3,1},{4,6},{5,7},{6,4},{7,5},{8,10},{9,11},{10,... | collective-permute-start | bytes 1572872 | tf_op jit(solution)/shard_map/ppermute | solution.py:44
  46.7 18.6 %collective-permute-start.3 = (bf16[1,2,1,128,1024]{4,3,2,1,0:T(8,128)(2,1)S(1)}, bf16[1,2,1,128,1024]{4,3,2,1,0:T(8,128)(2,1)S(1)}, u32[]{:S(2)}, u32[]{:S(2)}) collective-permute-start(bf16[1,2,1,128,1024]{4,3,2,1,0:T(8,128)(2,1)S(1)} %pad_maximum_fusion.6), channel_id=1, source_target_pairs={{0,16},{16,0},{1,17},{17,1},{2,18},{18,2},{3,19},{19,3},{4,20},{20... | collective-permute-start | bytes 1572872 | tf_op jit(solution)/shard_map/ppermute | solution.py:44
  67.4 6.9 %collective-permute-start.9 = (bf16[1,1,1,128,1024]{4,3,2,1,0:T(8,128)(2,1)S(1)}, bf16[1,1,1,128,1024]{4,3,2,1,0:T(8,128)(2,1)S(1)}, u32[]{:S(2)}, u32[]{:S(2)}) collective-permute-start(bf16[1,1,1,128,1024]{4,3,2,1,0:T(8,128)(2,1)S(1)} %get-tuple-element.119), channel_id=1, source_target_pairs={{0,2},{1,3},{2,0},{3,1},{4,6},{5,7},{6,4},{7,5},{8,10},{9,11},{10,... | collective-permute-start | bytes 786440 | tf_op jit(solution)/shard_map/ppermute | solution.py:44
  68.9 7.4 %collective-permute-start.11 = (bf16[1,1,1,128,1024]{4,3,2,1,0:T(8,128)(2,1)S(1)}, bf16[1,1,1,128,1024]{4,3,2,1,0:T(8,128)(2,1)S(1)}, u32[]{:S(2)}, u32[]{:S(2)}) collective-permute-start(bf16[1,1,1,128,1024]{4,3,2,1,0:T(8,128)(2,1)S(1)} %get-tuple-element.120), channel_id=1, source_target_pairs={{0,16},{16,0},{1,17},{17,1},{2,18},{18,2},{3,19},{19,3},{4,20},{20... | collective-permute-start | bytes 786440 | tf_op jit(solution)/shard_map/ppermute | solution.py:44
  74.3 12.5 %collective-permute-start.10 = (bf16[1,2,1,128,1024]{4,3,2,1,0:T(8,128)(2,1)S(1)}, bf16[1,2,1,128,1024]{4,3,2,1,0:T(8,128)(2,1)S(1)}, u32[]{:S(2)}, u32[]{:S(2)}) collective-permute-start(bf16[1,2,1,128,1024]{4,3,2,1,0:T(8,128)(2,1)S(1)} %constant_dynamic-update-slice_fusion), channel_id=1, source_target_pairs={{0,16},{16,0},{1,17},{17,1},{2,18},{18,2},{3,19},{19,3},{4,20},{20... | collective-permute-start | bytes 1572872 | tf_op jit(solution)/shard_map/ppermute | solution.py:44
  76.3 11.0 %collective-permute-start.12 = (bf16[1,1,2,128,1024]{4,3,2,1,0:T(8,128)(2,1)S(1)}, bf16[1,1,2,128,1024]{4,3,2,1,0:T(8,128)(2,1)S(1)}, u32[]{:S(2)}, u32[]{:S(2)}) collective-permute-start(bf16[1,1,2,128,1024]{4,3,2,1,0:T(8,128)(2,1)S(1)} %constant_dynamic-update-slice_fusion.2), channel_id=1, source_target_pairs={{0,2},{1,3},{2,0},{3,1},{4,6},{5,7},{6,4},{7,5},{8,10},{9,11},{10,... | collective-permute-start | bytes 1572872 | tf_op jit(solution)/shard_map/ppermute | solution.py:44
  77.5 68.4 %collective-permute-start.7 = (bf16[4,2,256,384]{3,2,1,0:T(8,128)(2,1)}, bf16[4,2,256,384]{3,2,1,0:T(8,128)(2,1)}, u32[]{:S(2)}, u32[]{:S(2)}) collective-permute-start(bf16[4,2,256,384]{3,2,1,0:T(8,128)(2,1)} %all-to-all-done.refs_4_.refs_7_), channel_id=1, source_target_pairs={{0,8},{4,12},{8,0},{12,4},{1,9},{5,13},{9,1},{13,5},{2,10},{6,14},... | collective-permute-start | bytes 4718600 | tf_op jit(solution)/shard_map/ppermute | solution.py:44
  86.8 7.3 %collective-permute-start.13 = (bf16[1,2,2,128,1024]{4,3,2,1,0:T(8,128)(2,1)S(1)}, bf16[1,2,2,128,1024]{4,3,2,1,0:T(8,128)(2,1)S(1)}, u32[]{:S(2)}, u32[]{:S(2)}) collective-permute-start(bf16[1,2,2,128,1024]{4,3,2,1,0:T(8,128)(2,1)S(1)} %pad_maximum_fusion.2.refs_0_), channel_id=1, source_target_pairs={{0,1},{1,0},{2,3},{3,2},{4,5},{5,4},{6,7},{7,6},{8,9},{9,8},{10,11... | collective-permute-start | bytes 3145736 | tf_op jit(solution)/shard_map/ppermute | solution.py:44
  87.4 6.8 %collective-permute-start.14 = (bf16[1,2,2,128,1024]{4,3,2,1,0:T(8,128)(2,1)S(1)}, bf16[1,2,2,128,1024]{4,3,2,1,0:T(8,128)(2,1)}, u32[]{:S(2)}, u32[]{:S(2)}) collective-permute-start(bf16[1,2,2,128,1024]{4,3,2,1,0:T(8,128)(2,1)S(1)} %pad_maximum_fusion.3.refs_1_), channel_id=1, source_target_pairs={{0,1},{1,0},{2,3},{3,2},{4,5},{5,4},{6,7},{7,6},{8,9},{9,8},{10,11... | collective-permute-start | bytes 3145736 | tf_op jit(solution)/shard_map/ppermute | solution.py:44
  87.6 45.8 %collective-permute-start.8 = (bf16[16,128,256]{2,1,0:T(8,128)(2,1)}, bf16[16,128,256]{2,1,0:T(8,128)(2,1)}, u32[]{:S(2)}, u32[]{:S(2)}) collective-permute-start(bf16[16,128,256]{2,1,0:T(8,128)(2,1)} %get-tuple-element.138.refs_2_), channel_id=1, source_target_pairs={{0,4},{4,0},{8,12},{12,8},{1,5},{5,1},{9,13},{13,9},{2,6},{6,2},{1... | collective-permute-start | bytes 3145736 | tf_op jit(solution)/shard_map/ppermute | solution.py:44
  89.6 56.3 %all-to-all-start.1 = ((bf16[4,2,256,384]{3,2,1,0:T(8,128)(2,1)}), bf16[4,2,256,384]{3,2,1,0:T(8,128)(2,1)}, u32[]{:S(2)}, u32[]{:S(2)}) async-start(bf16[4,2,256,384]{3,2,1,0:T(8,128)(2,1)} %copy.25), calls=%async_computation.1 | async-start | bytes 3145728 | tf_op jit(solution)/shard_map/all_to_all | solution.py:555
  94.2 51.7 %collective-permute-start.15 = (bf16[1,2,2,128,1024]{4,3,2,1,0:T(8,128)(2,1)}, bf16[1,2,2,128,1024]{4,3,2,1,0:T(8,128)(2,1)}, u32[]{:S(2)}, u32[]{:S(2)}) collective-permute-start(bf16[1,2,2,128,1024]{4,3,2,1,0:T(8,128)(2,1)} %pad_maximum_fusion.refs_3_), channel_id=1, source_target_pairs={{0,1},{1,0},{2,3},{3,2},{4,5},{5,4},{6,7},{7,6},{8,9},{9,8},{10,11... | collective-permute-start | bytes 3145736 | tf_op jit(solution)/shard_map/ppermute | solution.py:44
  94.5 51.4 %collective-permute-start.16 = (bf16[1,2,2,128,1024]{4,3,2,1,0:T(8,128)(2,1)}, bf16[1,2,2,128,1024]{4,3,2,1,0:T(8,128)(2,1)}, u32[]{:S(2)}, u32[]{:S(2)}) collective-permute-start(bf16[1,2,2,128,1024]{4,3,2,1,0:T(8,128)(2,1)} %pad_maximum_fusion.1.refs_4_), channel_id=1, source_target_pairs={{0,1},{1,0},{2,3},{3,2},{4,5},{5,4},{6,7},{7,6},{8,9},{9,8},{10,11... | collective-permute-start | bytes 3145736 | tf_op jit(solution)/shard_map/ppermute | solution.py:44
  145.9 69.8 %collective-permute-start.20 = (bf16[4,2,256,384]{3,2,1,0:T(8,128)(2,1)}, bf16[4,2,256,384]{3,2,1,0:T(8,128)(2,1)}, u32[]{:S(2)}, u32[]{:S(2)}) collective-permute-start(bf16[4,2,256,384]{3,2,1,0:T(8,128)(2,1)} %all-to-all-done.1.refs_4_.refs_7_), channel_id=1, source_target_pairs={{0,8},{4,12},{8,0},{12,4},{1,9},{5,13},{9,1},{13,5},{2,10},{6,14},... | collective-permute-start | bytes 4718600 | tf_op jit(solution)/shard_map/ppermute | solution.py:44
  151.5 7.7 %copy-start.13 = (bf16[16,128,256]{2,1,0:T(8,128)(2,1)S(1)}, bf16[16,128,256]{2,1,0:T(8,128)(2,1)}, u32[]{:S(2)}) copy-start(bf16[16,128,256]{2,1,0:T(8,128)(2,1)} %refs_1_.6) | copy-start | bytes 3145732
  151.5 7.7 %copy-start.15 = (bf16[16,128,256]{2,1,0:T(8,128)(2,1)S(1)}, bf16[16,128,256]{2,1,0:T(8,128)(2,1)}, u32[]{:S(2)}) copy-start(bf16[16,128,256]{2,1,0:T(8,128)(2,1)} %get-tuple-element.139.refs_3_) | copy-start | bytes 3145732
  151.5 7.7 %copy-start.19 = (s32[4]{0:T(128)S(1)}, s32[4]{0:T(128)}, u32[]{:S(2)}) copy-start(s32[4]{0:T(128)} %copy-done.18) | copy-start | bytes 52
  151.5 47.9 %collective-permute-start.17 = (bf16[1,1024,384]{2,1,0:T(8,128)(2,1)S(1)}, bf16[1,1024,384]{2,1,0:T(8,128)(2,1)S(1)}, u32[]{:S(2)}, u32[]{:S(2)}) collective-permute-start(bf16[1,1024,384]{2,1,0:T(8,128)(2,1)S(1)} %partner_product.3), channel_id=1, source_target_pairs={{0,4},{4,0},{8,12},{12,8},{1,5},{5,1},{9,13},{13,9},{2,6},{6,2},{1... | collective-permute-start | bytes 2359304 | tf_op jit(solution)/shard_map/ppermute | solution.py:44
  159.0 40.5 %copy-start = (f32[1024,128]{1,0:T(8,128)S(1)}, f32[1024,128]{1,0:T(8,128)}, u32[]{:S(2)}) copy-start(f32[1024,128]{1,0:T(8,128)} %get-tuple-element.185.refs_10_) | copy-start | bytes 1572868
  159.0 40.5 %copy-start.3 = (f32[1024,128]{1,0:T(8,128)S(1)}, f32[1024,128]{1,0:T(8,128)}, u32[]{:S(2)}) copy-start(f32[1024,128]{1,0:T(8,128)} %get-tuple-element.186.refs_11_) | copy-start | bytes 1572868
  159.0 40.5 %copy-start.22 = (s32[4]{0:T(128)S(1)}, s32[4]{0:T(128)}, u32[]{:S(2)}) copy-start(s32[4]{0:T(128)} %refs_1_.12) | copy-start | bytes 52
  159.0 40.5 %copy-start.24 = (s32[4,16]{1,0:T(4,128)S(1)}, s32[4,16]{1,0:T(4,128)}, u32[]{:S(2)}) copy-start(s32[4,16]{1,0:T(4,128)} %refs_2_.5) | copy-start | bytes 772
  159.0 60.7 %collective-permute-start.18 = (bf16[1,1024,384]{2,1,0:T(8,128)(2,1)}, bf16[1,1024,384]{2,1,0:T(8,128)(2,1)}, u32[]{:S(2)}, u32[]{:S(2)}) collective-permute-start(bf16[1,1024,384]{2,1,0:T(8,128)(2,1)} %partner_product.4), channel_id=1, source_target_pairs={{0,4},{4,0},{8,12},{12,8},{1,5},{5,1},{9,13},{13,9},{2,6},{6,2},{1... | collective-permute-start | bytes 2359304 | tf_op jit(solution)/shard_map/ppermute | solution.py:44
  163.6 56.1 %collective-permute-start.19 = (bf16[4,16,128,128]{3,2,1,0:T(8,128)(2,1)}, bf16[4,16,128,128]{3,2,1,0:T(8,128)(2,1)}, u32[]{:S(2)}, u32[]{:S(2)}) collective-permute-start(bf16[4,16,128,128]{3,2,1,0:T(8,128)(2,1)} %get-tuple-element.142), channel_id=1, source_target_pairs={{0,16},{16,0},{1,17},{17,1},{2,18},{18,2},{3,19},{19,3},{4,20},{20... | collective-permute-start | bytes 6291464 | tf_op jit(solution)/shard_map/ppermute | solution.py:44
  219.7 46.3 %all-to-all-start.2 = ((bf16[4,1,4,128,256]{4,3,2,1,0:T(8,128)(2,1)}), bf16[4,1,4,128,256]{4,3,2,1,0:T(8,128)(2,1)}, u32[]{:S(2)}, u32[]{:S(2)}) async-start(bf16[4,1,4,128,256]{4,3,2,1,0:T(8,128)(2,1)} %copy-done.17), calls=%async_computation.2 | async-start | bytes 2097152 | tf_op jit(solution)/shard_map/all_to_all | solution.py:561
  224.5 11.6 %copy-start.1 = (f32[1024,128]{1,0:T(8,128)S(1)}, f32[1024,128]{1,0:T(8,128)}, u32[]{:S(2)}) copy-start(f32[1024,128]{1,0:T(8,128)} %get-tuple-element.185.refs_10_) | copy-start | bytes 1572868
  224.5 11.6 %copy-start.4 = (f32[1024,128]{1,0:T(8,128)S(1)}, f32[1024,128]{1,0:T(8,128)}, u32[]{:S(2)}) copy-start(f32[1024,128]{1,0:T(8,128)} %get-tuple-element.186.refs_11_) | copy-start | bytes 1572868
  224.5 11.6 %copy-start.20 = (s32[4]{0:T(128)S(1)}, s32[4]{0:T(128)}, u32[]{:S(2)}) copy-start(s32[4]{0:T(128)} %copy-done.18) | copy-start | bytes 52
  224.5 11.6 %copy-start.23 = (s32[4]{0:T(128)S(1)}, s32[4]{0:T(128)}, u32[]{:S(2)}) copy-start(s32[4]{0:T(128)} %refs_1_.12) | copy-start | bytes 52
  224.5 11.6 %copy-start.25 = (s32[4,16]{1,0:T(4,128)S(1)}, s32[4,16]{1,0:T(4,128)}, u32[]{:S(2)}) copy-start(s32[4,16]{1,0:T(4,128)} %refs_2_.5) | copy-start | bytes 772
  231.9 44.5 %collective-permute-start.21 = (bf16[2,1024,384]{2,1,0:T(8,128)(2,1)}, bf16[2,1024,384]{2,1,0:T(8,128)(2,1)}, u32[]{:S(2)}, u32[]{:S(2)}) collective-permute-start(bf16[2,1024,384]{2,1,0:T(8,128)(2,1)} %partner_product.5), channel_id=1, source_target_pairs={{0,4},{4,0},{8,12},{12,8},{1,5},{5,1},{9,13},{13,9},{2,6},{6,2},{1... | collective-permute-start | bytes 4718600 | tf_op jit(solution)/shard_map/ppermute | solution.py:44
  233.9 13.4 %collective-permute-start.22 = (bf16[1,1,1024,128]{3,2,1,0:T(8,128)(2,1)S(1)}, bf16[1,1,1024,128]{3,2,1,0:T(8,128)(2,1)S(1)}, u32[]{:S(2)}, u32[]{:S(2)}) collective-permute-start(bf16[1,1,1024,128]{3,2,1,0:T(8,128)(2,1)S(1)} %bitcast.29), channel_id=1, source_target_pairs={{0,2},{1,3},{2,0},{3,1},{4,6},{5,7},{6,4},{7,5},{8,10},{9,11},{10,... | collective-permute-start | bytes 786440 | tf_op jit(solution)/shard_map/ppermute | solution.py:44
  242.6 4.7 %copy-start.16 = (bf16[4,1,4,128,256]{4,3,2,1,0:T(8,128)(2,1)}, bf16[4,1,4,128,256]{4,3,2,1,0:T(8,128)(2,1)S(1)}, u32[]{:S(2)}) copy-start(bf16[4,1,4,128,256]{4,3,2,1,0:T(8,128)(2,1)S(1)} %get-tuple-element.199) | copy-start | bytes 3145732
  247.2 9.3 %collective-permute-start.25 = (bf16[1,1,1024,128]{3,2,1,0:T(8,128)(2,1)S(1)}, bf16[1,1,1024,128]{3,2,1,0:T(8,128)(2,1)S(1)}, u32[]{:S(2)}, u32[]{:S(2)}) collective-permute-start(bf16[1,1,1024,128]{3,2,1,0:T(8,128)(2,1)S(1)} %bitcast.32), channel_id=1, source_target_pairs={{0,16},{16,0},{1,17},{17,1},{2,18},{18,2},{3,19},{19,3},{4,20},{20... | collective-permute-start | bytes 786440 | tf_op jit(solution)/shard_map/ppermute | solution.py:44
  247.4 17.3 %collective-permute-start.23 = (bf16[2,1,1024,128]{3,2,1,0:T(8,128)(2,1)S(1)}, bf16[2,1,1024,128]{3,2,1,0:T(8,128)(2,1)S(1)}, u32[]{:S(2)}, u32[]{:S(2)}) collective-permute-start(bf16[2,1,1024,128]{3,2,1,0:T(8,128)(2,1)S(1)} %pad_maximum_fusion.8), channel_id=1, source_target_pairs={{0,16},{16,0},{1,17},{17,1},{2,18},{18,2},{3,19},{19,3},{4,20},{20... | collective-permute-start | bytes 1572872 | tf_op jit(solution)/shard_map/ppermute | solution.py:44
  256.6 9.2 %collective-permute-start.26 = (bf16[1,2,1024,128]{3,2,1,0:T(8,128)(2,1)S(1)}, bf16[1,2,1024,128]{3,2,1,0:T(8,128)(2,1)S(1)}, u32[]{:S(2)}, u32[]{:S(2)}) collective-permute-start(bf16[1,2,1024,128]{3,2,1,0:T(8,128)(2,1)S(1)} %pad_maximum_fusion.9), channel_id=1, source_target_pairs={{0,2},{1,3},{2,0},{3,1},{4,6},{5,7},{6,4},{7,5},{8,10},{9,11},{10,... | collective-permute-start | bytes 1572872 | tf_op jit(solution)/shard_map/ppermute | solution.py:44
  264.8 11.7 %copy-start.8 = (bf16[2,2,1024,128]{3,2,1,0:T(8,128)(2,1)}, bf16[2,2,1024,128]{3,2,1,0:T(8,128)(2,1)S(1)}, u32[]{:S(2)}) copy-start(bf16[2,2,1024,128]{3,2,1,0:T(8,128)(2,1)S(1)} %pad_maximum_fusion.4.refs_1_) | copy-start | bytes 3145732
  264.8 11.7 %collective-permute-start.24 = (bf16[2,2,1024,128]{3,2,1,0:T(8,128)(2,1)S(1)}, bf16[2,2,1024,128]{3,2,1,0:T(8,128)(2,1)}, u32[]{:S(2)}, u32[]{:S(2)}) collective-permute-start(bf16[2,2,1024,128]{3,2,1,0:T(8,128)(2,1)S(1)} %pad_maximum_fusion.4.refs_1_), channel_id=1, source_target_pairs={{0,1},{1,0},{2,3},{3,2},{4,5},{5,4},{6,7},{7,6},{8,9},{9,8},{10,11... | collective-permute-start | bytes 3145736 | tf_op jit(solution)/shard_map/ppermute | solution.py:44
  266.0 10.5 %copy-start.10 = (bf16[2,2,1024,128]{3,2,1,0:T(8,128)(2,1)}, bf16[2,2,1024,128]{3,2,1,0:T(8,128)(2,1)S(1)}, u32[]{:S(2)}) copy-start(bf16[2,2,1024,128]{3,2,1,0:T(8,128)(2,1)S(1)} %pad_maximum_fusion.5.refs_3_) | copy-start | bytes 3145732
  266.0 10.5 %collective-permute-start.27 = (bf16[2,2,1024,128]{3,2,1,0:T(8,128)(2,1)S(1)}, bf16[2,2,1024,128]{3,2,1,0:T(8,128)(2,1)}, u32[]{:S(2)}, u32[]{:S(2)}) collective-permute-start(bf16[2,2,1024,128]{3,2,1,0:T(8,128)(2,1)S(1)} %pad_maximum_fusion.5.refs_3_), channel_id=1, source_target_pairs={{0,1},{1,0},{2,3},{3,2},{4,5},{5,4},{6,7},{7,6},{8,9},{9,8},{10,11... | collective-permute-start | bytes 3145736 | tf_op jit(solution)/shard_map/ppermute | solution.py:44
  276.5 28.5 %all-to-all-start.3 = ((bf16[4,1,4,128,256]{4,3,2,1,0:T(8,128)(2,1)}), bf16[4,1,4,128,256]{4,3,2,1,0:T(8,128)(2,1)S(1)}, u32[]{:S(2)}, u32[]{:S(2)}) async-start(bf16[4,1,4,128,256]{4,3,2,1,0:T(8,128)(2,1)} %copy-done.16), calls=%async_computation.3 | async-start | bytes 2097152 | tf_op jit(solution)/shard_map/all_to_all | solution.py:561
  305.0 55.0 %all-to-all-start.4 = ((bf16[4,2,4,128,256]{4,3,2,1,0:T(8,128)(2,1)}), bf16[4,2,4,128,256]{4,3,2,1,0:T(8,128)(2,1)S(1)}, u32[]{:S(2)}, u32[]{:S(2)}) async-start(bf16[4,2,4,128,256]{4,3,2,1,0:T(8,128)(2,1)} %get-tuple-element.209), calls=%async_computation.4 | async-start | bytes 4194304 | tf_op jit(solution)/shard_map/all_to_all | solution.py:600
  309.8 10.7 %collective-permute-start.31 = (bf16[1,1,1024,128]{3,2,1,0:T(8,128)(2,1)S(1)}, bf16[1,1,1024,128]{3,2,1,0:T(8,128)(2,1)S(1)}, u32[]{:S(2)}, u32[]{:S(2)}) collective-permute-start(bf16[1,1,1024,128]{3,2,1,0:T(8,128)(2,1)S(1)} %get-tuple-element.212), channel_id=1, source_target_pairs={{0,16},{16,0},{1,17},{17,1},{2,18},{18,2},{3,19},{19,3},{4,20},{20... | collective-permute-start | bytes 786440 | tf_op jit(solution)/shard_map/ppermute | solution.py:44
  310.0 10.6 %collective-permute-start.28 = (bf16[1,1,1024,128]{3,2,1,0:T(8,128)(2,1)S(1)}, bf16[1,1,1024,128]{3,2,1,0:T(8,128)(2,1)S(1)}, u32[]{:S(2)}, u32[]{:S(2)}) collective-permute-start(bf16[1,1,1024,128]{3,2,1,0:T(8,128)(2,1)S(1)} %get-tuple-element.213), channel_id=1, source_target_pairs={{0,2},{1,3},{2,0},{3,1},{4,6},{5,7},{6,4},{7,5},{8,10},{9,11},{10,... | collective-permute-start | bytes 786440 | tf_op jit(solution)/shard_map/ppermute | solution.py:44
  320.5 12.7 %collective-permute-start.32 = (bf16[1,2,1024,128]{3,2,1,0:T(8,128)(2,1)S(1)}, bf16[1,2,1024,128]{3,2,1,0:T(8,128)(2,1)S(1)}, u32[]{:S(2)}, u32[]{:S(2)}) collective-permute-start(bf16[1,2,1024,128]{3,2,1,0:T(8,128)(2,1)S(1)} %pad_maximum_fusion.11), channel_id=1, source_target_pairs={{0,2},{1,3},{2,0},{3,1},{4,6},{5,7},{6,4},{7,5},{8,10},{9,11},{10,... | collective-permute-start | bytes 1572872 | tf_op jit(solution)/shard_map/ppermute | solution.py:44
  320.7 12.7 %collective-permute-start.29 = (bf16[2,1,1024,128]{3,2,1,0:T(8,128)(2,1)S(1)}, bf16[2,1,1024,128]{3,2,1,0:T(8,128)(2,1)S(1)}, u32[]{:S(2)}, u32[]{:S(2)}) collective-permute-start(bf16[2,1,1024,128]{3,2,1,0:T(8,128)(2,1)S(1)} %pad_maximum_fusion.10), channel_id=1, source_target_pairs={{0,16},{16,0},{1,17},{17,1},{2,18},{18,2},{3,19},{19,3},{4,20},{20... | collective-permute-start | bytes 1572872 | tf_op jit(solution)/shard_map/ppermute | solution.py:44
  333.2 2.7 collective-permute-start.33
  333.4 4.0 %collective-permute-start.30 = (bf16[2,2,1024,128]{3,2,1,0:T(8,128)(2,1)S(1)}, bf16[2,2,1024,128]{3,2,1,0:T(8,128)(2,1)S(1)}, u32[]{:S(2)}, u32[]{:S(2)}) collective-permute-start(bf16[2,2,1024,128]{3,2,1,0:T(8,128)(2,1)S(1)} %constant_dynamic-update-slice_fusion.4.refs_1_), channel_id=1, source_target_pairs={{0,1},{1,0},{2,3},{3,2},{4,5},{5,4},{6,7},{7,6},{8,9},{9,8},{10,11... | collective-permute-start | bytes 3145736 | tf_op jit(solution)/shard_map/ppermute | solution.py:44
  342.8 5.6 %collective-permute-start.34 = (bf16[128,512]{1,0:T(8,128)(2,1)S(1)}, bf16[128,512]{1,0:T(8,128)(2,1)S(1)}, u32[]{:S(2)}, u32[]{:S(2)}) collective-permute-start(bf16[128,512]{1,0:T(8,128)(2,1)S(1)} %get-tuple-element.201), channel_id=1, source_target_pairs={{0,16},{1,17},{2,18},{3,19},{16,0},{17,1},{18,2},{19,3},{4,20},{5,... | collective-permute-start | bytes 393224 | tf_op jit(solution)/shard_map/ppermute | solution.py:450
  344.5 6.4 %collective-permute-start.35 = (bf16[128,512]{1,0:T(8,128)(2,1)S(1)}, bf16[128,512]{1,0:T(8,128)(2,1)S(1)}, u32[]{:S(2)}, u32[]{:S(2)}) collective-permute-start(bf16[128,512]{1,0:T(8,128)(2,1)S(1)} %get-tuple-element.202), channel_id=1, source_target_pairs={{0,2},{1,3},{2,0},{3,1},{16,18},{17,19},{18,16},{19,17},{4,6},{5,7... | collective-permute-start | bytes 393224 | tf_op jit(solution)/shard_map/ppermute | solution.py:450
  344.9 9.9 %collective-permute-start.36 = (bf16[128,512]{1,0:T(8,128)(2,1)S(1)}, bf16[128,512]{1,0:T(8,128)(2,1)S(1)}, u32[]{:S(2)}, u32[]{:S(2)}) collective-permute-start(bf16[128,512]{1,0:T(8,128)(2,1)S(1)} %get-tuple-element.203), channel_id=1, source_target_pairs={{0,18},{1,19},{2,16},{3,17},{16,2},{17,3},{18,0},{19,1},{4,22},{5,... | collective-permute-start | bytes 393224 | tf_op jit(solution)/shard_map/ppermute | solution.py:450
  346.3 8.5 %collective-permute-start.37 = (bf16[128,512]{1,0:T(8,128)(2,1)S(1)}, bf16[128,512]{1,0:T(8,128)(2,1)S(1)}, u32[]{:S(2)}, u32[]{:S(2)}) collective-permute-start(bf16[128,512]{1,0:T(8,128)(2,1)S(1)} %get-tuple-element.204), channel_id=1, source_target_pairs={{0,1},{1,0},{2,3},{3,2},{16,17},{17,16},{18,19},{19,18},{4,5},{5,4... | collective-permute-start | bytes 393224 | tf_op jit(solution)/shard_map/ppermute | solution.py:450
  346.3 8.5 %collective-permute-start.38 = (bf16[128,512]{1,0:T(8,128)(2,1)S(1)}, bf16[128,512]{1,0:T(8,128)(2,1)S(1)}, u32[]{:S(2)}, u32[]{:S(2)}) collective-permute-start(bf16[128,512]{1,0:T(8,128)(2,1)S(1)} %get-tuple-element.205), channel_id=1, source_target_pairs={{0,17},{1,16},{2,19},{3,18},{16,1},{17,0},{18,3},{19,2},{4,21},{5,... | collective-permute-start | bytes 393224 | tf_op jit(solution)/shard_map/ppermute | solution.py:450
  348.4 6.4 %collective-permute-start.39 = (bf16[128,512]{1,0:T(8,128)(2,1)S(1)}, bf16[128,512]{1,0:T(8,128)(2,1)S(1)}, u32[]{:S(2)}, u32[]{:S(2)}) collective-permute-start(bf16[128,512]{1,0:T(8,128)(2,1)S(1)} %get-tuple-element.206), channel_id=1, source_target_pairs={{0,3},{1,2},{2,1},{3,0},{16,19},{17,18},{18,17},{19,16},{4,7},{5,6... | collective-permute-start | bytes 393224 | tf_op jit(solution)/shard_map/ppermute | solution.py:450
  350.9 7.1 %copy-start.7 = (bf16[1,1,128,4096]{3,2,1,0:T(8,128)(2,1)S(1)}, bf16[1,1,128,4096]{3,2,1,0:T(8,128)(2,1)}, u32[]{:S(2)}) copy-start(bf16[1,1,128,4096]{3,2,1,0:T(8,128)(2,1)} %param.7) | copy-start | bytes 3145732
  350.9 7.1 %collective-permute-start.40 = (bf16[128,512]{1,0:T(8,128)(2,1)S(1)}, bf16[128,512]{1,0:T(8,128)(2,1)S(1)}, u32[]{:S(2)}, u32[]{:S(2)}) collective-permute-start(bf16[128,512]{1,0:T(8,128)(2,1)S(1)} %get-tuple-element.207), channel_id=1, source_target_pairs={{0,19},{1,18},{2,17},{3,16},{16,3},{17,2},{18,1},{19,0},{4,23},{5,... | collective-permute-start | bytes 393224 | tf_op jit(solution)/shard_map/ppermute | solution.py:450
  (10 other events, 30.4 us)

commit v4 on v3

--- a/solution.py
+++ b/solution.py
@@ -21,8 +21,8 @@
     return pltpu.CompilerParams(vmem_limit_bytes=VMEM_LIMIT)
 
 
-def cost():
-    return pl.CostEstimate(flops=1, bytes_accessed=1, transcendentals=0)
+def cost(microseconds=0):
+    return pl.CostEstimate(flops=1 + int(microseconds * 1e9), bytes_accessed=1, transcendentals=0)
 
 
 def hold(xs, microseconds):
@@ -439,7 +439,7 @@
         in_specs=[pl.BlockSpec(memory_space=SMEM)] + [vmem] * (1 + len(pieces)),
         out_specs=vmem,
         compiler_params=params(),
-        cost_estimate=cost(),
+        cost_estimate=cost(9),
         name="residual",
     )(meta, hidden, *pieces)
 
@@ -462,10 +462,9 @@
         return x
 
     first, second = (over_h, over_t) if h_first else (over_t, over_h)
-    x = first(x[None, None])
+    x = second(first(x[None, None]))
     if token is not None:
         x = after(x, token)
-    x = second(x)
     return [x, swap(x, "hg", h_strides[-1])]
 
 

time: 363 us -> 359 us (0.989)
  waiting for transfers between devices: 184 us -> 179 us
  other arithmetic: 9.87 us -> 14.2 us
    ppermute x34, waiting for transfers between devices: 172 us -> 167 us  [swap(): return lax.ppermute(x, axis, [(i, i ^ stride) for i in range(size)])]
    unnamed x62 -> x58, local copies, waits for them, and re-layouts: 9.66 us -> 7.57 us
  transfers between devices with their start and end apart: 46 -> 46, of which waited for: 22 -> 26; matrix products, arithmetic and copies ran while one was open for 7% -> 8% of each run, Pallas kernels for 22% -> 22%
where the time goes in v4:
time: 359 us; the launch traced here: 358 us
  waiting for transfers between devices  179 us (50%)
  Pallas kernels  81.9 us (23%)
  starting transfers between devices  65.4 us (18%)
  local copies, waits for them, and re-layouts  16 us (4%)
  other arithmetic  14.2 us (4%)
    ppermute x34, waiting for transfers between devices, swap(): return lax.ppermute(x, axis, [(i, i ^ stride) for i in range(size)])  167 us
    ppermute x34, starting transfers between devices, swap(): return lax.ppermute(x, axis, [(i, i ^ stride) for i in range(size)])  39.8 us
    pallas_call x3, Pallas kernels, finish_call(): pl.pallas_call(lambda *refs: finish_body(len(xs), cap, *orders, *refs), o...  23.4 us
    pallas_call x3, Pallas kernels, attend_call(): pl.pallas_call(lambda *refs: attend_body(q_rows, *refs), out_shape=out, g...  17 us
    pallas_call x3, Pallas kernels, partner_call(): pl.pallas_call(lambda *refs: partner_body(len(xs), *refs), grid=(heads,),...  16.3 us
    pallas_call x2, Pallas kernels, output_call(): pl.pallas_call(lambda *refs: output_body(first, heads, group, order_h, or...  11.8 us
    all_to_all x2, starting transfers between devices, on_device(): lax.all_to_all(live['placed'][f], 'dp', 0, 0, tiled=True)  8.67 us
    unnamed x58, local copies, waits for them, and re-layouts  7.57 us
  transfers between devices with their start and end apart: 46, of which 26 were waited for; matrix products, arithmetic and copies ran while one was open for 8% of the time, Pallas kernels for 22%

profile of v4, /device:TPU:0, one launch (start us, length us, event | category | flops | bytes accessed | tf_op | source)
XLA Modules:
  0.0 358.1 jit_solution(6761046726100563862)
XLA Ops:
  0.6 4.1 %collective-permute-start = (bf16[16,128,256]{2,1,0:T(8,128)(2,1)}, bf16[16,128,256]{2,1,0:T(8,128)(2,1)}, u32[]{:S(2)}, u32[]{:S(2)}) collective-permute-start(bf16[16,128,256]{2,1,0:T(8,128)(2,1)} %refs_1_.6), channel_id=1, source_target_pairs={{0,8},{4,12},{8,0},{12,4},{1,9},{5,13},{9,1},{13,5},{2,10},{6,14},... | collective-permute-start | bytes 3145736 | tf_op jit(solution)/shard_map/ppermute | solution.py:44
  4.7 1.6 collective-permute-start.1
  6.3 4.9 %copy.21 = bf16[256,3,16,128]{0,3,1,2:T(8,128)(2,1)} copy(bf16[256,3,16,128]{3,2,1,0:T(8,128)(2,1)} %param.9) | data formatting | bytes 6291456 | tf_op args[2]
  11.2 3.3 fusion.1
  14.5 1.6 copy.26
  16.0 4.5 %all-to-all-start = ((bf16[4,2,256,384]{3,2,1,0:T(8,128)(2,1)}), bf16[4,2,256,384]{3,2,1,0:T(8,128)(2,1)}, u32[]{:S(2)}, u32[]{:S(2)}) async-start(bf16[4,2,256,384]{3,2,1,0:T(8,128)(2,1)} %copy.26), calls=%async_computation | async-start | bytes 3145728 | tf_op jit(solution)/shard_map/all_to_all | solution.py:508
  20.6 1.5 layer_norm.1
  22.2 1.6 collective-permute-start.4
  23.8 2.0 collective-permute-start.2
  27.4 3.0 fusion
  30.6 2.6 copy.25
  34.4 12.3 %collective-permute-done.2 = bf16[1,1,1,128,1024]{4,3,2,1,0:T(8,128)(2,1)S(1)} collective-permute-done((bf16[1,1,1,128,1024]{4,3,2,1,0:T(8,128)(2,1)S(1)}, bf16[1,1,1,128,1024]{4,3,2,1,0:T(8,128)(2,1)S(1)}, u32[]{:S(2)}, u32[]{:S(2)}) %collective-permute-start.2) | collective-permute-done | bytes 262176 | tf_op jit(solution)/shard_map/ppermute | solution.py:44
  46.7 1.6 collective-permute-start.3
  49.7 12.6 %collective-permute-done.6 = bf16[2,128,1024]{2,1,0:T(8,128)(2,1)} collective-permute-done((bf16[2,128,1024]{2,1,0:T(8,128)(2,1)S(1)}, bf16[2,128,1024]{2,1,0:T(8,128)(2,1)}, u32[]{:S(2)}, u32[]{:S(2)}) %collective-permute-start.6) | collective-permute-done | bytes 524320 | tf_op jit(solution)/shard_map/ppermute | solution.py:44
  63.3 2.0 pad_maximum_fusion.1.refs_4_
  67.4 1.5 collective-permute-start.9
  68.9 1.5 collective-permute-start.11
  70.5 3.8 %collective-permute-done.9 = bf16[1,1,1,128,1024]{4,3,2,1,0:T(8,128)(2,1)S(1)} collective-permute-done((bf16[1,1,1,128,1024]{4,3,2,1,0:T(8,128)(2,1)S(1)}, bf16[1,1,1,128,1024]{4,3,2,1,0:T(8,128)(2,1)S(1)}, u32[]{:S(2)}, u32[]{:S(2)}) %collective-permute-start.9) | collective-permute-done | bytes 262176 | tf_op jit(solution)/shard_map/ppermute | solution.py:44
  74.3 1.6 collective-permute-start.10
  77.5 1.7 collective-permute-start.7
  79.2 7.5 %collective-permute-done.10 = bf16[1,2,1,128,1024]{4,3,2,1,0:T(8,128)(2,1)S(1)} collective-permute-done((bf16[1,2,1,128,1024]{4,3,2,1,0:T(8,128)(2,1)S(1)}, bf16[1,2,1,128,1024]{4,3,2,1,0:T(8,128)(2,1)S(1)}, u32[]{:S(2)}, u32[]{:S(2)}) %collective-permute-start.10) | collective-permute-done | bytes 524320 | tf_op jit(solution)/shard_map/ppermute | solution.py:44
  87.6 2.0 collective-permute-start.8
  89.6 4.5 %all-to-all-start.1 = ((bf16[4,2,256,384]{3,2,1,0:T(8,128)(2,1)}), bf16[4,2,256,384]{3,2,1,0:T(8,128)(2,1)}, u32[]{:S(2)}, u32[]{:S(2)}) async-start(bf16[4,2,256,384]{3,2,1,0:T(8,128)(2,1)} %copy.25), calls=%async_computation.1 | async-start | bytes 3145728 | tf_op jit(solution)/shard_map/all_to_all | solution.py:554
  94.8 38.6 %collective-permute-done.8.refs_1_ = bf16[16,128,256]{2,1,0:T(8,128)(2,1)} collective-permute-done((bf16[16,128,256]{2,1,0:T(8,128)(2,1)}, bf16[16,128,256]{2,1,0:T(8,128)(2,1)}, u32[]{:S(2)}, u32[]{:S(2)}) %collective-permute-start.8) | collective-permute-done | bytes 1048608 | tf_op jit(solution)/shard_map/ppermute | solution.py:44
  133.4 12.5 %collective-permute-done.7.refs_0_ = bf16[4,2,256,384]{3,2,1,0:T(8,128)(2,1)} collective-permute-done((bf16[4,2,256,384]{3,2,1,0:T(8,128)(2,1)}, bf16[4,2,256,384]{3,2,1,0:T(8,128)(2,1)}, u32[]{:S(2)}, u32[]{:S(2)}) %collective-permute-start.7) | collective-permute-done | bytes 1572896 | tf_op jit(solution)/shard_map/ppermute | solution.py:44
  145.9 1.6 collective-permute-start.20
  147.5 4.0 %partner_product.3 = bf16[1,1024,384]{2,1,0:T(8,128)(2,1)S(1)} custom-call(bf16[1,2,2,128,1024]{4,3,2,1,0:T(8,128)(2,1)S(1)} %pad_maximum_fusion.2.refs_0_, bf16[1,2,2,128,1024]{4,3,2,1,0:T(8,128)(2,1)S(1)} %pad_maximum_fusion.3.refs_1_, bf16[1,2,2,128,1024]{4,3,2,1,0:T(8,128)(2,1)S(1)} %collective-permute-done.13.refs_2_, ...), custom_call_target="tpu_custom_call" | custom-call | flops 1 | bytes 1 | tf_op jit(solution)/shard_map/partner_product/pallas_call | solution.py:145
  151.5 2.5 collective-permute-start.17
  154.1 4.9 %partner_product.4 = bf16[1,1024,384]{2,1,0:T(8,128)(2,1)} custom-call(bf16[1,2,2,128,1024]{4,3,2,1,0:T(8,128)(2,1)S(1)} %pad_maximum_fusion.2.refs_0_, bf16[1,2,2,128,1024]{4,3,2,1,0:T(8,128)(2,1)S(1)} %pad_maximum_fusion.3.refs_1_, bf16[1,2,2,128,1024]{4,3,2,1,0:T(8,128)(2,1)S(1)} %collective-permute-done.13.refs_2_, ...), custom_call_target="tpu_custom_call" | custom-call | flops 1 | bytes 1 | tf_op jit(solution)/shard_map/partner_product/pallas_call | solution.py:145
  159.2 4.4 %split_columns.1 = (bf16[4,16,128,128]{3,2,1,0:T(8,128)(2,1)}, bf16[4,16,128,128]{3,2,1,0:T(8,128)(2,1)}) custom-call(s32[4]{0:T(128)S(1)} %copy-done.18, bf16[16,128,256]{2,1,0:T(8,128)(2,1)S(1)} %copy-done.10, bf16[16,128,256]{2,1,0:T(8,128)(2,1)} %get-tuple-element.138.refs_2_, bf16[16,128,256]{2,1,0:T(8,128)(2,1)S(1)} %copy-done.12, ...), custom_call_target="tpu_custom_call" | custom-call | flops 1 | bytes 1 | tf_op jit(solution)/shard_map/split_columns/pallas_call | solution.py:320
  164.8 34.7 %collective-permute-done.17.refs_9_ = bf16[1,1024,384]{2,1,0:T(8,128)(2,1)S(1)} collective-permute-done((bf16[1,1024,384]{2,1,0:T(8,128)(2,1)S(1)}, bf16[1,1024,384]{2,1,0:T(8,128)(2,1)S(1)}, u32[]{:S(2)}, u32[]{:S(2)}) %collective-permute-start.17) | collective-permute-done | bytes 786464 | tf_op jit(solution)/shard_map/ppermute | solution.py:44
  199.5 6.3 %finish_projection.3 = (bf16[1,1024,128]{2,1,0:T(8,128)(2,1)S(1)}, bf16[1,1024,256]{2,1,0:T(8,128)(2,1)S(1)}, bf16[4,1,4,128,256]{4,3,2,1,0:T(8,128)(2,1)S(1)}) custom-call(s32[4]{0:T(128)S(1)} %copy-done.18, s32[4]{0:T(128)S(1)} %copy-done.21, s32[4,16]{1,0:T(4,128)S(1)} %copy-done.23, bf16[1,2,2,128,1024]{4,3,2,1,0:T(8,128)(2,1)} %pad_maximum_fusion.refs_3_, ...), custom_call_target="tpu_custom_call" | custom-call | flops 1 | bytes 1 | tf_op jit(solution)/shard_map/finish_projection/pallas_call | solution.py:236
  205.8 4.6 %attention.3 = bf16[1,1024,128]{2,1,0:T(8,128)(2,1)S(1)} custom-call(s32[4]{0:T(128)S(1)} %copy-done.18, s32[4]{0:T(128)S(1)} %copy-done.21, bf16[1,1024,128]{2,1,0:T(8,128)(2,1)S(1)} %get-tuple-element.150.refs_2_, bf16[1,1024,256]{2,1,0:T(8,128)(2,1)S(1)} %get-tuple-element.151.refs_3_, bf16[1,16,1024,256]{3,2,1,0:T(8,128)(2,1)} %refs_4_.5), custom_call_target="tpu_custom_call" | custom-call | flops 1 | bytes 1 | tf_op jit(solution)/shard_map/attention/pallas_call | solution.py:289
  210.4 5.3 %collective-permute-done.20.refs_0_ = bf16[4,2,256,384]{3,2,1,0:T(8,128)(2,1)} collective-permute-done((bf16[4,2,256,384]{3,2,1,0:T(8,128)(2,1)}, bf16[4,2,256,384]{3,2,1,0:T(8,128)(2,1)}, u32[]{:S(2)}, u32[]{:S(2)}) %collective-permute-start.20) | collective-permute-done | bytes 1572896 | tf_op jit(solution)/shard_map/ppermute | solution.py:44
  215.8 4.0 %collective-permute-done.18.refs_9_ = bf16[1,1024,384]{2,1,0:T(8,128)(2,1)} collective-permute-done((bf16[1,1024,384]{2,1,0:T(8,128)(2,1)}, bf16[1,1024,384]{2,1,0:T(8,128)(2,1)}, u32[]{:S(2)}, u32[]{:S(2)}) %collective-permute-start.18) | collective-permute-done | bytes 786464 | tf_op jit(solution)/shard_map/ppermute | solution.py:44
  219.7 4.8 %all-to-all-start.2 = ((bf16[4,1,4,128,256]{4,3,2,1,0:T(8,128)(2,1)}), bf16[4,1,4,128,256]{4,3,2,1,0:T(8,128)(2,1)}, u32[]{:S(2)}, u32[]{:S(2)}) async-start(bf16[4,1,4,128,256]{4,3,2,1,0:T(8,128)(2,1)} %copy-done.16), calls=%async_computation.2 | async-start | bytes 2097152 | tf_op jit(solution)/shard_map/all_to_all | solution.py:560
  224.5 7.4 %partner_product.5 = bf16[2,1024,384]{2,1,0:T(8,128)(2,1)} custom-call(bf16[1,2,2,128,1024]{4,3,2,1,0:T(8,128)(2,1)S(1)} %pad_maximum_fusion.2.refs_0_, bf16[1,2,2,128,1024]{4,3,2,1,0:T(8,128)(2,1)S(1)} %pad_maximum_fusion.3.refs_1_, bf16[1,2,2,128,1024]{4,3,2,1,0:T(8,128)(2,1)S(1)} %collective-permute-done.13.refs_2_, ...), custom_call_target="tpu_custom_call" | custom-call | flops 1 | bytes 1 | tf_op jit(solution)/shard_map/partner_product/pallas_call | solution.py:145
  231.9 2.0 collective-permute-start.21
  233.9 2.2 collective-permute-start.22
  236.2 6.4 %finish_projection.4 = (bf16[1,1024,128]{2,1,0:T(8,128)(2,1)S(1)}, bf16[1,1024,256]{2,1,0:T(8,128)(2,1)S(1)}, bf16[4,1,4,128,256]{4,3,2,1,0:T(8,128)(2,1)S(1)}) custom-call(s32[4]{0:T(128)S(1)} %copy-done.19, s32[4]{0:T(128)S(1)} %copy-done.22, s32[4,16]{1,0:T(4,128)S(1)} %copy-done.24, bf16[1,2,2,128,1024]{4,3,2,1,0:T(8,128)(2,1)} %pad_maximum_fusion.refs_3_, ...), custom_call_target="tpu_custom_call" | custom-call | flops 1 | bytes 1 | tf_op jit(solution)/shard_map/finish_projection/pallas_call | solution.py:236
  242.6 4.6 %attention.4 = bf16[1,1024,128]{2,1,0:T(8,128)(2,1)S(1)} custom-call(s32[4]{0:T(128)S(1)} %copy-done.19, s32[4]{0:T(128)S(1)} %copy-done.22, bf16[1,1024,128]{2,1,0:T(8,128)(2,1)S(1)} %get-tuple-element.172.refs_2_, bf16[1,1024,256]{2,1,0:T(8,128)(2,1)S(1)} %get-tuple-element.173.refs_3_, bf16[1,16,1024,256]{3,2,1,0:T(8,128)(2,1)} %refs_4_.5), custom_call_target="tpu_custom_call" | custom-call | flops 1 | bytes 1 | tf_op jit(solution)/shard_map/attention/pallas_call | solution.py:289
  247.4 2.1 collective-permute-start.23
  249.5 7.1 %collective-permute-done.25 = bf16[1,1,1024,128]{3,2,1,0:T(8,128)(2,1)S(1)} collective-permute-done((bf16[1,1,1024,128]{3,2,1,0:T(8,128)(2,1)S(1)}, bf16[1,1,1024,128]{3,2,1,0:T(8,128)(2,1)S(1)}, u32[]{:S(2)}, u32[]{:S(2)}) %collective-permute-start.25) | collective-permute-done | bytes 262176 | tf_op jit(solution)/shard_map/ppermute | solution.py:44
  256.7 8.0 %collective-permute-done.23 = bf16[2,1,1024,128]{3,2,1,0:T(8,128)(2,1)S(1)} collective-permute-done((bf16[2,1,1024,128]{3,2,1,0:T(8,128)(2,1)S(1)}, bf16[2,1,1024,128]{3,2,1,0:T(8,128)(2,1)S(1)}, u32[]{:S(2)}, u32[]{:S(2)}) %collective-permute-start.23) | collective-permute-done | bytes 524320 | tf_op jit(solution)/shard_map/ppermute | solution.py:44
  266.1 10.4 %collective-permute-done.21.refs_1_ = bf16[2,1024,384]{2,1,0:T(8,128)(2,1)} collective-permute-done((bf16[2,1024,384]{2,1,0:T(8,128)(2,1)}, bf16[2,1024,384]{2,1,0:T(8,128)(2,1)}, u32[]{:S(2)}, u32[]{:S(2)}) %collective-permute-start.21) | collective-permute-done | bytes 1572896 | tf_op jit(solution)/shard_map/ppermute | solution.py:44
  276.5 3.9 %all-to-all-start.3 = ((bf16[4,1,4,128,256]{4,3,2,1,0:T(8,128)(2,1)}), bf16[4,1,4,128,256]{4,3,2,1,0:T(8,128)(2,1)S(1)}, u32[]{:S(2)}, u32[]{:S(2)}) async-start(bf16[4,1,4,128,256]{4,3,2,1,0:T(8,128)(2,1)} %copy-done.15), calls=%async_computation.3 | async-start | bytes 2097152 | tf_op jit(solution)/shard_map/all_to_all | solution.py:560
  280.4 10.7 %finish_projection.5 = (bf16[2,1024,128]{2,1,0:T(8,128)(2,1)S(1)}, bf16[2,1024,256]{2,1,0:T(8,128)(2,1)S(1)}, bf16[4,2,4,128,256]{4,3,2,1,0:T(8,128)(2,1)}) custom-call(s32[4]{0:T(128)S(1)} %copy-done.19, s32[4]{0:T(128)S(1)} %copy-done.22, s32[4,16]{1,0:T(4,128)S(1)} %copy-done.24, bf16[1,2,2,128,1024]{4,3,2,1,0:T(8,128)(2,1)} %pad_maximum_fusion.refs_3_, ...), custom_call_target="tpu_custom_call" | custom-call | flops 1 | bytes 1 | tf_op jit(solution)/shard_map/finish_projection/pallas_call | solution.py:236
  291.1 7.8 %attention.5 = bf16[2,1024,128]{2,1,0:T(8,128)(2,1)S(1)} custom-call(s32[4]{0:T(128)S(1)} %copy-done.19, s32[4]{0:T(128)S(1)} %copy-done.22, bf16[2,1024,128]{2,1,0:T(8,128)(2,1)S(1)} %get-tuple-element.187.refs_2_, bf16[2,1024,256]{2,1,0:T(8,128)(2,1)S(1)} %get-tuple-element.188.refs_3_, bf16[1,16,1024,256]{3,2,1,0:T(8,128)(2,1)} %refs_4_.5), custom_call_target="tpu_custom_call" | custom-call | flops 1 | bytes 1 | tf_op jit(solution)/shard_map/attention/pallas_call | solution.py:289
  299.9 2.2 collective-permute-start.28
  302.1 2.9 all-to-all-done.3.refs_1_
  305.0 3.6 %all-to-all-start.4 = ((bf16[4,2,4,128,256]{4,3,2,1,0:T(8,128)(2,1)}), bf16[4,2,4,128,256]{4,3,2,1,0:T(8,128)(2,1)S(1)}, u32[]{:S(2)}, u32[]{:S(2)}) async-start(bf16[4,2,4,128,256]{4,3,2,1,0:T(8,128)(2,1)} %get-tuple-element.209), calls=%async_computation.4 | async-start | bytes 4194304 | tf_op jit(solution)/shard_map/all_to_all | solution.py:599
  309.9 2.8 collective-permute-start.32
  313.8 6.6 %output_projection.2.refs_7_ = f32[1024,512]{1,0:T(8,128)} custom-call(s32[4]{0:T(128)S(1)} %copy-done.19, bf16[2,2,1024,128]{3,2,1,0:T(8,128)(2,1)S(1)} %copy-done.7, bf16[2,2,1024,128]{3,2,1,0:T(8,128)(2,1)} %collective-permute-done.24.refs_2_, bf16[2,2,1024,128]{3,2,1,0:T(8,128)(2,1)S(1)} %copy-done.9, ...), custom_call_target="tpu_custom_call" | custom-call | flops 1 | bytes 1 | tf_op jit(solution)/shard_map/output_projection/pallas_call | solution.py:367
  320.4 3.5 collective-permute-done.32
  328.0 2.1 collective-permute-done.30.refs_2_
  330.1 1.5 collective-permute-done.33.refs_4_
  331.6 5.3 %output_projection.3 = (bf16[128,512]{1,0:T(8,128)(2,1)S(1)}, bf16[128,512]{1,0:T(8,128)(2,1)S(1)}, bf16[128,512]{1,0:T(8,128)(2,1)S(1)}, bf16[128,512]{1,0:T(8,...) custom-call(s32[4]{0:T(128)S(1)} %copy-done.19, ...), custom_call_target="tpu_custom_call" | custom-call | flops 1 | bytes 1 | tf_op jit(solution)/shard_map/output_projection/pallas_call | solution.py:367
  337.6 2.9 collective-permute-start.36
  340.9 1.6 collective-permute-done.34.refs_3_
  344.0 3.6 collect_blocks.2.refs_1_
  348.4 2.6 collective-permute-done.40.refs_9_
  351.0 2.0 residual.1
  353.0 3.2 all-to-all-done.4.refs_0_
  356.3 1.8 collect_blocks.3
  (137 shorter events, 24.6 us)
Async XLA Ops:
  0.6 65.8 %collective-permute-start = (bf16[16,128,256]{2,1,0:T(8,128)(2,1)}, bf16[16,128,256]{2,1,0:T(8,128)(2,1)}, u32[]{:S(2)}, u32[]{:S(2)}) collective-permute-start(bf16[16,128,256]{2,1,0:T(8,128)(2,1)} %refs_1_.6), channel_id=1, source_target_pairs={{0,8},{4,12},{8,0},{12,4},{1,9},{5,13},{9,1},{13,5},{2,10},{6,14},... | collective-permute-start | bytes 3145736 | tf_op jit(solution)/shard_map/ppermute | solution.py:44
  4.7 61.7 %collective-permute-start.1 = (bf16[16,128,256]{2,1,0:T(8,128)(2,1)}, bf16[16,128,256]{2,1,0:T(8,128)(2,1)S(1)}, u32[]{:S(2)}, u32[]{:S(2)}) collective-permute-start(bf16[16,128,256]{2,1,0:T(8,128)(2,1)} %refs_1_.6), channel_id=1, source_target_pairs={{0,4},{4,0},{8,12},{12,8},{1,5},{5,1},{9,13},{13,9},{2,6},{6,2},{1... | collective-permute-start | bytes 3145736 | tf_op jit(solution)/shard_map/ppermute | solution.py:44
  16.0 51.4 %all-to-all-start = ((bf16[4,2,256,384]{3,2,1,0:T(8,128)(2,1)}), bf16[4,2,256,384]{3,2,1,0:T(8,128)(2,1)}, u32[]{:S(2)}, u32[]{:S(2)}) async-start(bf16[4,2,256,384]{3,2,1,0:T(8,128)(2,1)} %copy.26), calls=%async_computation | async-start | bytes 3145728 | tf_op jit(solution)/shard_map/all_to_all | solution.py:508
  20.5 5.7 %copy-start.20 = (s32[4]{0:T(128)S(1)}, s32[4]{0:T(128)}, u32[]{:S(2)}) copy-start(s32[4]{0:T(128)} %refs_1_.12) | copy-start | bytes 52
  22.2 11.0 %collective-permute-start.4 = (bf16[1,1,1,128,1024]{4,3,2,1,0:T(8,128)(2,1)S(1)}, bf16[1,1,1,128,1024]{4,3,2,1,0:T(8,128)(2,1)}, u32[]{:S(2)}, u32[]{:S(2)}) collective-permute-start(bf16[1,1,1,128,1024]{4,3,2,1,0:T(8,128)(2,1)S(1)} %get-tuple-element.216), channel_id=1, source_target_pairs={{0,16},{16,0},{1,17},{17,1},{2,18},{18,2},{3,19},{19,3},{4,20},{20... | collective-permute-start | bytes 786440 | tf_op jit(solution)/shard_map/ppermute | solution.py:44
  23.8 22.9 %collective-permute-start.2 = (bf16[1,1,1,128,1024]{4,3,2,1,0:T(8,128)(2,1)S(1)}, bf16[1,1,1,128,1024]{4,3,2,1,0:T(8,128)(2,1)S(1)}, u32[]{:S(2)}, u32[]{:S(2)}) collective-permute-start(bf16[1,1,1,128,1024]{4,3,2,1,0:T(8,128)(2,1)S(1)} %get-tuple-element.217), channel_id=1, source_target_pairs={{0,2},{1,3},{2,0},{3,1},{4,6},{5,7},{6,4},{7,5},{8,10},{9,11},{10,... | collective-permute-start | bytes 786440 | tf_op jit(solution)/shard_map/ppermute | solution.py:44
  25.7 36.5 %collective-permute-start.6 = (bf16[2,128,1024]{2,1,0:T(8,128)(2,1)S(1)}, bf16[2,128,1024]{2,1,0:T(8,128)(2,1)}, u32[]{:S(2)}, u32[]{:S(2)}) collective-permute-start(bf16[2,128,1024]{2,1,0:T(8,128)(2,1)S(1)} %get-tuple-element.110), channel_id=1, source_target_pairs={{0,4},{4,0},{8,12},{12,8},{1,5},{5,1},{9,13},{13,9},{2,6},{6,2},{1... | collective-permute-start | bytes 1572872 | tf_op jit(solution)/shard_map/ppermute | solution.py:44
  33.2 15.1 %copy-start.26 = (f32[1024,16]{1,0:T(8,128)S(1)}, f32[1024,16]{1,0:T(8,128)}, u32[]{:S(2)}) copy-start(f32[1024,16]{1,0:T(8,128)} %get-tuple-element.220) | copy-start | bytes 196612
  34.2 29.1 %collective-permute-start.5 = (bf16[1,1,2,128,1024]{4,3,2,1,0:T(8,128)(2,1)S(1)}, bf16[1,1,2,128,1024]{4,3,2,1,0:T(8,128)(2,1)S(1)}, u32[]{:S(2)}, u32[]{:S(2)}) collective-permute-start(bf16[1,1,2,128,1024]{4,3,2,1,0:T(8,128)(2,1)S(1)} %pad_maximum_fusion.9), channel_id=1, source_target_pairs={{0,2},{1,3},{2,0},{3,1},{4,6},{5,7},{6,4},{7,5},{8,10},{9,11},{10,... | collective-permute-start | bytes 1572872 | tf_op jit(solution)/shard_map/ppermute | solution.py:44
  46.7 18.6 %collective-permute-start.3 = (bf16[1,2,1,128,1024]{4,3,2,1,0:T(8,128)(2,1)S(1)}, bf16[1,2,1,128,1024]{4,3,2,1,0:T(8,128)(2,1)S(1)}, u32[]{:S(2)}, u32[]{:S(2)}) collective-permute-start(bf16[1,2,1,128,1024]{4,3,2,1,0:T(8,128)(2,1)S(1)} %pad_maximum_fusion.8), channel_id=1, source_target_pairs={{0,16},{16,0},{1,17},{17,1},{2,18},{18,2},{3,19},{19,3},{4,20},{20... | collective-permute-start | bytes 1572872 | tf_op jit(solution)/shard_map/ppermute | solution.py:44
  67.4 6.9 %collective-permute-start.9 = (bf16[1,1,1,128,1024]{4,3,2,1,0:T(8,128)(2,1)S(1)}, bf16[1,1,1,128,1024]{4,3,2,1,0:T(8,128)(2,1)S(1)}, u32[]{:S(2)}, u32[]{:S(2)}) collective-permute-start(bf16[1,1,1,128,1024]{4,3,2,1,0:T(8,128)(2,1)S(1)} %get-tuple-element.119), channel_id=1, source_target_pairs={{0,2},{1,3},{2,0},{3,1},{4,6},{5,7},{6,4},{7,5},{8,10},{9,11},{10,... | collective-permute-start | bytes 786440 | tf_op jit(solution)/shard_map/ppermute | solution.py:44
  68.9 7.4 %collective-permute-start.11 = (bf16[1,1,1,128,1024]{4,3,2,1,0:T(8,128)(2,1)S(1)}, bf16[1,1,1,128,1024]{4,3,2,1,0:T(8,128)(2,1)S(1)}, u32[]{:S(2)}, u32[]{:S(2)}) collective-permute-start(bf16[1,1,1,128,1024]{4,3,2,1,0:T(8,128)(2,1)S(1)} %get-tuple-element.120), channel_id=1, source_target_pairs={{0,16},{16,0},{1,17},{17,1},{2,18},{18,2},{3,19},{19,3},{4,20},{20... | collective-permute-start | bytes 786440 | tf_op jit(solution)/shard_map/ppermute | solution.py:44
  74.3 12.5 %collective-permute-start.10 = (bf16[1,2,1,128,1024]{4,3,2,1,0:T(8,128)(2,1)S(1)}, bf16[1,2,1,128,1024]{4,3,2,1,0:T(8,128)(2,1)S(1)}, u32[]{:S(2)}, u32[]{:S(2)}) collective-permute-start(bf16[1,2,1,128,1024]{4,3,2,1,0:T(8,128)(2,1)S(1)} %constant_dynamic-update-slice_fusion), channel_id=1, source_target_pairs={{0,16},{16,0},{1,17},{17,1},{2,18},{18,2},{3,19},{19,3},{4,20},{20... | collective-permute-start | bytes 1572872 | tf_op jit(solution)/shard_map/ppermute | solution.py:44
  76.3 11.0 %collective-permute-start.12 = (bf16[1,1,2,128,1024]{4,3,2,1,0:T(8,128)(2,1)S(1)}, bf16[1,1,2,128,1024]{4,3,2,1,0:T(8,128)(2,1)S(1)}, u32[]{:S(2)}, u32[]{:S(2)}) collective-permute-start(bf16[1,1,2,128,1024]{4,3,2,1,0:T(8,128)(2,1)S(1)} %constant_dynamic-update-slice_fusion.2), channel_id=1, source_target_pairs={{0,2},{1,3},{2,0},{3,1},{4,6},{5,7},{6,4},{7,5},{8,10},{9,11},{10,... | collective-permute-start | bytes 1572872 | tf_op jit(solution)/shard_map/ppermute | solution.py:44
  77.5 68.4 %collective-permute-start.7 = (bf16[4,2,256,384]{3,2,1,0:T(8,128)(2,1)}, bf16[4,2,256,384]{3,2,1,0:T(8,128)(2,1)}, u32[]{:S(2)}, u32[]{:S(2)}) collective-permute-start(bf16[4,2,256,384]{3,2,1,0:T(8,128)(2,1)} %all-to-all-done.refs_4_.refs_7_), channel_id=1, source_target_pairs={{0,8},{4,12},{8,0},{12,4},{1,9},{5,13},{9,1},{13,5},{2,10},{6,14},... | collective-permute-start | bytes 4718600 | tf_op jit(solution)/shard_map/ppermute | solution.py:44
  86.8 7.3 %collective-permute-start.13 = (bf16[1,2,2,128,1024]{4,3,2,1,0:T(8,128)(2,1)S(1)}, bf16[1,2,2,128,1024]{4,3,2,1,0:T(8,128)(2,1)S(1)}, u32[]{:S(2)}, u32[]{:S(2)}) collective-permute-start(bf16[1,2,2,128,1024]{4,3,2,1,0:T(8,128)(2,1)S(1)} %pad_maximum_fusion.2.refs_0_), channel_id=1, source_target_pairs={{0,1},{1,0},{2,3},{3,2},{4,5},{5,4},{6,7},{7,6},{8,9},{9,8},{10,11... | collective-permute-start | bytes 3145736 | tf_op jit(solution)/shard_map/ppermute | solution.py:44
  87.4 6.8 %collective-permute-start.14 = (bf16[1,2,2,128,1024]{4,3,2,1,0:T(8,128)(2,1)S(1)}, bf16[1,2,2,128,1024]{4,3,2,1,0:T(8,128)(2,1)}, u32[]{:S(2)}, u32[]{:S(2)}) collective-permute-start(bf16[1,2,2,128,1024]{4,3,2,1,0:T(8,128)(2,1)S(1)} %pad_maximum_fusion.3.refs_1_), channel_id=1, source_target_pairs={{0,1},{1,0},{2,3},{3,2},{4,5},{5,4},{6,7},{7,6},{8,9},{9,8},{10,11... | collective-permute-start | bytes 3145736 | tf_op jit(solution)/shard_map/ppermute | solution.py:44
  87.6 45.8 %collective-permute-start.8 = (bf16[16,128,256]{2,1,0:T(8,128)(2,1)}, bf16[16,128,256]{2,1,0:T(8,128)(2,1)}, u32[]{:S(2)}, u32[]{:S(2)}) collective-permute-start(bf16[16,128,256]{2,1,0:T(8,128)(2,1)} %get-tuple-element.138.refs_2_), channel_id=1, source_target_pairs={{0,4},{4,0},{8,12},{12,8},{1,5},{5,1},{9,13},{13,9},{2,6},{6,2},{1... | collective-permute-start | bytes 3145736 | tf_op jit(solution)/shard_map/ppermute | solution.py:44
  89.6 56.3 %all-to-all-start.1 = ((bf16[4,2,256,384]{3,2,1,0:T(8,128)(2,1)}), bf16[4,2,256,384]{3,2,1,0:T(8,128)(2,1)}, u32[]{:S(2)}, u32[]{:S(2)}) async-start(bf16[4,2,256,384]{3,2,1,0:T(8,128)(2,1)} %copy.25), calls=%async_computation.1 | async-start | bytes 3145728 | tf_op jit(solution)/shard_map/all_to_all | solution.py:554
  94.2 51.7 %collective-permute-start.15 = (bf16[1,2,2,128,1024]{4,3,2,1,0:T(8,128)(2,1)}, bf16[1,2,2,128,1024]{4,3,2,1,0:T(8,128)(2,1)}, u32[]{:S(2)}, u32[]{:S(2)}) collective-permute-start(bf16[1,2,2,128,1024]{4,3,2,1,0:T(8,128)(2,1)} %pad_maximum_fusion.refs_3_), channel_id=1, source_target_pairs={{0,1},{1,0},{2,3},{3,2},{4,5},{5,4},{6,7},{7,6},{8,9},{9,8},{10,11... | collective-permute-start | bytes 3145736 | tf_op jit(solution)/shard_map/ppermute | solution.py:44
  94.5 51.4 %collective-permute-start.16 = (bf16[1,2,2,128,1024]{4,3,2,1,0:T(8,128)(2,1)}, bf16[1,2,2,128,1024]{4,3,2,1,0:T(8,128)(2,1)}, u32[]{:S(2)}, u32[]{:S(2)}) collective-permute-start(bf16[1,2,2,128,1024]{4,3,2,1,0:T(8,128)(2,1)} %pad_maximum_fusion.1.refs_4_), channel_id=1, source_target_pairs={{0,1},{1,0},{2,3},{3,2},{4,5},{5,4},{6,7},{7,6},{8,9},{9,8},{10,11... | collective-permute-start | bytes 3145736 | tf_op jit(solution)/shard_map/ppermute | solution.py:44
  145.9 69.8 %collective-permute-start.20 = (bf16[4,2,256,384]{3,2,1,0:T(8,128)(2,1)}, bf16[4,2,256,384]{3,2,1,0:T(8,128)(2,1)}, u32[]{:S(2)}, u32[]{:S(2)}) collective-permute-start(bf16[4,2,256,384]{3,2,1,0:T(8,128)(2,1)} %all-to-all-done.1.refs_4_.refs_7_), channel_id=1, source_target_pairs={{0,8},{4,12},{8,0},{12,4},{1,9},{5,13},{9,1},{13,5},{2,10},{6,14},... | collective-permute-start | bytes 4718600 | tf_op jit(solution)/shard_map/ppermute | solution.py:44
  151.5 7.7 %copy-start.10 = (bf16[16,128,256]{2,1,0:T(8,128)(2,1)S(1)}, bf16[16,128,256]{2,1,0:T(8,128)(2,1)}, u32[]{:S(2)}) copy-start(bf16[16,128,256]{2,1,0:T(8,128)(2,1)} %refs_1_.6) | copy-start | bytes 3145732
  151.5 7.7 %copy-start.12 = (bf16[16,128,256]{2,1,0:T(8,128)(2,1)S(1)}, bf16[16,128,256]{2,1,0:T(8,128)(2,1)}, u32[]{:S(2)}) copy-start(bf16[16,128,256]{2,1,0:T(8,128)(2,1)} %get-tuple-element.139.refs_3_) | copy-start | bytes 3145732
  151.5 7.7 %copy-start.18 = (s32[4]{0:T(128)S(1)}, s32[4]{0:T(128)}, u32[]{:S(2)}) copy-start(s32[4]{0:T(128)} %copy-done.17) | copy-start | bytes 52
  151.5 47.9 %collective-permute-start.17 = (bf16[1,1024,384]{2,1,0:T(8,128)(2,1)S(1)}, bf16[1,1024,384]{2,1,0:T(8,128)(2,1)S(1)}, u32[]{:S(2)}, u32[]{:S(2)}) collective-permute-start(bf16[1,1024,384]{2,1,0:T(8,128)(2,1)S(1)} %partner_product.3), channel_id=1, source_target_pairs={{0,4},{4,0},{8,12},{12,8},{1,5},{5,1},{9,13},{13,9},{2,6},{6,2},{1... | collective-permute-start | bytes 2359304 | tf_op jit(solution)/shard_map/ppermute | solution.py:44
  159.0 40.5 %copy-start = (f32[1024,128]{1,0:T(8,128)S(1)}, f32[1024,128]{1,0:T(8,128)}, u32[]{:S(2)}) copy-start(f32[1024,128]{1,0:T(8,128)} %get-tuple-element.185.refs_10_) | copy-start | bytes 1572868
  159.0 40.5 %copy-start.3 = (f32[1024,128]{1,0:T(8,128)S(1)}, f32[1024,128]{1,0:T(8,128)}, u32[]{:S(2)}) copy-start(f32[1024,128]{1,0:T(8,128)} %get-tuple-element.186.refs_11_) | copy-start | bytes 1572868
  159.0 40.5 %copy-start.21 = (s32[4]{0:T(128)S(1)}, s32[4]{0:T(128)}, u32[]{:S(2)}) copy-start(s32[4]{0:T(128)} %refs_1_.12) | copy-start | bytes 52
  159.0 40.5 %copy-start.23 = (s32[4,16]{1,0:T(4,128)S(1)}, s32[4,16]{1,0:T(4,128)}, u32[]{:S(2)}) copy-start(s32[4,16]{1,0:T(4,128)} %refs_2_.5) | copy-start | bytes 772
  159.0 60.7 %collective-permute-start.18 = (bf16[1,1024,384]{2,1,0:T(8,128)(2,1)}, bf16[1,1024,384]{2,1,0:T(8,128)(2,1)}, u32[]{:S(2)}, u32[]{:S(2)}) collective-permute-start(bf16[1,1024,384]{2,1,0:T(8,128)(2,1)} %partner_product.4), channel_id=1, source_target_pairs={{0,4},{4,0},{8,12},{12,8},{1,5},{5,1},{9,13},{13,9},{2,6},{6,2},{1... | collective-permute-start | bytes 2359304 | tf_op jit(solution)/shard_map/ppermute | solution.py:44
  163.6 56.1 %collective-permute-start.19 = (bf16[4,16,128,128]{3,2,1,0:T(8,128)(2,1)}, bf16[4,16,128,128]{3,2,1,0:T(8,128)(2,1)}, u32[]{:S(2)}, u32[]{:S(2)}) collective-permute-start(bf16[4,16,128,128]{3,2,1,0:T(8,128)(2,1)} %get-tuple-element.142), channel_id=1, source_target_pairs={{0,16},{16,0},{1,17},{17,1},{2,18},{18,2},{3,19},{19,3},{4,20},{20... | collective-permute-start | bytes 6291464 | tf_op jit(solution)/shard_map/ppermute | solution.py:44
  219.7 46.3 %all-to-all-start.2 = ((bf16[4,1,4,128,256]{4,3,2,1,0:T(8,128)(2,1)}), bf16[4,1,4,128,256]{4,3,2,1,0:T(8,128)(2,1)}, u32[]{:S(2)}, u32[]{:S(2)}) async-start(bf16[4,1,4,128,256]{4,3,2,1,0:T(8,128)(2,1)} %copy-done.16), calls=%async_computation.2 | async-start | bytes 2097152 | tf_op jit(solution)/shard_map/all_to_all | solution.py:560
  224.5 11.7 %copy-start.1 = (f32[1024,128]{1,0:T(8,128)S(1)}, f32[1024,128]{1,0:T(8,128)}, u32[]{:S(2)}) copy-start(f32[1024,128]{1,0:T(8,128)} %get-tuple-element.185.refs_10_) | copy-start | bytes 1572868
  224.5 11.7 %copy-start.4 = (f32[1024,128]{1,0:T(8,128)S(1)}, f32[1024,128]{1,0:T(8,128)}, u32[]{:S(2)}) copy-start(f32[1024,128]{1,0:T(8,128)} %get-tuple-element.186.refs_11_) | copy-start | bytes 1572868
  224.5 11.7 %copy-start.19 = (s32[4]{0:T(128)S(1)}, s32[4]{0:T(128)}, u32[]{:S(2)}) copy-start(s32[4]{0:T(128)} %copy-done.17) | copy-start | bytes 52
  224.5 11.7 %copy-start.22 = (s32[4]{0:T(128)S(1)}, s32[4]{0:T(128)}, u32[]{:S(2)}) copy-start(s32[4]{0:T(128)} %refs_1_.12) | copy-start | bytes 52
  224.5 11.6 %copy-start.24 = (s32[4,16]{1,0:T(4,128)S(1)}, s32[4,16]{1,0:T(4,128)}, u32[]{:S(2)}) copy-start(s32[4,16]{1,0:T(4,128)} %refs_2_.5) | copy-start | bytes 772
  231.9 44.5 %collective-permute-start.21 = (bf16[2,1024,384]{2,1,0:T(8,128)(2,1)}, bf16[2,1024,384]{2,1,0:T(8,128)(2,1)}, u32[]{:S(2)}, u32[]{:S(2)}) collective-permute-start(bf16[2,1024,384]{2,1,0:T(8,128)(2,1)} %partner_product.5), channel_id=1, source_target_pairs={{0,4},{4,0},{8,12},{12,8},{1,5},{5,1},{9,13},{13,9},{2,6},{6,2},{1... | collective-permute-start | bytes 4718600 | tf_op jit(solution)/shard_map/ppermute | solution.py:44
  233.9 13.4 %collective-permute-start.22 = (bf16[1,1,1024,128]{3,2,1,0:T(8,128)(2,1)S(1)}, bf16[1,1,1024,128]{3,2,1,0:T(8,128)(2,1)S(1)}, u32[]{:S(2)}, u32[]{:S(2)}) collective-permute-start(bf16[1,1,1024,128]{3,2,1,0:T(8,128)(2,1)S(1)} %bitcast.27), channel_id=1, source_target_pairs={{0,2},{1,3},{2,0},{3,1},{4,6},{5,7},{6,4},{7,5},{8,10},{9,11},{10,... | collective-permute-start | bytes 786440 | tf_op jit(solution)/shard_map/ppermute | solution.py:44
  247.3 9.3 %collective-permute-start.25 = (bf16[1,1,1024,128]{3,2,1,0:T(8,128)(2,1)S(1)}, bf16[1,1,1024,128]{3,2,1,0:T(8,128)(2,1)S(1)}, u32[]{:S(2)}, u32[]{:S(2)}) collective-permute-start(bf16[1,1,1024,128]{3,2,1,0:T(8,128)(2,1)S(1)} %bitcast.30), channel_id=1, source_target_pairs={{0,16},{16,0},{1,17},{17,1},{2,18},{18,2},{3,19},{19,3},{4,20},{20... | collective-permute-start | bytes 786440 | tf_op jit(solution)/shard_map/ppermute | solution.py:44
  247.4 17.3 %collective-permute-start.23 = (bf16[2,1,1024,128]{3,2,1,0:T(8,128)(2,1)S(1)}, bf16[2,1,1024,128]{3,2,1,0:T(8,128)(2,1)S(1)}, u32[]{:S(2)}, u32[]{:S(2)}) collective-permute-start(bf16[2,1,1024,128]{3,2,1,0:T(8,128)(2,1)S(1)} %pad_maximum_fusion.10), channel_id=1, source_target_pairs={{0,16},{16,0},{1,17},{17,1},{2,18},{18,2},{3,19},{19,3},{4,20},{20... | collective-permute-start | bytes 1572872 | tf_op jit(solution)/shard_map/ppermute | solution.py:44
  256.6 9.2 %collective-permute-start.26 = (bf16[1,2,1024,128]{3,2,1,0:T(8,128)(2,1)S(1)}, bf16[1,2,1024,128]{3,2,1,0:T(8,128)(2,1)S(1)}, u32[]{:S(2)}, u32[]{:S(2)}) collective-permute-start(bf16[1,2,1024,128]{3,2,1,0:T(8,128)(2,1)S(1)} %pad_maximum_fusion.11), channel_id=1, source_target_pairs={{0,2},{1,3},{2,0},{3,1},{4,6},{5,7},{6,4},{7,5},{8,10},{9,11},{10,... | collective-permute-start | bytes 1572872 | tf_op jit(solution)/shard_map/ppermute | solution.py:44
  264.8 11.6 %copy-start.6 = (bf16[2,2,1024,128]{3,2,1,0:T(8,128)(2,1)}, bf16[2,2,1024,128]{3,2,1,0:T(8,128)(2,1)S(1)}, u32[]{:S(2)}) copy-start(bf16[2,2,1024,128]{3,2,1,0:T(8,128)(2,1)S(1)} %pad_maximum_fusion.4.refs_1_) | copy-start | bytes 3145732
  264.8 11.6 %collective-permute-start.24 = (bf16[2,2,1024,128]{3,2,1,0:T(8,128)(2,1)S(1)}, bf16[2,2,1024,128]{3,2,1,0:T(8,128)(2,1)}, u32[]{:S(2)}, u32[]{:S(2)}) collective-permute-start(bf16[2,2,1024,128]{3,2,1,0:T(8,128)(2,1)S(1)} %pad_maximum_fusion.4.refs_1_), channel_id=1, source_target_pairs={{0,1},{1,0},{2,3},{3,2},{4,5},{5,4},{6,7},{7,6},{8,9},{9,8},{10,11... | collective-permute-start | bytes 3145736 | tf_op jit(solution)/shard_map/ppermute | solution.py:44
  266.0 10.5 %copy-start.8 = (bf16[2,2,1024,128]{3,2,1,0:T(8,128)(2,1)}, bf16[2,2,1024,128]{3,2,1,0:T(8,128)(2,1)S(1)}, u32[]{:S(2)}) copy-start(bf16[2,2,1024,128]{3,2,1,0:T(8,128)(2,1)S(1)} %pad_maximum_fusion.5.refs_3_) | copy-start | bytes 3145732
  266.0 10.5 %collective-permute-start.27 = (bf16[2,2,1024,128]{3,2,1,0:T(8,128)(2,1)S(1)}, bf16[2,2,1024,128]{3,2,1,0:T(8,128)(2,1)}, u32[]{:S(2)}, u32[]{:S(2)}) collective-permute-start(bf16[2,2,1024,128]{3,2,1,0:T(8,128)(2,1)S(1)} %pad_maximum_fusion.5.refs_3_), channel_id=1, source_target_pairs={{0,1},{1,0},{2,3},{3,2},{4,5},{5,4},{6,7},{7,6},{8,9},{9,8},{10,11... | collective-permute-start | bytes 3145736 | tf_op jit(solution)/shard_map/ppermute | solution.py:44
  276.5 28.5 %all-to-all-start.3 = ((bf16[4,1,4,128,256]{4,3,2,1,0:T(8,128)(2,1)}), bf16[4,1,4,128,256]{4,3,2,1,0:T(8,128)(2,1)S(1)}, u32[]{:S(2)}, u32[]{:S(2)}) async-start(bf16[4,1,4,128,256]{4,3,2,1,0:T(8,128)(2,1)} %copy-done.15), calls=%async_computation.3 | async-start | bytes 2097152 | tf_op jit(solution)/shard_map/all_to_all | solution.py:560
  299.6 9.0 %collective-permute-start.31 = (bf16[1,1,1024,128]{3,2,1,0:T(8,128)(2,1)}, bf16[1,1,1024,128]{3,2,1,0:T(8,128)(2,1)}, u32[]{:S(2)}, u32[]{:S(2)}) collective-permute-start(bf16[1,1,1024,128]{3,2,1,0:T(8,128)(2,1)} %get-tuple-element.212), channel_id=1, source_target_pairs={{0,16},{16,0},{1,17},{17,1},{2,18},{18,2},{3,19},{19,3},{4,20},{20... | collective-permute-start | bytes 786440 | tf_op jit(solution)/shard_map/ppermute | solution.py:44
  299.9 12.8 %collective-permute-start.28 = (bf16[1,1,1024,128]{3,2,1,0:T(8,128)(2,1)S(1)}, bf16[1,1,1024,128]{3,2,1,0:T(8,128)(2,1)}, u32[]{:S(2)}, u32[]{:S(2)}) collective-permute-start(bf16[1,1,1024,128]{3,2,1,0:T(8,128)(2,1)S(1)} %get-tuple-element.213), channel_id=1, source_target_pairs={{0,2},{1,3},{2,0},{3,1},{4,6},{5,7},{6,4},{7,5},{8,10},{9,11},{10,... | collective-permute-start | bytes 786440 | tf_op jit(solution)/shard_map/ppermute | solution.py:44
  305.0 51.3 %all-to-all-start.4 = ((bf16[4,2,4,128,256]{4,3,2,1,0:T(8,128)(2,1)}), bf16[4,2,4,128,256]{4,3,2,1,0:T(8,128)(2,1)S(1)}, u32[]{:S(2)}, u32[]{:S(2)}) async-start(bf16[4,2,4,128,256]{4,3,2,1,0:T(8,128)(2,1)} %get-tuple-element.209), calls=%async_computation.4 | async-start | bytes 4194304 | tf_op jit(solution)/shard_map/all_to_all | solution.py:599
  308.6 5.2 %copy-start.7 = (bf16[2,2,1024,128]{3,2,1,0:T(8,128)(2,1)S(1)}, bf16[2,2,1024,128]{3,2,1,0:T(8,128)(2,1)}, u32[]{:S(2)}) copy-start(bf16[2,2,1024,128]{3,2,1,0:T(8,128)(2,1)} %copy-done.6) | copy-start | bytes 3145732
  309.9 14.0 %collective-permute-start.32 = (bf16[1,2,1024,128]{3,2,1,0:T(8,128)(2,1)S(1)}, bf16[1,2,1024,128]{3,2,1,0:T(8,128)(2,1)S(1)}, u32[]{:S(2)}, u32[]{:S(2)}) collective-permute-start(bf16[1,2,1024,128]{3,2,1,0:T(8,128)(2,1)S(1)} %pad_maximum_fusion.13), channel_id=1, source_target_pairs={{0,2},{1,3},{2,0},{3,1},{4,6},{5,7},{6,4},{7,5},{8,10},{9,11},{10,... | collective-permute-start | bytes 1572872 | tf_op jit(solution)/shard_map/ppermute | solution.py:44
  313.7 12.7 %collective-permute-start.29 = (bf16[2,1,1024,128]{3,2,1,0:T(8,128)(2,1)S(1)}, bf16[2,1,1024,128]{3,2,1,0:T(8,128)(2,1)S(1)}, u32[]{:S(2)}, u32[]{:S(2)}) collective-permute-start(bf16[2,1,1024,128]{3,2,1,0:T(8,128)(2,1)S(1)} %pad_maximum_fusion.12), channel_id=1, source_target_pairs={{0,16},{16,0},{1,17},{17,1},{2,18},{18,2},{3,19},{19,3},{4,20},{20... | collective-permute-start | bytes 1572872 | tf_op jit(solution)/shard_map/ppermute | solution.py:44
  327.4 2.7 collective-permute-start.30
  327.5 4.1 %collective-permute-start.33 = (bf16[2,2,1024,128]{3,2,1,0:T(8,128)(2,1)S(1)}, bf16[2,2,1024,128]{3,2,1,0:T(8,128)(2,1)S(1)}, u32[]{:S(2)}, u32[]{:S(2)}) collective-permute-start(bf16[2,2,1024,128]{3,2,1,0:T(8,128)(2,1)S(1)} %pad_maximum_fusion.7.refs_3_), channel_id=1, source_target_pairs={{0,1},{1,0},{2,3},{3,2},{4,5},{5,4},{6,7},{7,6},{8,9},{9,8},{10,11... | collective-permute-start | bytes 3145736 | tf_op jit(solution)/shard_map/ppermute | solution.py:44
  336.9 5.6 %collective-permute-start.34 = (bf16[128,512]{1,0:T(8,128)(2,1)S(1)}, bf16[128,512]{1,0:T(8,128)(2,1)S(1)}, u32[]{:S(2)}, u32[]{:S(2)}) collective-permute-start(bf16[128,512]{1,0:T(8,128)(2,1)S(1)} %get-tuple-element.201), channel_id=1, source_target_pairs={{0,16},{1,17},{2,18},{3,19},{16,0},{17,1},{18,2},{19,3},{4,20},{5,... | collective-permute-start | bytes 393224 | tf_op jit(solution)/shard_map/ppermute | solution.py:450
  337.3 6.4 %collective-permute-start.35 = (bf16[128,512]{1,0:T(8,128)(2,1)S(1)}, bf16[128,512]{1,0:T(8,128)(2,1)S(1)}, u32[]{:S(2)}, u32[]{:S(2)}) collective-permute-start(bf16[128,512]{1,0:T(8,128)(2,1)S(1)} %get-tuple-element.202), channel_id=1, source_target_pairs={{0,2},{1,3},{2,0},{3,1},{16,18},{17,19},{18,16},{19,17},{4,6},{5,7... | collective-permute-start | bytes 393224 | tf_op jit(solution)/shard_map/ppermute | solution.py:450
  337.6 10.1 %collective-permute-start.36 = (bf16[128,512]{1,0:T(8,128)(2,1)S(1)}, bf16[128,512]{1,0:T(8,128)(2,1)S(1)}, u32[]{:S(2)}, u32[]{:S(2)}) collective-permute-start(bf16[128,512]{1,0:T(8,128)(2,1)S(1)} %get-tuple-element.203), channel_id=1, source_target_pairs={{0,18},{1,19},{2,16},{3,17},{16,2},{17,3},{18,0},{19,1},{4,22},{5,... | collective-permute-start | bytes 393224 | tf_op jit(solution)/shard_map/ppermute | solution.py:450
  340.5 7.2 %collective-permute-start.37 = (bf16[128,512]{1,0:T(8,128)(2,1)S(1)}, bf16[128,512]{1,0:T(8,128)(2,1)S(1)}, u32[]{:S(2)}, u32[]{:S(2)}) collective-permute-start(bf16[128,512]{1,0:T(8,128)(2,1)S(1)} %get-tuple-element.204), channel_id=1, source_target_pairs={{0,1},{1,0},{2,3},{3,2},{16,17},{17,16},{18,19},{19,18},{4,5},{5,4... | collective-permute-start | bytes 393224 | tf_op jit(solution)/shard_map/ppermute | solution.py:450
  340.5 7.9 %collective-permute-start.38 = (bf16[128,512]{1,0:T(8,128)(2,1)S(1)}, bf16[128,512]{1,0:T(8,128)(2,1)S(1)}, u32[]{:S(2)}, u32[]{:S(2)}) collective-permute-start(bf16[128,512]{1,0:T(8,128)(2,1)S(1)} %get-tuple-element.205), channel_id=1, source_target_pairs={{0,17},{1,16},{2,19},{3,18},{16,1},{17,0},{18,3},{19,2},{4,21},{5,... | collective-permute-start | bytes 393224 | tf_op jit(solution)/shard_map/ppermute | solution.py:450
  342.6 5.9 %collective-permute-start.39 = (bf16[128,512]{1,0:T(8,128)(2,1)S(1)}, bf16[128,512]{1,0:T(8,128)(2,1)S(1)}, u32[]{:S(2)}, u32[]{:S(2)}) collective-permute-start(bf16[128,512]{1,0:T(8,128)(2,1)S(1)} %get-tuple-element.206), channel_id=1, source_target_pairs={{0,3},{1,2},{2,1},{3,0},{16,19},{17,18},{18,17},{19,16},{4,7},{5,6... | collective-permute-start | bytes 393224 | tf_op jit(solution)/shard_map/ppermute | solution.py:450
  343.7 7.4 %copy-start.14 = (bf16[1,1,128,4096]{3,2,1,0:T(8,128)(2,1)S(1)}, bf16[1,1,128,4096]{3,2,1,0:T(8,128)(2,1)}, u32[]{:S(2)}) copy-start(bf16[1,1,128,4096]{3,2,1,0:T(8,128)(2,1)} %param.7) | copy-start | bytes 3145732
  343.7 7.4 %collective-permute-start.40 = (bf16[128,512]{1,0:T(8,128)(2,1)S(1)}, bf16[128,512]{1,0:T(8,128)(2,1)S(1)}, u32[]{:S(2)}, u32[]{:S(2)}) collective-permute-start(bf16[128,512]{1,0:T(8,128)(2,1)S(1)} %get-tuple-element.207), channel_id=1, source_target_pairs={{0,19},{1,18},{2,17},{3,16},{16,3},{17,2},{18,1},{19,0},{4,23},{5,... | collective-permute-start | bytes 393224 | tf_op jit(solution)/shard_map/ppermute | solution.py:450
  (9 other events, 34.1 us)

commit v5 on v4

--- a/solution.py
+++ b/solution.py
@@ -553,8 +553,9 @@
         if stage == 1:
             live["mine"] = live["mine"] + [lax.all_to_all(g, "hg", 0, 0, tiled=True) for g in live.pop("given")]
             pair = [over_t(over_h(live["pair"][0])), over_h(over_t(live["pair"][1]))]
+            pair = after(pair, weights[0][-1])
             live["pair"] = pair + [swap(x, "hg", h_strides[-1]) for x in pair]
-            own = after(live["own"], tuple(live["pair"]))
+            own = live["own"]
             live["own"] = own + [swap(x, "hg", h_strides[-1]) for x in own]
         moved = [f for f, _, at, handover in finishing if at < handover == stage]
         come = [lax.all_to_all(live["placed"][f], "dp", 0, 0, tiled=True) for f in moved]

time: 359 us -> 360 us (level)
  local copies, waits for them, and re-layouts: 16 us -> 21.8 us
  waiting for transfers between devices: 179 us -> 174 us
    ppermute x34, waiting for transfers between devices: 167 us -> 162 us  [swap(): return lax.ppermute(x, axis, [(i, i ^ stride) for i in range(size)])]
    unnamed x58 -> x76, local copies, waits for them, and re-layouts: 7.57 us -> 12 us
  transfers between devices with their start and end apart: 46 -> 46, of which waited for: 26 -> 24; matrix products, arithmetic and copies ran while one was open for 8% -> 10% of each run, Pallas kernels for 22% -> 22%
where the time goes in v5:
time: 360 us; the launch traced here: 359 us
  waiting for transfers between devices  174 us (48%)
  Pallas kernels  81.4 us (23%)
  starting transfers between devices  64.1 us (18%)
  local copies, waits for them, and re-layouts  21.8 us (6%)
  other arithmetic  16.3 us (5%)
    ppermute x34, waiting for transfers between devices, swap(): return lax.ppermute(x, axis, [(i, i ^ stride) for i in range(size)])  162 us
    ppermute x34, starting transfers between devices, swap(): return lax.ppermute(x, axis, [(i, i ^ stride) for i in range(size)])  37.5 us
    pallas_call x3, Pallas kernels, finish_call(): pl.pallas_call(lambda *refs: finish_body(len(xs), cap, *orders, *refs), o...  23.3 us
    pallas_call x3, Pallas kernels, attend_call(): pl.pallas_call(lambda *refs: attend_body(q_rows, *refs), out_shape=out, g...  17 us
    pallas_call x3, Pallas kernels, partner_call(): pl.pallas_call(lambda *refs: partner_body(len(xs), *refs), grid=(heads,),...  16.3 us
    unnamed x76, local copies, waits for them, and re-layouts  12 us
    pallas_call x2, Pallas kernels, output_call(): pl.pallas_call(lambda *refs: output_body(first, heads, group, order_h, or...  11.8 us
    all_to_all x2, starting transfers between devices, on_device(): lax.all_to_all(live['placed'][f], 'dp', 0, 0, tiled=True)  8.38 us
  transfers between devices with their start and end apart: 46, of which 24 were waited for; matrix products, arithmetic and copies ran while one was open for 10% of the time, Pallas kernels for 22%

profile of v5, /device:TPU:0, one launch (start us, length us, event | category | flops | bytes accessed | tf_op | source)
XLA Modules:
  0.0 359.2 jit_solution(15246057123330017563)
XLA Ops:
  0.6 4.1 %collective-permute-start = (bf16[16,128,256]{2,1,0:T(8,128)(2,1)}, bf16[16,128,256]{2,1,0:T(8,128)(2,1)S(1)}, u32[]{:S(2)}, u32[]{:S(2)}) collective-permute-start(bf16[16,128,256]{2,1,0:T(8,128)(2,1)} %refs_1_.6), channel_id=1, source_target_pairs={{0,8},{4,12},{8,0},{12,4},{1,9},{5,13},{9,1},{13,5},{2,10},{6,14},... | collective-permute-start | bytes 3145736 | tf_op jit(solution)/shard_map/ppermute | solution.py:44
  4.7 1.6 collective-permute-start.1
  6.3 4.9 %copy.21 = bf16[256,3,16,128]{0,3,1,2:T(8,128)(2,1)} copy(bf16[256,3,16,128]{3,2,1,0:T(8,128)(2,1)} %param.9) | data formatting | bytes 6291456 | tf_op args[2]
  11.2 3.8 %fusion.1 = (bf16[4,2,256,384]{2,3,1,0:T(8,128)(2,1)}, bf16[4,2,256,384]{2,3,1,0:T(8,128)(2,1)}) fusion(bf16[4,4,256,384]{2,3,1,0:T(8,128)(2,1)} %bitcast.36), kind=kLoop, calls=%fused_computation.32 | loop fusion | bytes 6291456 | tf_op jit(solution)/shard_map/slice | solution.py:507
  15.0 2.6 copy.26
  17.6 4.5 %all-to-all-start = ((bf16[4,2,256,384]{3,2,1,0:T(8,128)(2,1)}), bf16[4,2,256,384]{3,2,1,0:T(8,128)(2,1)}, u32[]{:S(2)}, u32[]{:S(2)}) async-start(bf16[4,2,256,384]{3,2,1,0:T(8,128)(2,1)} %copy.26), calls=%async_computation | async-start | bytes 3145728 | tf_op jit(solution)/shard_map/all_to_all | solution.py:508
  22.2 2.3 layer_norm.1
  24.6 1.6 collective-permute-start.4
  26.1 2.0 collective-permute-start.2
  29.8 3.1 fusion
  33.0 2.6 copy.25
  36.8 11.4 %collective-permute-done.2 = bf16[1,1,1,128,1024]{4,3,2,1,0:T(8,128)(2,1)S(1)} collective-permute-done((bf16[1,1,1,128,1024]{4,3,2,1,0:T(8,128)(2,1)S(1)}, bf16[1,1,1,128,1024]{4,3,2,1,0:T(8,128)(2,1)S(1)}, u32[]{:S(2)}, u32[]{:S(2)}) %collective-permute-start.2) | collective-permute-done | bytes 262176 | tf_op jit(solution)/shard_map/ppermute | solution.py:44
  48.3 1.6 collective-permute-start.3
  51.2 11.0 %collective-permute-done.6 = bf16[2,128,1024]{2,1,0:T(8,128)(2,1)} collective-permute-done((bf16[2,128,1024]{2,1,0:T(8,128)(2,1)}, bf16[2,128,1024]{2,1,0:T(8,128)(2,1)}, u32[]{:S(2)}, u32[]{:S(2)}) %collective-permute-start.6) | collective-permute-done | bytes 524320 | tf_op jit(solution)/shard_map/ppermute | solution.py:44
  62.2 1.8 slice_bitcast_fusion.2
  64.0 2.0 pad_maximum_fusion.1.refs_4_
  70.5 1.5 collective-permute-start.13
  72.0 1.5 collective-permute-start.11
  73.5 1.7 collective-permute-start.8
  77.7 1.5 collective-permute-start.14
  79.3 1.6 collective-permute-start.12
  80.8 4.5 %all-to-all-start.1 = ((bf16[4,2,256,384]{3,2,1,0:T(8,128)(2,1)}), bf16[4,2,256,384]{3,2,1,0:T(8,128)(2,1)}, u32[]{:S(2)}, u32[]{:S(2)}) async-start(bf16[4,2,256,384]{3,2,1,0:T(8,128)(2,1)} %copy.25), calls=%async_computation.1 | async-start | bytes 3145728 | tf_op jit(solution)/shard_map/all_to_all | solution.py:554
  85.6 5.8 %collective-permute-done.14 = bf16[1,1,2,128,1024]{4,3,2,1,0:T(8,128)(2,1)S(1)} collective-permute-done((bf16[1,1,2,128,1024]{4,3,2,1,0:T(8,128)(2,1)S(1)}, bf16[1,1,2,128,1024]{4,3,2,1,0:T(8,128)(2,1)S(1)}, u32[]{:S(2)}, u32[]{:S(2)}) %collective-permute-start.14) | collective-permute-done | bytes 524320 | tf_op jit(solution)/shard_map/ppermute | solution.py:44
  93.7 32.5 %collective-permute-done.8.refs_1_ = bf16[16,128,256]{2,1,0:T(8,128)(2,1)S(1)} collective-permute-done((bf16[16,128,256]{2,1,0:T(8,128)(2,1)}, bf16[16,128,256]{2,1,0:T(8,128)(2,1)S(1)}, u32[]{:S(2)}, u32[]{:S(2)}) %collective-permute-start.8) | collective-permute-done | bytes 1048608 | tf_op jit(solution)/shard_map/ppermute | solution.py:44
  126.1 14.1 %collective-permute-done.7.refs_0_ = bf16[4,2,256,384]{3,2,1,0:T(8,128)(2,1)} collective-permute-done((bf16[4,2,256,384]{3,2,1,0:T(8,128)(2,1)}, bf16[4,2,256,384]{3,2,1,0:T(8,128)(2,1)}, u32[]{:S(2)}, u32[]{:S(2)}) %collective-permute-start.7) | collective-permute-done | bytes 1572896 | tf_op jit(solution)/shard_map/ppermute | solution.py:44
  142.0 2.1 collective-permute-done.15.refs_2_
  144.1 1.6 collective-permute-done.16.refs_3_
  145.7 4.0 %partner_product.3 = bf16[1,1024,384]{2,1,0:T(8,128)(2,1)S(1)} custom-call(bf16[1,2,2,128,1024]{4,3,2,1,0:T(8,128)(2,1)S(1)} %copy-done.1, bf16[1,2,2,128,1024]{4,3,2,1,0:T(8,128)(2,1)S(1)} %copy-done, bf16[1,2,2,128,1024]{4,3,2,1,0:T(8,128)(2,1)S(1)} %collective-permute-done.15.refs_2_, bf16[1,2,2,128,1024]{4,3,2,1,0:T(8,128)(2,1)} %collective-permute-done.16.refs_3_, ...), custom_call_target="tpu_custom_call" | custom-call | flops 1 | bytes 1 | tf_op jit(solution)/shard_map/partner_product/pallas_call | solution.py:145
  149.8 2.0 collective-permute-start.17
  151.8 4.9 %partner_product.4 = bf16[1,1024,384]{2,1,0:T(8,128)(2,1)} custom-call(bf16[1,2,2,128,1024]{4,3,2,1,0:T(8,128)(2,1)S(1)} %copy-done.1, bf16[1,2,2,128,1024]{4,3,2,1,0:T(8,128)(2,1)S(1)} %copy-done, bf16[1,2,2,128,1024]{4,3,2,1,0:T(8,128)(2,1)S(1)} %collective-permute-done.15.refs_2_, bf16[1,2,2,128,1024]{4,3,2,1,0:T(8,128)(2,1)} %collective-permute-done.16.refs_3_, ...), custom_call_target="tpu_custom_call" | custom-call | flops 1 | bytes 1 | tf_op jit(solution)/shard_map/partner_product/pallas_call | solution.py:145
  157.0 3.3 split_columns.1
  161.7 35.8 %collective-permute-done.17.refs_9_ = bf16[1,1024,384]{2,1,0:T(8,128)(2,1)S(1)} collective-permute-done((bf16[1,1024,384]{2,1,0:T(8,128)(2,1)S(1)}, bf16[1,1024,384]{2,1,0:T(8,128)(2,1)S(1)}, u32[]{:S(2)}, u32[]{:S(2)}) %collective-permute-start.17) | collective-permute-done | bytes 786464 | tf_op jit(solution)/shard_map/ppermute | solution.py:44
  197.6 6.3 %finish_projection.3 = (bf16[1,1024,128]{2,1,0:T(8,128)(2,1)S(1)}, bf16[1,1024,256]{2,1,0:T(8,128)(2,1)S(1)}, bf16[4,1,4,128,256]{4,3,2,1,0:T(8,128)(2,1)S(1)}) custom-call(s32[4]{0:T(128)S(1)} %copy-done.24, s32[4]{0:T(128)S(1)} %copy-done.26, s32[4,16]{1,0:T(4,128)S(1)} %copy-done.29, bf16[1,2,2,128,1024]{4,3,2,1,0:T(8,128)(2,1)} %pad_maximum_fusion.refs_3_, ...), custom_call_target="tpu_custom_call" | custom-call | flops 1 | bytes 1 | tf_op jit(solution)/shard_map/finish_projection/pallas_call | solution.py:236
  203.9 4.6 %attention.3 = bf16[1,1024,128]{2,1,0:T(8,128)(2,1)S(1)} custom-call(s32[4]{0:T(128)S(1)} %copy-done.24, s32[4]{0:T(128)S(1)} %copy-done.27, bf16[1,1024,128]{2,1,0:T(8,128)(2,1)S(1)} %get-tuple-element.150.refs_2_, bf16[1,1024,256]{2,1,0:T(8,128)(2,1)S(1)} %get-tuple-element.151.refs_3_, bf16[1,16,1024,256]{3,2,1,0:T(8,128)(2,1)} %refs_4_.5), custom_call_target="tpu_custom_call" | custom-call | flops 1 | bytes 1 | tf_op jit(solution)/shard_map/attention/pallas_call | solution.py:289
  208.5 7.5 %collective-permute-done.20.refs_0_ = bf16[4,2,256,384]{3,2,1,0:T(8,128)(2,1)} collective-permute-done((bf16[4,2,256,384]{3,2,1,0:T(8,128)(2,1)}, bf16[4,2,256,384]{3,2,1,0:T(8,128)(2,1)}, u32[]{:S(2)}, u32[]{:S(2)}) %collective-permute-start.20) | collective-permute-done | bytes 1572896 | tf_op jit(solution)/shard_map/ppermute | solution.py:44
  216.0 4.1 %collective-permute-done.18.refs_9_ = bf16[1,1024,384]{2,1,0:T(8,128)(2,1)} collective-permute-done((bf16[1,1024,384]{2,1,0:T(8,128)(2,1)}, bf16[1,1024,384]{2,1,0:T(8,128)(2,1)}, u32[]{:S(2)}, u32[]{:S(2)}) %collective-permute-start.18) | collective-permute-done | bytes 786464 | tf_op jit(solution)/shard_map/ppermute | solution.py:44
  220.0 4.5 %all-to-all-start.2 = ((bf16[4,1,4,128,256]{4,3,2,1,0:T(8,128)(2,1)}), bf16[4,1,4,128,256]{4,3,2,1,0:T(8,128)(2,1)}, u32[]{:S(2)}, u32[]{:S(2)}) async-start(bf16[4,1,4,128,256]{4,3,2,1,0:T(8,128)(2,1)} %copy-done.22), calls=%async_computation.2 | async-start | bytes 2097152 | tf_op jit(solution)/shard_map/all_to_all | solution.py:561
  224.5 7.4 %partner_product.5 = bf16[2,1024,384]{2,1,0:T(8,128)(2,1)} custom-call(bf16[1,2,2,128,1024]{4,3,2,1,0:T(8,128)(2,1)S(1)} %copy-done.1, bf16[1,2,2,128,1024]{4,3,2,1,0:T(8,128)(2,1)S(1)} %copy-done, bf16[1,2,2,128,1024]{4,3,2,1,0:T(8,128)(2,1)S(1)} %collective-permute-done.15.refs_2_, bf16[1,2,2,128,1024]{4,3,2,1,0:T(8,128)(2,1)} %collective-permute-done.16.refs_3_, ...), custom_call_target="tpu_custom_call" | custom-call | flops 1 | bytes 1 | tf_op jit(solution)/shard_map/partner_product/pallas_call | solution.py:145
  231.9 1.7 collective-permute-start.21
  235.1 6.4 %finish_projection.4 = (bf16[1,1024,128]{2,1,0:T(8,128)(2,1)S(1)}, bf16[1,1024,256]{2,1,0:T(8,128)(2,1)S(1)}, bf16[4,1,4,128,256]{4,3,2,1,0:T(8,128)(2,1)S(1)}) custom-call(s32[4]{0:T(128)S(1)} %copy-done.25, s32[4]{0:T(128)S(1)} %copy-done.28, s32[4,16]{1,0:T(4,128)S(1)} %copy-done.30, bf16[1,2,2,128,1024]{4,3,2,1,0:T(8,128)(2,1)} %pad_maximum_fusion.refs_3_, ...), custom_call_target="tpu_custom_call" | custom-call | flops 1 | bytes 1 | tf_op jit(solution)/shard_map/finish_projection/pallas_call | solution.py:236
  241.5 4.6 %attention.4 = bf16[1,1024,128]{2,1,0:T(8,128)(2,1)S(1)} custom-call(s32[4]{0:T(128)S(1)} %copy-done.25, s32[4]{0:T(128)S(1)} %copy-done.28, bf16[1,1024,128]{2,1,0:T(8,128)(2,1)S(1)} %get-tuple-element.172.refs_2_, bf16[1,1024,256]{2,1,0:T(8,128)(2,1)S(1)} %get-tuple-element.173.refs_3_, bf16[1,16,1024,256]{3,2,1,0:T(8,128)(2,1)} %refs_4_.5), custom_call_target="tpu_custom_call" | custom-call | flops 1 | bytes 1 | tf_op jit(solution)/shard_map/attention/pallas_call | solution.py:289
  246.2 1.6 collective-permute-start.25
  248.4 7.1 %collective-permute-done.25 = bf16[1,1,1024,128]{3,2,1,0:T(8,128)(2,1)S(1)} collective-permute-done((bf16[1,1,1024,128]{3,2,1,0:T(8,128)(2,1)S(1)}, bf16[1,1,1024,128]{3,2,1,0:T(8,128)(2,1)S(1)}, u32[]{:S(2)}, u32[]{:S(2)}) %collective-permute-start.25) | collective-permute-done | bytes 262176 | tf_op jit(solution)/shard_map/ppermute | solution.py:44
  256.2 7.9 %collective-permute-done.23 = bf16[2,1,1024,128]{3,2,1,0:T(8,128)(2,1)S(1)} collective-permute-done((bf16[2,1,1024,128]{3,2,1,0:T(8,128)(2,1)S(1)}, bf16[2,1,1024,128]{3,2,1,0:T(8,128)(2,1)S(1)}, u32[]{:S(2)}, u32[]{:S(2)}) %collective-permute-start.23) | collective-permute-done | bytes 524320 | tf_op jit(solution)/shard_map/ppermute | solution.py:44
  265.0 12.0 %collective-permute-done.21.refs_1_ = bf16[2,1024,384]{2,1,0:T(8,128)(2,1)} collective-permute-done((bf16[2,1024,384]{2,1,0:T(8,128)(2,1)}, bf16[2,1024,384]{2,1,0:T(8,128)(2,1)}, u32[]{:S(2)}, u32[]{:S(2)}) %collective-permute-start.21) | collective-permute-done | bytes 1572896 | tf_op jit(solution)/shard_map/ppermute | solution.py:44
  277.0 3.9 %all-to-all-start.3 = ((bf16[4,1,4,128,256]{4,3,2,1,0:T(8,128)(2,1)}), bf16[4,1,4,128,256]{4,3,2,1,0:T(8,128)(2,1)S(1)}, u32[]{:S(2)}, u32[]{:S(2)}) async-start(bf16[4,1,4,128,256]{4,3,2,1,0:T(8,128)(2,1)} %copy-done.21), calls=%async_computation.3 | async-start | bytes 2097152 | tf_op jit(solution)/shard_map/all_to_all | solution.py:561
  281.0 10.6 %finish_projection.5 = (bf16[2,1024,128]{2,1,0:T(8,128)(2,1)S(1)}, bf16[2,1024,256]{2,1,0:T(8,128)(2,1)S(1)}, bf16[4,2,4,128,256]{4,3,2,1,0:T(8,128)(2,1)}) custom-call(s32[4]{0:T(128)S(1)} %copy-done.25, s32[4]{0:T(128)S(1)} %copy-done.28, s32[4,16]{1,0:T(4,128)S(1)} %copy-done.30, bf16[1,2,2,128,1024]{4,3,2,1,0:T(8,128)(2,1)} %pad_maximum_fusion.refs_3_, ...), custom_call_target="tpu_custom_call" | custom-call | flops 1 | bytes 1 | tf_op jit(solution)/shard_map/finish_projection/pallas_call | solution.py:236
  291.5 7.8 %attention.5 = bf16[2,1024,128]{2,1,0:T(8,128)(2,1)S(1)} custom-call(s32[4]{0:T(128)S(1)} %copy-done.25, s32[4]{0:T(128)S(1)} %copy-done.28, bf16[2,1024,128]{2,1,0:T(8,128)(2,1)S(1)} %get-tuple-element.187.refs_2_, bf16[2,1024,256]{2,1,0:T(8,128)(2,1)S(1)} %get-tuple-element.188.refs_3_, bf16[1,16,1024,256]{3,2,1,0:T(8,128)(2,1)} %refs_4_.5), custom_call_target="tpu_custom_call" | custom-call | flops 1 | bytes 1 | tf_op jit(solution)/shard_map/attention/pallas_call | solution.py:289
  303.0 3.1 all-to-all-done.3.refs_1_
  306.1 3.6 %all-to-all-start.4 = ((bf16[4,2,4,128,256]{4,3,2,1,0:T(8,128)(2,1)}), bf16[4,2,4,128,256]{4,3,2,1,0:T(8,128)(2,1)S(1)}, u32[]{:S(2)}, u32[]{:S(2)}) async-start(bf16[4,2,4,128,256]{4,3,2,1,0:T(8,128)(2,1)} %get-tuple-element.209), calls=%async_computation.4 | async-start | bytes 4194304 | tf_op jit(solution)/shard_map/all_to_all | solution.py:600
  313.4 1.6 collective-permute-start.29
  315.0 6.5 %output_projection.2.refs_7_ = f32[1024,512]{1,0:T(8,128)} custom-call(s32[4]{0:T(128)S(1)} %copy-done.25, bf16[2,2,1024,128]{3,2,1,0:T(8,128)(2,1)S(1)} %copy-done.9, bf16[2,2,1024,128]{3,2,1,0:T(8,128)(2,1)} %collective-permute-done.24.refs_2_, bf16[2,2,1024,128]{3,2,1,0:T(8,128)(2,1)S(1)} %copy-done.11, ...), custom_call_target="tpu_custom_call" | custom-call | flops 1 | bytes 1 | tf_op jit(solution)/shard_map/output_projection/pallas_call | solution.py:367
  321.5 2.4 collective-permute-done.32
  327.7 2.1 collective-permute-done.30.refs_2_
  329.9 1.5 collective-permute-done.33.refs_4_
  331.4 5.3 %output_projection.3 = (bf16[128,512]{1,0:T(8,128)(2,1)S(1)}, bf16[128,512]{1,0:T(8,128)(2,1)S(1)}, bf16[128,512]{1,0:T(8,128)(2,1)S(1)}, bf16[128,512]{1,0:T(8,...) custom-call(s32[4]{0:T(128)S(1)} %copy-done.25, ...), custom_call_target="tpu_custom_call" | custom-call | flops 1 | bytes 1 | tf_op jit(solution)/shard_map/output_projection/pallas_call | solution.py:367
  336.7 1.6 collective-permute-start.34
  340.2 1.6 collective-permute-start.38
  342.3 2.4 collective-permute-done.35.refs_4_
  345.0 3.6 collect_blocks.2.refs_1_
  348.6 3.3 collective-permute-done.40.refs_9_
  351.9 2.0 residual.1
  353.9 3.5 all-to-all-done.4.refs_0_
  357.4 1.8 collect_blocks.3
  (155 shorter events, 35.0 us)
Async XLA Ops:
  0.6 66.5 %collective-permute-start = (bf16[16,128,256]{2,1,0:T(8,128)(2,1)}, bf16[16,128,256]{2,1,0:T(8,128)(2,1)S(1)}, u32[]{:S(2)}, u32[]{:S(2)}) collective-permute-start(bf16[16,128,256]{2,1,0:T(8,128)(2,1)} %refs_1_.6), channel_id=1, source_target_pairs={{0,8},{4,12},{8,0},{12,4},{1,9},{5,13},{9,1},{13,5},{2,10},{6,14},... | collective-permute-start | bytes 3145736 | tf_op jit(solution)/shard_map/ppermute | solution.py:44
  4.7 62.4 %collective-permute-start.1 = (bf16[16,128,256]{2,1,0:T(8,128)(2,1)}, bf16[16,128,256]{2,1,0:T(8,128)(2,1)S(1)}, u32[]{:S(2)}, u32[]{:S(2)}) collective-permute-start(bf16[16,128,256]{2,1,0:T(8,128)(2,1)} %refs_1_.6), channel_id=1, source_target_pairs={{0,4},{4,0},{8,12},{12,8},{1,5},{5,1},{9,13},{13,9},{2,6},{6,2},{1... | collective-permute-start | bytes 3145736 | tf_op jit(solution)/shard_map/ppermute | solution.py:44
  17.6 51.5 %all-to-all-start = ((bf16[4,2,256,384]{3,2,1,0:T(8,128)(2,1)}), bf16[4,2,256,384]{3,2,1,0:T(8,128)(2,1)}, u32[]{:S(2)}, u32[]{:S(2)}) async-start(bf16[4,2,256,384]{3,2,1,0:T(8,128)(2,1)} %copy.26), calls=%async_computation | async-start | bytes 3145728 | tf_op jit(solution)/shard_map/all_to_all | solution.py:508
  24.6 11.1 %collective-permute-start.4 = (bf16[1,1,1,128,1024]{4,3,2,1,0:T(8,128)(2,1)S(1)}, bf16[1,1,1,128,1024]{4,3,2,1,0:T(8,128)(2,1)}, u32[]{:S(2)}, u32[]{:S(2)}) collective-permute-start(bf16[1,1,1,128,1024]{4,3,2,1,0:T(8,128)(2,1)S(1)} %get-tuple-element.216), channel_id=1, source_target_pairs={{0,16},{16,0},{1,17},{17,1},{2,18},{18,2},{3,19},{19,3},{4,20},{20... | collective-permute-start | bytes 786440 | tf_op jit(solution)/shard_map/ppermute | solution.py:44
  26.1 22.1 %collective-permute-start.2 = (bf16[1,1,1,128,1024]{4,3,2,1,0:T(8,128)(2,1)S(1)}, bf16[1,1,1,128,1024]{4,3,2,1,0:T(8,128)(2,1)S(1)}, u32[]{:S(2)}, u32[]{:S(2)}) collective-permute-start(bf16[1,1,1,128,1024]{4,3,2,1,0:T(8,128)(2,1)S(1)} %get-tuple-element.217), channel_id=1, source_target_pairs={{0,2},{1,3},{2,0},{3,1},{4,6},{5,7},{6,4},{7,5},{8,10},{9,11},{10,... | collective-permute-start | bytes 786440 | tf_op jit(solution)/shard_map/ppermute | solution.py:44
  28.1 34.1 %collective-permute-start.6 = (bf16[2,128,1024]{2,1,0:T(8,128)(2,1)}, bf16[2,128,1024]{2,1,0:T(8,128)(2,1)}, u32[]{:S(2)}, u32[]{:S(2)}) collective-permute-start(bf16[2,128,1024]{2,1,0:T(8,128)(2,1)} %get-tuple-element.110), channel_id=1, source_target_pairs={{0,4},{4,0},{8,12},{12,8},{1,5},{5,1},{9,13},{13,9},{2,6},{6,2},{1... | collective-permute-start | bytes 1572872 | tf_op jit(solution)/shard_map/ppermute | solution.py:44
  35.6 14.3 %copy-start.32 = (f32[1024,16]{1,0:T(8,128)S(1)}, f32[1024,16]{1,0:T(8,128)}, u32[]{:S(2)}) copy-start(f32[1024,16]{1,0:T(8,128)} %get-tuple-element.219) | copy-start | bytes 196612
  35.6 14.3 %copy-start.33 = (f32[1024,16]{1,0:T(8,128)S(1)}, f32[1024,16]{1,0:T(8,128)}, u32[]{:S(2)}) copy-start(f32[1024,16]{1,0:T(8,128)} %get-tuple-element.220) | copy-start | bytes 196612
  36.7 27.3 %collective-permute-start.5 = (bf16[1,1,2,128,1024]{4,3,2,1,0:T(8,128)(2,1)S(1)}, bf16[1,1,2,128,1024]{4,3,2,1,0:T(8,128)(2,1)S(1)}, u32[]{:S(2)}, u32[]{:S(2)}) collective-permute-start(bf16[1,1,2,128,1024]{4,3,2,1,0:T(8,128)(2,1)S(1)} %pad_maximum_fusion.9), channel_id=1, source_target_pairs={{0,2},{1,3},{2,0},{3,1},{4,6},{5,7},{6,4},{7,5},{8,10},{9,11},{10,... | collective-permute-start | bytes 1572872 | tf_op jit(solution)/shard_map/ppermute | solution.py:44
  48.3 17.8 %collective-permute-start.3 = (bf16[1,2,1,128,1024]{4,3,2,1,0:T(8,128)(2,1)S(1)}, bf16[1,2,1,128,1024]{4,3,2,1,0:T(8,128)(2,1)S(1)}, u32[]{:S(2)}, u32[]{:S(2)}) collective-permute-start(bf16[1,2,1,128,1024]{4,3,2,1,0:T(8,128)(2,1)S(1)} %pad_maximum_fusion.8), channel_id=1, source_target_pairs={{0,16},{16,0},{1,17},{17,1},{2,18},{18,2},{3,19},{19,3},{4,20},{20... | collective-permute-start | bytes 1572872 | tf_op jit(solution)/shard_map/ppermute | solution.py:44
  69.1 71.1 %collective-permute-start.7 = (bf16[4,2,256,384]{3,2,1,0:T(8,128)(2,1)}, bf16[4,2,256,384]{3,2,1,0:T(8,128)(2,1)}, u32[]{:S(2)}, u32[]{:S(2)}) collective-permute-start(bf16[4,2,256,384]{3,2,1,0:T(8,128)(2,1)} %all-to-all-done.refs_4_.refs_7_), channel_id=1, source_target_pairs={{0,8},{4,12},{8,0},{12,4},{1,9},{5,13},{9,1},{13,5},{2,10},{6,14},... | collective-permute-start | bytes 4718600 | tf_op jit(solution)/shard_map/ppermute | solution.py:44
  70.5 7.2 %collective-permute-start.13 = (bf16[1,1,1,128,1024]{4,3,2,1,0:T(8,128)(2,1)}, bf16[1,1,1,128,1024]{4,3,2,1,0:T(8,128)(2,1)S(1)}, u32[]{:S(2)}, u32[]{:S(2)}) collective-permute-start(bf16[1,1,1,128,1024]{4,3,2,1,0:T(8,128)(2,1)} %get-tuple-element.120), channel_id=1, source_target_pairs={{0,16},{16,0},{1,17},{17,1},{2,18},{18,2},{3,19},{19,3},{4,20},{20... | collective-permute-start | bytes 786440 | tf_op jit(solution)/shard_map/ppermute | solution.py:44
  72.0 7.2 %collective-permute-start.11 = (bf16[1,1,1,128,1024]{4,3,2,1,0:T(8,128)(2,1)S(1)}, bf16[1,1,1,128,1024]{4,3,2,1,0:T(8,128)(2,1)S(1)}, u32[]{:S(2)}, u32[]{:S(2)}) collective-permute-start(bf16[1,1,1,128,1024]{4,3,2,1,0:T(8,128)(2,1)S(1)} %get-tuple-element.119), channel_id=1, source_target_pairs={{0,2},{1,3},{2,0},{3,1},{4,6},{5,7},{6,4},{7,5},{8,10},{9,11},{10,... | collective-permute-start | bytes 786440 | tf_op jit(solution)/shard_map/ppermute | solution.py:44
  73.5 52.7 %collective-permute-start.8 = (bf16[16,128,256]{2,1,0:T(8,128)(2,1)}, bf16[16,128,256]{2,1,0:T(8,128)(2,1)S(1)}, u32[]{:S(2)}, u32[]{:S(2)}) collective-permute-start(bf16[16,128,256]{2,1,0:T(8,128)(2,1)} %get-tuple-element.138.refs_2_), channel_id=1, source_target_pairs={{0,4},{4,0},{8,12},{12,8},{1,5},{5,1},{9,13},{13,9},{2,6},{6,2},{1... | collective-permute-start | bytes 3145736 | tf_op jit(solution)/shard_map/ppermute | solution.py:44
  77.7 13.8 %collective-permute-start.14 = (bf16[1,1,2,128,1024]{4,3,2,1,0:T(8,128)(2,1)S(1)}, bf16[1,1,2,128,1024]{4,3,2,1,0:T(8,128)(2,1)S(1)}, u32[]{:S(2)}, u32[]{:S(2)}) collective-permute-start(bf16[1,1,2,128,1024]{4,3,2,1,0:T(8,128)(2,1)S(1)} %constant_dynamic-update-slice_fusion.2), channel_id=1, source_target_pairs={{0,2},{1,3},{2,0},{3,1},{4,6},{5,7},{6,4},{7,5},{8,10},{9,11},{10,... | collective-permute-start | bytes 1572872 | tf_op jit(solution)/shard_map/ppermute | solution.py:44
  79.3 13.3 %collective-permute-start.12 = (bf16[1,2,1,128,1024]{4,3,2,1,0:T(8,128)(2,1)S(1)}, bf16[1,2,1,128,1024]{4,3,2,1,0:T(8,128)(2,1)S(1)}, u32[]{:S(2)}, u32[]{:S(2)}) collective-permute-start(bf16[1,2,1,128,1024]{4,3,2,1,0:T(8,128)(2,1)S(1)} %constant_dynamic-update-slice_fusion), channel_id=1, source_target_pairs={{0,16},{16,0},{1,17},{17,1},{2,18},{18,2},{3,19},{19,3},{4,20},{20... | collective-permute-start | bytes 1572872 | tf_op jit(solution)/shard_map/ppermute | solution.py:44
  80.8 61.1 %all-to-all-start.1 = ((bf16[4,2,256,384]{3,2,1,0:T(8,128)(2,1)}), bf16[4,2,256,384]{3,2,1,0:T(8,128)(2,1)}, u32[]{:S(2)}, u32[]{:S(2)}) async-start(bf16[4,2,256,384]{3,2,1,0:T(8,128)(2,1)} %copy.25), calls=%async_computation.1 | async-start | bytes 3145728 | tf_op jit(solution)/shard_map/all_to_all | solution.py:554
  85.4 56.6 %collective-permute-start.9 = (bf16[1,2,2,128,1024]{4,3,2,1,0:T(8,128)(2,1)}, bf16[1,2,2,128,1024]{4,3,2,1,0:T(8,128)(2,1)}, u32[]{:S(2)}, u32[]{:S(2)}) collective-permute-start(bf16[1,2,2,128,1024]{4,3,2,1,0:T(8,128)(2,1)} %pad_maximum_fusion.refs_3_), channel_id=1, source_target_pairs={{0,1},{1,0},{2,3},{3,2},{4,5},{5,4},{6,7},{7,6},{8,9},{9,8},{10,11... | collective-permute-start | bytes 3145736 | tf_op jit(solution)/shard_map/ppermute | solution.py:44
  91.5 50.5 %collective-permute-start.10 = (bf16[1,2,2,128,1024]{4,3,2,1,0:T(8,128)(2,1)}, bf16[1,2,2,128,1024]{4,3,2,1,0:T(8,128)(2,1)}, u32[]{:S(2)}, u32[]{:S(2)}) collective-permute-start(bf16[1,2,2,128,1024]{4,3,2,1,0:T(8,128)(2,1)} %pad_maximum_fusion.1.refs_4_), channel_id=1, source_target_pairs={{0,1},{1,0},{2,3},{3,2},{4,5},{5,4},{6,7},{7,6},{8,9},{9,8},{10,11... | collective-permute-start | bytes 3145736 | tf_op jit(solution)/shard_map/ppermute | solution.py:44
  126.1 14.1 %copy-start.17 = (bf16[16,128,256]{2,1,0:T(8,128)(2,1)}, bf16[16,128,256]{2,1,0:T(8,128)(2,1)S(1)}, u32[]{:S(2)}) copy-start(bf16[16,128,256]{2,1,0:T(8,128)(2,1)S(1)} %collective-permute-done.8.refs_1_) | copy-start | bytes 3145732
  141.4 2.7 collective-permute-start.15
  141.7 4.0 %collective-permute-start.16 = (bf16[1,2,2,128,1024]{4,3,2,1,0:T(8,128)(2,1)S(1)}, bf16[1,2,2,128,1024]{4,3,2,1,0:T(8,128)(2,1)}, u32[]{:S(2)}, u32[]{:S(2)}) collective-permute-start(bf16[1,2,2,128,1024]{4,3,2,1,0:T(8,128)(2,1)S(1)} %copy-done), channel_id=1, source_target_pairs={{0,1},{1,0},{2,3},{3,2},{4,5},{5,4},{6,7},{7,6},{8,9},{9,8},{10,11... | collective-permute-start | bytes 3145736 | tf_op jit(solution)/shard_map/ppermute | solution.py:44
  145.7 70.2 %collective-permute-start.20 = (bf16[4,2,256,384]{3,2,1,0:T(8,128)(2,1)}, bf16[4,2,256,384]{3,2,1,0:T(8,128)(2,1)}, u32[]{:S(2)}, u32[]{:S(2)}) collective-permute-start(bf16[4,2,256,384]{3,2,1,0:T(8,128)(2,1)} %all-to-all-done.1.refs_4_.refs_7_), channel_id=1, source_target_pairs={{0,8},{4,12},{8,0},{12,4},{1,9},{5,13},{9,1},{13,5},{2,10},{6,14},... | collective-permute-start | bytes 4718600 | tf_op jit(solution)/shard_map/ppermute | solution.py:44
  149.7 7.2 %copy-start.12 = (bf16[16,128,256]{2,1,0:T(8,128)(2,1)S(1)}, bf16[16,128,256]{2,1,0:T(8,128)(2,1)}, u32[]{:S(2)}) copy-start(bf16[16,128,256]{2,1,0:T(8,128)(2,1)} %refs_1_.6) | copy-start | bytes 3145732
  149.8 7.2 %copy-start.14 = (bf16[16,128,256]{2,1,0:T(8,128)(2,1)S(1)}, bf16[16,128,256]{2,1,0:T(8,128)(2,1)}, u32[]{:S(2)}) copy-start(bf16[16,128,256]{2,1,0:T(8,128)(2,1)} %get-tuple-element.138.refs_2_) | copy-start | bytes 3145732
  149.8 7.2 %copy-start.16 = (bf16[16,128,256]{2,1,0:T(8,128)(2,1)S(1)}, bf16[16,128,256]{2,1,0:T(8,128)(2,1)}, u32[]{:S(2)}) copy-start(bf16[16,128,256]{2,1,0:T(8,128)(2,1)} %get-tuple-element.139.refs_3_) | copy-start | bytes 3145732
  149.8 47.8 %collective-permute-start.17 = (bf16[1,1024,384]{2,1,0:T(8,128)(2,1)S(1)}, bf16[1,1024,384]{2,1,0:T(8,128)(2,1)S(1)}, u32[]{:S(2)}, u32[]{:S(2)}) collective-permute-start(bf16[1,1024,384]{2,1,0:T(8,128)(2,1)S(1)} %partner_product.3), channel_id=1, source_target_pairs={{0,4},{4,0},{8,12},{12,8},{1,5},{5,1},{9,13},{13,9},{2,6},{6,2},{1... | collective-permute-start | bytes 2359304 | tf_op jit(solution)/shard_map/ppermute | solution.py:44
  156.7 40.8 %copy-start.2 = (f32[1024,128]{1,0:T(8,128)S(1)}, f32[1024,128]{1,0:T(8,128)}, u32[]{:S(2)}) copy-start(f32[1024,128]{1,0:T(8,128)} %get-tuple-element.185.refs_10_) | copy-start | bytes 1572868
  156.7 40.8 %copy-start.5 = (f32[1024,128]{1,0:T(8,128)S(1)}, f32[1024,128]{1,0:T(8,128)}, u32[]{:S(2)}) copy-start(f32[1024,128]{1,0:T(8,128)} %get-tuple-element.186.refs_11_) | copy-start | bytes 1572868
  156.7 40.8 %copy-start.29 = (s32[4,16]{1,0:T(4,128)S(1)}, s32[4,16]{1,0:T(4,128)}, u32[]{:S(2)}) copy-start(s32[4,16]{1,0:T(4,128)} %refs_2_.5) | copy-start | bytes 772
  156.7 63.3 %collective-permute-start.18 = (bf16[1,1024,384]{2,1,0:T(8,128)(2,1)}, bf16[1,1024,384]{2,1,0:T(8,128)(2,1)}, u32[]{:S(2)}, u32[]{:S(2)}) collective-permute-start(bf16[1,1024,384]{2,1,0:T(8,128)(2,1)} %partner_product.4), channel_id=1, source_target_pairs={{0,4},{4,0},{8,12},{12,8},{1,5},{5,1},{9,13},{13,9},{2,6},{6,2},{1... | collective-permute-start | bytes 2359304 | tf_op jit(solution)/shard_map/ppermute | solution.py:44
  160.3 43.6 %copy-start.27 = (s32[4]{0:T(128)S(1)}, s32[4]{0:T(128)}, u32[]{:S(2)}) copy-start(s32[4]{0:T(128)} %refs_1_.12) | copy-start | bytes 52
  160.3 59.7 %collective-permute-start.19 = (bf16[4,16,128,128]{3,2,1,0:T(8,128)(2,1)}, bf16[4,16,128,128]{3,2,1,0:T(8,128)(2,1)}, u32[]{:S(2)}, u32[]{:S(2)}) collective-permute-start(bf16[4,16,128,128]{3,2,1,0:T(8,128)(2,1)} %get-tuple-element.142), channel_id=1, source_target_pairs={{0,16},{16,0},{1,17},{17,1},{2,18},{18,2},{3,19},{19,3},{4,20},{20... | collective-permute-start | bytes 6291464 | tf_op jit(solution)/shard_map/ppermute | solution.py:44
  220.0 45.0 %all-to-all-start.2 = ((bf16[4,1,4,128,256]{4,3,2,1,0:T(8,128)(2,1)}), bf16[4,1,4,128,256]{4,3,2,1,0:T(8,128)(2,1)}, u32[]{:S(2)}, u32[]{:S(2)}) async-start(bf16[4,1,4,128,256]{4,3,2,1,0:T(8,128)(2,1)} %copy-done.22), calls=%async_computation.2 | async-start | bytes 2097152 | tf_op jit(solution)/shard_map/all_to_all | solution.py:561
  224.5 10.6 %copy-start.3 = (f32[1024,128]{1,0:T(8,128)S(1)}, f32[1024,128]{1,0:T(8,128)}, u32[]{:S(2)}) copy-start(f32[1024,128]{1,0:T(8,128)} %get-tuple-element.185.refs_10_) | copy-start | bytes 1572868
  224.5 10.6 %copy-start.6 = (f32[1024,128]{1,0:T(8,128)S(1)}, f32[1024,128]{1,0:T(8,128)}, u32[]{:S(2)}) copy-start(f32[1024,128]{1,0:T(8,128)} %get-tuple-element.186.refs_11_) | copy-start | bytes 1572868
  224.5 10.5 %copy-start.25 = (s32[4]{0:T(128)S(1)}, s32[4]{0:T(128)}, u32[]{:S(2)}) copy-start(s32[4]{0:T(128)} %copy-done.23) | copy-start | bytes 52
  224.5 10.5 %copy-start.28 = (s32[4]{0:T(128)S(1)}, s32[4]{0:T(128)}, u32[]{:S(2)}) copy-start(s32[4]{0:T(128)} %refs_1_.12) | copy-start | bytes 52
  224.5 10.5 %copy-start.30 = (s32[4,16]{1,0:T(4,128)S(1)}, s32[4,16]{1,0:T(4,128)}, u32[]{:S(2)}) copy-start(s32[4,16]{1,0:T(4,128)} %refs_2_.5) | copy-start | bytes 772
  231.9 45.1 %collective-permute-start.21 = (bf16[2,1024,384]{2,1,0:T(8,128)(2,1)}, bf16[2,1024,384]{2,1,0:T(8,128)(2,1)}, u32[]{:S(2)}, u32[]{:S(2)}) collective-permute-start(bf16[2,1024,384]{2,1,0:T(8,128)(2,1)} %partner_product.5), channel_id=1, source_target_pairs={{0,4},{4,0},{8,12},{12,8},{1,5},{5,1},{9,13},{13,9},{2,6},{6,2},{1... | collective-permute-start | bytes 4718600 | tf_op jit(solution)/shard_map/ppermute | solution.py:44
  233.6 14.1 %collective-permute-start.22 = (bf16[1,1,1024,128]{3,2,1,0:T(8,128)(2,1)S(1)}, bf16[1,1,1024,128]{3,2,1,0:T(8,128)(2,1)S(1)}, u32[]{:S(2)}, u32[]{:S(2)}) collective-permute-start(bf16[1,1,1024,128]{3,2,1,0:T(8,128)(2,1)S(1)} %bitcast.27), channel_id=1, source_target_pairs={{0,2},{1,3},{2,0},{3,1},{4,6},{5,7},{6,4},{7,5},{8,10},{9,11},{10,... | collective-permute-start | bytes 786440 | tf_op jit(solution)/shard_map/ppermute | solution.py:44
  246.2 9.3 %collective-permute-start.25 = (bf16[1,1,1024,128]{3,2,1,0:T(8,128)(2,1)S(1)}, bf16[1,1,1024,128]{3,2,1,0:T(8,128)(2,1)S(1)}, u32[]{:S(2)}, u32[]{:S(2)}) collective-permute-start(bf16[1,1,1024,128]{3,2,1,0:T(8,128)(2,1)S(1)} %bitcast.30), channel_id=1, source_target_pairs={{0,16},{16,0},{1,17},{17,1},{2,18},{18,2},{3,19},{19,3},{4,20},{20... | collective-permute-start | bytes 786440 | tf_op jit(solution)/shard_map/ppermute | solution.py:44
  247.8 16.3 %collective-permute-start.23 = (bf16[2,1,1024,128]{3,2,1,0:T(8,128)(2,1)S(1)}, bf16[2,1,1024,128]{3,2,1,0:T(8,128)(2,1)S(1)}, u32[]{:S(2)}, u32[]{:S(2)}) collective-permute-start(bf16[2,1,1024,128]{3,2,1,0:T(8,128)(2,1)S(1)} %pad_maximum_fusion.10), channel_id=1, source_target_pairs={{0,16},{16,0},{1,17},{17,1},{2,18},{18,2},{3,19},{19,3},{4,20},{20... | collective-permute-start | bytes 1572872 | tf_op jit(solution)/shard_map/ppermute | solution.py:44
  255.5 9.2 %collective-permute-start.26 = (bf16[1,2,1024,128]{3,2,1,0:T(8,128)(2,1)S(1)}, bf16[1,2,1024,128]{3,2,1,0:T(8,128)(2,1)S(1)}, u32[]{:S(2)}, u32[]{:S(2)}) collective-permute-start(bf16[1,2,1024,128]{3,2,1,0:T(8,128)(2,1)S(1)} %pad_maximum_fusion.11), channel_id=1, source_target_pairs={{0,2},{1,3},{2,0},{3,1},{4,6},{5,7},{6,4},{7,5},{8,10},{9,11},{10,... | collective-permute-start | bytes 1572872 | tf_op jit(solution)/shard_map/ppermute | solution.py:44
  264.2 12.7 %copy-start.8 = (bf16[2,2,1024,128]{3,2,1,0:T(8,128)(2,1)}, bf16[2,2,1024,128]{3,2,1,0:T(8,128)(2,1)S(1)}, u32[]{:S(2)}) copy-start(bf16[2,2,1024,128]{3,2,1,0:T(8,128)(2,1)S(1)} %pad_maximum_fusion.4.refs_1_) | copy-start | bytes 3145732
  264.3 12.8 %collective-permute-start.24 = (bf16[2,2,1024,128]{3,2,1,0:T(8,128)(2,1)S(1)}, bf16[2,2,1024,128]{3,2,1,0:T(8,128)(2,1)}, u32[]{:S(2)}, u32[]{:S(2)}) collective-permute-start(bf16[2,2,1024,128]{3,2,1,0:T(8,128)(2,1)S(1)} %pad_maximum_fusion.4.refs_1_), channel_id=1, source_target_pairs={{0,1},{1,0},{2,3},{3,2},{4,5},{5,4},{6,7},{7,6},{8,9},{9,8},{10,11... | collective-permute-start | bytes 3145736 | tf_op jit(solution)/shard_map/ppermute | solution.py:44
  264.9 12.1 %copy-start.10 = (bf16[2,2,1024,128]{3,2,1,0:T(8,128)(2,1)}, bf16[2,2,1024,128]{3,2,1,0:T(8,128)(2,1)S(1)}, u32[]{:S(2)}) copy-start(bf16[2,2,1024,128]{3,2,1,0:T(8,128)(2,1)S(1)} %pad_maximum_fusion.5.refs_3_) | copy-start | bytes 3145732
  264.9 12.1 %collective-permute-start.27 = (bf16[2,2,1024,128]{3,2,1,0:T(8,128)(2,1)S(1)}, bf16[2,2,1024,128]{3,2,1,0:T(8,128)(2,1)}, u32[]{:S(2)}, u32[]{:S(2)}) collective-permute-start(bf16[2,2,1024,128]{3,2,1,0:T(8,128)(2,1)S(1)} %pad_maximum_fusion.5.refs_3_), channel_id=1, source_target_pairs={{0,1},{1,0},{2,3},{3,2},{4,5},{5,4},{6,7},{7,6},{8,9},{9,8},{10,11... | collective-permute-start | bytes 3145736 | tf_op jit(solution)/shard_map/ppermute | solution.py:44
  277.0 29.1 %all-to-all-start.3 = ((bf16[4,1,4,128,256]{4,3,2,1,0:T(8,128)(2,1)}), bf16[4,1,4,128,256]{4,3,2,1,0:T(8,128)(2,1)S(1)}, u32[]{:S(2)}, u32[]{:S(2)}) async-start(bf16[4,1,4,128,256]{4,3,2,1,0:T(8,128)(2,1)} %copy-done.21), calls=%async_computation.3 | async-start | bytes 2097152 | tf_op jit(solution)/shard_map/all_to_all | solution.py:561
  300.1 9.7 %collective-permute-start.31 = (bf16[1,1,1024,128]{3,2,1,0:T(8,128)(2,1)}, bf16[1,1,1024,128]{3,2,1,0:T(8,128)(2,1)}, u32[]{:S(2)}, u32[]{:S(2)}) collective-permute-start(bf16[1,1,1024,128]{3,2,1,0:T(8,128)(2,1)} %get-tuple-element.212), channel_id=1, source_target_pairs={{0,16},{16,0},{1,17},{17,1},{2,18},{18,2},{3,19},{19,3},{4,20},{20... | collective-permute-start | bytes 786440 | tf_op jit(solution)/shard_map/ppermute | solution.py:44
  301.5 10.9 %collective-permute-start.28 = (bf16[1,1,1024,128]{3,2,1,0:T(8,128)(2,1)S(1)}, bf16[1,1,1024,128]{3,2,1,0:T(8,128)(2,1)}, u32[]{:S(2)}, u32[]{:S(2)}) collective-permute-start(bf16[1,1,1024,128]{3,2,1,0:T(8,128)(2,1)S(1)} %get-tuple-element.213), channel_id=1, source_target_pairs={{0,2},{1,3},{2,0},{3,1},{4,6},{5,7},{6,4},{7,5},{8,10},{9,11},{10,... | collective-permute-start | bytes 786440 | tf_op jit(solution)/shard_map/ppermute | solution.py:44
  306.1 51.3 %all-to-all-start.4 = ((bf16[4,2,4,128,256]{4,3,2,1,0:T(8,128)(2,1)}), bf16[4,2,4,128,256]{4,3,2,1,0:T(8,128)(2,1)S(1)}, u32[]{:S(2)}, u32[]{:S(2)}) async-start(bf16[4,2,4,128,256]{4,3,2,1,0:T(8,128)(2,1)} %get-tuple-element.209), calls=%async_computation.4 | async-start | bytes 4194304 | tf_op jit(solution)/shard_map/all_to_all | solution.py:600
  311.0 12.9 %collective-permute-start.32 = (bf16[1,2,1024,128]{3,2,1,0:T(8,128)(2,1)S(1)}, bf16[1,2,1024,128]{3,2,1,0:T(8,128)(2,1)S(1)}, u32[]{:S(2)}, u32[]{:S(2)}) collective-permute-start(bf16[1,2,1024,128]{3,2,1,0:T(8,128)(2,1)S(1)} %pad_maximum_fusion.13), channel_id=1, source_target_pairs={{0,2},{1,3},{2,0},{3,1},{4,6},{5,7},{6,4},{7,5},{8,10},{9,11},{10,... | collective-permute-start | bytes 1572872 | tf_op jit(solution)/shard_map/ppermute | solution.py:44
  313.4 12.7 %collective-permute-start.29 = (bf16[2,1,1024,128]{3,2,1,0:T(8,128)(2,1)S(1)}, bf16[2,1,1024,128]{3,2,1,0:T(8,128)(2,1)S(1)}, u32[]{:S(2)}, u32[]{:S(2)}) collective-permute-start(bf16[2,1,1024,128]{3,2,1,0:T(8,128)(2,1)S(1)} %pad_maximum_fusion.12), channel_id=1, source_target_pairs={{0,16},{16,0},{1,17},{17,1},{2,18},{18,2},{3,19},{19,3},{4,20},{20... | collective-permute-start | bytes 1572872 | tf_op jit(solution)/shard_map/ppermute | solution.py:44
  327.2 2.7 collective-permute-start.30
  327.2 4.1 %collective-permute-start.33 = (bf16[2,2,1024,128]{3,2,1,0:T(8,128)(2,1)S(1)}, bf16[2,2,1024,128]{3,2,1,0:T(8,128)(2,1)S(1)}, u32[]{:S(2)}, u32[]{:S(2)}) collective-permute-start(bf16[2,2,1024,128]{3,2,1,0:T(8,128)(2,1)S(1)} %pad_maximum_fusion.7.refs_3_), channel_id=1, source_target_pairs={{0,1},{1,0},{2,3},{3,2},{4,5},{5,4},{6,7},{7,6},{8,9},{9,8},{10,11... | collective-permute-start | bytes 3145736 | tf_op jit(solution)/shard_map/ppermute | solution.py:44
  336.7 5.6 %collective-permute-start.34 = (bf16[128,512]{1,0:T(8,128)(2,1)S(1)}, bf16[128,512]{1,0:T(8,128)(2,1)S(1)}, u32[]{:S(2)}, u32[]{:S(2)}) collective-permute-start(bf16[128,512]{1,0:T(8,128)(2,1)S(1)} %get-tuple-element.201), channel_id=1, source_target_pairs={{0,16},{1,17},{2,18},{3,19},{16,0},{17,1},{18,2},{19,3},{4,20},{5,... | collective-permute-start | bytes 393224 | tf_op jit(solution)/shard_map/ppermute | solution.py:450
  338.3 6.4 %collective-permute-start.35 = (bf16[128,512]{1,0:T(8,128)(2,1)S(1)}, bf16[128,512]{1,0:T(8,128)(2,1)S(1)}, u32[]{:S(2)}, u32[]{:S(2)}) collective-permute-start(bf16[128,512]{1,0:T(8,128)(2,1)S(1)} %get-tuple-element.202), channel_id=1, source_target_pairs={{0,2},{1,3},{2,0},{3,1},{16,18},{17,19},{18,16},{19,17},{4,6},{5,7... | collective-permute-start | bytes 393224 | tf_op jit(solution)/shard_map/ppermute | solution.py:450
  338.8 9.8 %collective-permute-start.36 = (bf16[128,512]{1,0:T(8,128)(2,1)S(1)}, bf16[128,512]{1,0:T(8,128)(2,1)S(1)}, u32[]{:S(2)}, u32[]{:S(2)}) collective-permute-start(bf16[128,512]{1,0:T(8,128)(2,1)S(1)} %get-tuple-element.203), channel_id=1, source_target_pairs={{0,18},{1,19},{2,16},{3,17},{16,2},{17,3},{18,0},{19,1},{4,22},{5,... | collective-permute-start | bytes 393224 | tf_op jit(solution)/shard_map/ppermute | solution.py:450
  340.2 8.3 %collective-permute-start.37 = (bf16[128,512]{1,0:T(8,128)(2,1)S(1)}, bf16[128,512]{1,0:T(8,128)(2,1)S(1)}, u32[]{:S(2)}, u32[]{:S(2)}) collective-permute-start(bf16[128,512]{1,0:T(8,128)(2,1)S(1)} %get-tuple-element.204), channel_id=1, source_target_pairs={{0,1},{1,0},{2,3},{3,2},{16,17},{17,16},{18,19},{19,18},{4,5},{5,4... | collective-permute-start | bytes 393224 | tf_op jit(solution)/shard_map/ppermute | solution.py:450
  340.2 8.3 %collective-permute-start.38 = (bf16[128,512]{1,0:T(8,128)(2,1)S(1)}, bf16[128,512]{1,0:T(8,128)(2,1)S(1)}, u32[]{:S(2)}, u32[]{:S(2)}) collective-permute-start(bf16[128,512]{1,0:T(8,128)(2,1)S(1)} %get-tuple-element.205), channel_id=1, source_target_pairs={{0,17},{1,16},{2,19},{3,18},{16,1},{17,0},{18,3},{19,2},{4,21},{5,... | collective-permute-start | bytes 393224 | tf_op jit(solution)/shard_map/ppermute | solution.py:450
  342.3 6.3 %collective-permute-start.39 = (bf16[128,512]{1,0:T(8,128)(2,1)S(1)}, bf16[128,512]{1,0:T(8,128)(2,1)S(1)}, u32[]{:S(2)}, u32[]{:S(2)}) collective-permute-start(bf16[128,512]{1,0:T(8,128)(2,1)S(1)} %get-tuple-element.206), channel_id=1, source_target_pairs={{0,3},{1,2},{2,1},{3,0},{16,19},{17,18},{18,17},{19,16},{4,7},{5,6... | collective-permute-start | bytes 393224 | tf_op jit(solution)/shard_map/ppermute | solution.py:450
  344.6 7.3 %copy-start.20 = (bf16[1,1,128,4096]{3,2,1,0:T(8,128)(2,1)S(1)}, bf16[1,1,128,4096]{3,2,1,0:T(8,128)(2,1)}, u32[]{:S(2)}) copy-start(bf16[1,1,128,4096]{3,2,1,0:T(8,128)(2,1)} %param.7) | copy-start | bytes 3145732
  344.6 7.3 %collective-permute-start.40 = (bf16[128,512]{1,0:T(8,128)(2,1)S(1)}, bf16[128,512]{1,0:T(8,128)(2,1)S(1)}, u32[]{:S(2)}, u32[]{:S(2)}) collective-permute-start(bf16[128,512]{1,0:T(8,128)(2,1)S(1)} %get-tuple-element.207), channel_id=1, source_target_pairs={{0,19},{1,18},{2,17},{3,16},{16,3},{17,2},{18,1},{19,0},{4,23},{5,... | collective-permute-start | bytes 393224 | tf_op jit(solution)/shard_map/ppermute | solution.py:450
  (18 other events, 71.8 us)
